TPU v7x, 128 devices: a whole 4x4x4 slice. The times are simulated.
128 devices in a mesh: gx: 8 (over z, core), gy: 16 (over x, y).
Axes of the slice: x: 4, y: 4, z: 4, core: 2. Of those that a mesh axis runs over, the one named last changes fastest.
Arguments:
- solvent_pos: float32 [3, 1572864], P(None, ('gx', 'gy')), may hold values from 0 to 48, as said below
- solvent_vel: float32 [3, 1572864], P(None, ('gx', 'gy')), may hold values from -6 to 6
- pair_index: int32 [49152, 128], P(('gx', 'gy')), may hold values from 0 to 110592, as said below
- random_pairs: bfloat16 [49152, 128, 128], P(('gx', 'gy')), may hold values from -4 to 4
- membrane_pos: float32 [3, 1314816], P(None, ('gx', 'gy')), may hold values from 0 to 48, as said below
- membrane_vel: float32 [3, 1314816], P(None, ('gx', 'gy')), may hold values from -6 to 6
- mem_vertex: int32 [8192, 128], P(('gx', 'gy')), may hold values from 0 to 10271, as said below
- mem_partner: int32 [8192, 128], P(('gx', 'gy')), may hold values from 0 to 110591, as said below
- bending: float32 [642, 642], replicated, may hold values from -1 to 2
- rest_size: float32 [2048], P(('gx', 'gy')), may hold values from 2 to 8
- cell_count: int32 [128], P(('gx', 'gy')), may hold values from 1 to 16, as said below
Outputs:
- solvent_velocity: float32 [3, 1572864], P(None, ('gx', 'gy'))
- membrane_velocity: float32 [3, 1314816], P(None, ('gx', 'gy'))
Inputs may be any that keep to these rules, and one draw needn't show every extreme that they name: `solvent_pos`: positions lie in the owning brick's frame: x and y in [0, 4), z in [0, 48); particle m lies in box b = m // 128, the cube of side 2 with corner (2 (b % 2), 2 (b // 2 % 2), 2 (b // 4)). `membrane_pos`: vertex positions lie in the owning brick's frame: x and y in [0, 4), z in [0, 48). `pair_index`: index (3 p + q) * 12288 + m names particle m of brick (i + p - 1, j + q - 1); 110592 marks an empty slot. `mem_vertex`: index c * 642 + v names vertex v of the brick's cell slot c. `mem_partner`: index (3 p + q) * 12288 + m names particle m of brick (i + p - 1, j + q - 1). Cell slots 0 to cell_count - 1 of a brick are live.
All inputs are finite; a program needn't handle non-finite values.
Results may differ from a plain program's by a relative error of at most 0.0003.
Values sent between devices are 32-bit elements; how exact they have to be, the bound alone decides.
A program may use at most 448 MiB of HBM per device.

v0:
```python
import math

import jax
import jax.numpy as jnp
from jax import lax
from jax.sharding import PartitionSpec as P

V = 642
TILE = 128
PAIRS = 4


TIME_STEP = 0.01
REPEL_STRENGTH = 25.0
FRICTION = 4.5
NOISE_SCALE = 30.0
BENDING_MODULUS = 20.0
AREA_MODULUS = 40.0
SOLVENT_PUSH = 0.5
RADIUS_FLOOR = 0.1
BRICK_SIDE = 4.0
FAR_AWAY = 1000.0


def shifted(array, axis, by):
    size = lax.axis_size(axis)
    return lax.ppermute(array, axis, [(i, (i + by) % size) for i in range(size)])


def extended_2(block, sides, width):
    for axis, dim in sides:
        count = lax.axis_size(axis)
        forward = [(i, i + 1) for i in range(count - 1)]
        forward.append((count - 1, 0))
        backward = [(target, source) for source, target in forward]
        low = lax.ppermute(
            lax.slice_in_dim(block, block.shape[dim] - width, None, axis=dim), axis, forward
        )
        high = lax.ppermute(lax.slice_in_dim(block, 0, width, axis=dim), axis, backward)
        block = jnp.concatenate([low, block, high], axis=dim)
    return block


def pair_terms(left_pos, left_vel, right_pos, right_vel, noise_block):
    offset = left_pos[..., :, None] - right_pos[..., None, :]
    radius = jnp.sqrt(jnp.sum(offset * offset, axis=0))
    weight = jnp.maximum(1.0 - radius, 0.0)
    direction_unit = offset / jnp.maximum(radius, RADIUS_FLOOR)
    approach = jnp.sum(direction_unit * (left_vel[..., :, None] - right_vel[..., None, :]), axis=0)
    magnitude = weight * (REPEL_STRENGTH - FRICTION * weight * approach + NOISE_SCALE * noise_block)
    return magnitude[None] * direction_unit


def neighbourhood(extended):
    shifts = (jnp.arange(3, dtype=jnp.int32) - 1).astype(jnp.float32) * BRICK_SIDE
    offsets = jnp.stack(
        [
            jnp.broadcast_to(shifts[:, None], (3, 3)),
            jnp.broadcast_to(shifts[None, :], (3, 3)),
            jnp.zeros((3, 3), jnp.float32),
        ],
        axis=2,
    )
    positions = extended[:, :, 0:3] + offsets[:, :, :, None]
    velocity = extended[:, :, 3:6]
    span = 9 * extended.shape[3]
    flat_pos = positions.transpose(2, 0, 1, 3).reshape(3, span)
    flat_vel = velocity.transpose(2, 0, 1, 3).reshape(3, span)
    flat_pos = jnp.concatenate([flat_pos, jnp.full((3, 1), FAR_AWAY, jnp.float32)], axis=1)
    flat_vel = jnp.concatenate([flat_vel, jnp.zeros((3, 1), jnp.float32)], axis=1)
    return (flat_pos, flat_vel)


def solvent_forces(own_pos, own_vel, flat_pos, flat_vel, pair_index, random_pairs):
    tiles_here = pair_index.shape[0]
    group_size = math.gcd(tiles_here, 16)
    box_count = group_size // PAIRS

    def solvent_add_group(loop_turn, force):
        tile_start = (loop_turn * group_size).astype(jnp.int32)
        chosen = lax.dynamic_slice_in_dim(pair_index, tile_start, group_size, 0)
        noise_block = lax.dynamic_slice_in_dim(random_pairs, tile_start, group_size, 0).astype(
            jnp.float32
        )
        row_start = tile_start // PAIRS * TILE
        left_pos = lax.dynamic_slice_in_dim(own_pos, row_start, box_count * TILE, 1).reshape(
            3, box_count, 1, TILE
        )
        left_pos = jnp.broadcast_to(left_pos, (3, box_count, PAIRS, TILE)).reshape(
            3, group_size, TILE
        )
        left_vel = lax.dynamic_slice_in_dim(own_vel, row_start, box_count * TILE, 1).reshape(
            3, box_count, 1, TILE
        )
        left_vel = jnp.broadcast_to(left_vel, (3, box_count, PAIRS, TILE)).reshape(
            3, group_size, TILE
        )
        right_pos = jnp.take(flat_pos, chosen, axis=1)
        right_vel = jnp.take(flat_vel, chosen, axis=1)
        terms = pair_terms(left_pos, left_vel, right_pos, right_vel, noise_block)
        box_force = (
            jnp.sum(terms, axis=3)
            .reshape(3, box_count, PAIRS, TILE)
            .sum(axis=2)
            .reshape(3, box_count * TILE)
        )
        return lax.dynamic_update_slice_in_dim(force, box_force, row_start, 1)

    return lax.fori_loop(0, tiles_here // group_size, solvent_add_group, jnp.zeros_like(own_pos))


def contact_forces(mem_pos, mem_vel, flat_pos, flat_vel, mem_vertex, mem_partner, cell_total):
    tiles_here = mem_vertex.shape[0]
    group_size = math.gcd(tiles_here, 16)
    slot_total = tiles_here * mem_vertex.shape[1]

    def contact_add_group(loop_turn, carried):
        vertex_force, slot_reaction = carried
        tile_start = (loop_turn * group_size).astype(jnp.int32)
        chosen_vertex = lax.dynamic_slice_in_dim(mem_vertex, tile_start, group_size, 0)
        chosen_partner = lax.dynamic_slice_in_dim(mem_partner, tile_start, group_size, 0)
        left_pos = jnp.take(mem_pos, chosen_vertex, axis=1)
        left_vel = jnp.take(mem_vel, chosen_vertex, axis=1)
        right_pos = jnp.take(flat_pos, chosen_partner, axis=1)
        right_vel = jnp.take(flat_vel, chosen_partner, axis=1)
        alive_mask = (chosen_vertex // V < cell_total).astype(jnp.float32)
        terms = (
            pair_terms(left_pos, left_vel, right_pos, right_vel, 0.0) * alive_mask[None, :, :, None]
        )
        vertex_force = vertex_force.at[:, chosen_vertex.reshape(-1)].add(
            jnp.sum(terms, axis=3).reshape(3, -1)
        )
        slot_part = -jnp.sum(terms, axis=2).reshape(3, -1)
        slot_reaction = lax.dynamic_update_slice_in_dim(
            slot_reaction, slot_part, tile_start * TILE, 1
        )
        return (vertex_force, slot_reaction)

    start_state = (jnp.zeros_like(mem_pos), jnp.zeros((3, slot_total), jnp.float32))
    vertex_force, slot_reaction = lax.fori_loop(
        0, tiles_here // group_size, contact_add_group, start_state
    )
    return (vertex_force, slot_reaction)


def dense_reaction(slot_reaction, mem_partner, flat_width):
    reaction = (
        jnp.zeros((3, flat_width), jnp.float32).at[:, mem_partner.reshape(-1)].add(slot_reaction)
    )
    width = (flat_width - 1) // 9
    return reaction[:, :-1].reshape(3, 3, 3, width).transpose(1, 2, 0, 3)


def membrane_forces(mem_pos, bending, rest_size, alive_mask):
    cells_here = rest_size.shape[0]
    shaped = mem_pos.reshape(3, cells_here, V)
    centre = jnp.mean(shaped, axis=2, keepdims=True)
    relative = shaped - centre
    bent_once = jnp.einsum("knv,uv->knu", relative, bending, precision=lax.Precision.HIGHEST)
    bent_twice = jnp.einsum("knv,uv->knu", bent_once, bending, precision=lax.Precision.HIGHEST)
    spread = jnp.sum(relative * relative, axis=(0, 2)) / V
    stretch = AREA_MODULUS * (spread / rest_size - 1.0)
    internal = (
        -(BENDING_MODULUS * bent_twice + stretch[None, :, None] * relative)
        * alive_mask[None, :, None]
    )
    return internal.reshape(3, cells_here * V)


def width_move(block, by_amount):
    return shifted(block, "gy", by_amount)


def length_move(block, by_amount):
    return shifted(block, "gx", by_amount)


def on_device(
    solvent_pos,
    solvent_vel,
    pair_index,
    random_pairs,
    membrane_pos,
    membrane_vel,
    mem_vertex,
    mem_partner,
    bending,
    rest_size,
    cell_count,
):
    solvent_state = jnp.concatenate([solvent_pos, solvent_vel], axis=0)[None, None]
    extended = extended_2(solvent_state, (("gx", 0), ("gy", 1)), 1)
    alive_mask = (jnp.arange(rest_size.shape[0], dtype=jnp.int32) < cell_count[0]).astype(
        jnp.float32
    )
    internal = membrane_forces(membrane_pos, bending, rest_size, alive_mask)
    flat_pos, flat_vel = neighbourhood(extended)
    solvent_force = solvent_forces(
        solvent_pos, solvent_vel, flat_pos, flat_vel, pair_index, random_pairs
    )
    contact, slot_reaction = contact_forces(
        membrane_pos, membrane_vel, flat_pos, flat_vel, mem_vertex, mem_partner, cell_count[0]
    )
    reaction = dense_reaction(slot_reaction, mem_partner, flat_pos.shape[1])
    column = reaction[:, 1] + width_move(reaction[:, 2], 1) + width_move(reaction[:, 0], -1)
    returned = column[1] + length_move(column[2], 1) + length_move(column[0], -1)
    push = jnp.array([SOLVENT_PUSH, 0.0, 0.0], jnp.float32)[:, None]
    solvent_velocity = solvent_vel + TIME_STEP * (solvent_force + returned + push)
    membrane_velocity = membrane_vel + TIME_STEP * (internal + contact)
    return (solvent_velocity, membrane_velocity)


def solution(mesh):
    return jax.shard_map(
        on_device,
        mesh=mesh,
        in_specs=(
            P(None, ("gx", "gy")),
            P(None, ("gx", "gy")),
            P(("gx", "gy"), None),
            P(("gx", "gy"), None, None),
            P(None, ("gx", "gy")),
            P(None, ("gx", "gy")),
            P(("gx", "gy"), None),
            P(("gx", "gy"), None),
            P(),
            P(("gx", "gy")),
            P(("gx", "gy")),
        ),
        out_specs=(P(None, ("gx", "gy")), P(None, ("gx", "gy"))),
        check_vma=False,
    )
```

profile of v0, /device:TPU:1, one launch (start us, length us, event | category | flops | bytes accessed | tf_op | source)
XLA Modules:
  0.0 2208.2 jit_solution(7051680419362618176)
XLA Ops:
  50.2 25.7 %copy.76 = f32[3,3,3,12288]{0,3,2,1:T(8,128)} copy(f32[3,3,3,12288]{3,2,0,1:T(4,128)} %get-tuple-element.558) | data formatting | bytes 2654208
  75.9 25.3 %copy.77 = f32[3,3,3,12288]{0,3,2,1:T(8,128)} copy(f32[3,3,3,12288]{3,2,0,1:T(4,128)S(1)} %get-tuple-element.557) | data formatting | bytes 2654208
  101.2 38.0 %concatenate.19.clone = f32[3,110593]{0,1:T(8,128)} pad(f32[3,110592]{0,1:T(8,128)} %bitcast.144, f32[]{:T(128)} %constant.334.clone.1), padding=0_0x0_1 | pad | bytes 2654224 | tf_op jit(solution)/shard_map/concatenate | solution.py:70
  139.1 38.0 %concatenate.18.clone = f32[3,110593]{0,1:T(8,128)} pad(f32[3,110592]{0,1:T(8,128)} %bitcast.143, f32[]{:T(128)} %constant.337.clone.1), padding=0_0x0_1 | pad | bytes 2654224 | tf_op jit(solution)/shard_map/concatenate | solution.py:69
  179.7 401.7 %while.33 = (s32[]{:T(128)}, f32[3,10272]{0,1:T(8,128)}, f32[3,8192]{1,0:T(4,128)S(1)}, s32[64,128]{1,0:T(8,128)}, f32[3,10272]{0,1:T(8,128)}, /*index=5*/s32[64...) while((s32[]{:T(128)}, f32[3,10272]{0,1:T(8,128)}, ...), condition=%wide.region_12.15_spmd, body=%wide.region_6.14_spmd.sunk | while | flops 12412938 | bytes 11698445 | solution.py:140
  584.1 66.6 %scatter_custom_fusion.1 = f32[3,110593]{0,1:T(8,128)} fusion(s32[8192]{0:T(1024)S(1)} %bitcast.164, f32[8192,3]{1,0:T(8,128)} %copy.70, f32[]{:T(128)} %constant.334.clone.1), kind=kCustom, calls=%fused_computation.52 | custom fusion | flops 24576 | bytes 1327628 | tf_op jit(solution)/shard_map/scatter-add | solution.py:148
  650.7 38.0 %slice.50 = f32[3,110592]{0,1:T(8,128)} slice(f32[3,110593]{0,1:T(8,128)} %scatter_custom_fusion.1), slice={[0:3], [0:110592]} | slice | bytes 2654208 | tf_op jit(solution)/shard_map/slice | solution.py:151
  688.6 29.2 %copy.71 = f32[3,3,3,12288]{3,0,1,2:T(4,128)S(1)} copy(f32[3,3,3,12288]{0,3,2,1:T(8,128)} %bitcast.142) | data formatting | bytes 2654208 | tf_op jit(solution)/shard_map/reshape | solution.py:151
  720.7 1472.2 %while.32 = (s32[]{:T(128)}, f32[3,12288]{1,0:T(4,128)S(1)}, f32[3,12288]{1,0:T(4,128)}, s32[384,128]{1,0:T(8,128)}, f32[3,110593]{0,1:T(8,128)}, /*index=5*/f32...) while((s32[]{:T(128)}, f32[3,12288]{1,0:T(4,128)S(1)}, ...), condition=%wide.region_5.7_spmd, body=%wide.region_0.6_spmd.sunk | while | flops 11565592 | bytes 11727278 | solution.py:109
  721.7 24.8 %gather_fusion = f32[2048,3]{1,0:T(8,128)} fusion(f32[3,110593]{0,1:T(8,128)} %get-tuple-element.741, s32[2048]{0:T(1024)S(1)} %bitcast_clamp_fusion.6), kind=kCustom, calls=%fused_computation.clone.clone.1 | custom fusion | bytes 57344 | tf_op jit(solution)/shard_map/while/body/eval_jaxpr/jit(_take)/gather | solution.py:98
  747.3 24.8 %gather_fusion.1 = f32[2048,3]{1,0:T(8,128)} fusion(f32[3,110593]{0,1:T(8,128)} %get-tuple-element.743, s32[2048]{0:T(1024)S(1)} %bitcast_clamp_fusion.6), kind=kCustom, calls=%fused_computation.2.clone.clone.1 | custom fusion | bytes 57344 | tf_op jit(solution)/shard_map/while/body/eval_jaxpr/jit(_take)/gather | solution.py:99
  783.1 24.8 %gather_fusion = f32[2048,3]{1,0:T(8,128)} fusion(f32[3,110593]{0,1:T(8,128)} %get-tuple-element.741, s32[2048]{0:T(1024)S(1)} %bitcast_clamp_fusion.6), kind=kCustom, calls=%fused_computation.clone.clone.1 | custom fusion | bytes 57344 | tf_op jit(solution)/shard_map/while/body/eval_jaxpr/jit(_take)/gather | solution.py:98
  808.6 24.8 %gather_fusion.1 = f32[2048,3]{1,0:T(8,128)} fusion(f32[3,110593]{0,1:T(8,128)} %get-tuple-element.743, s32[2048]{0:T(1024)S(1)} %bitcast_clamp_fusion.6), kind=kCustom, calls=%fused_computation.2.clone.clone.1 | custom fusion | bytes 57344 | tf_op jit(solution)/shard_map/while/body/eval_jaxpr/jit(_take)/gather | solution.py:99
  844.4 24.8 %gather_fusion = f32[2048,3]{1,0:T(8,128)} fusion(f32[3,110593]{0,1:T(8,128)} %get-tuple-element.741, s32[2048]{0:T(1024)S(1)} %bitcast_clamp_fusion.6), kind=kCustom, calls=%fused_computation.clone.clone.1 | custom fusion | bytes 57344 | tf_op jit(solution)/shard_map/while/body/eval_jaxpr/jit(_take)/gather | solution.py:98
  905.7 24.8 %gather_fusion = f32[2048,3]{1,0:T(8,128)} fusion(f32[3,110593]{0,1:T(8,128)} %get-tuple-element.741, s32[2048]{0:T(1024)S(1)} %bitcast_clamp_fusion.6), kind=kCustom, calls=%fused_computation.clone.clone.1 | custom fusion | bytes 57344 | tf_op jit(solution)/shard_map/while/body/eval_jaxpr/jit(_take)/gather | solution.py:98
  931.3 24.8 %gather_fusion.1 = f32[2048,3]{1,0:T(8,128)} fusion(f32[3,110593]{0,1:T(8,128)} %get-tuple-element.743, s32[2048]{0:T(1024)S(1)} %bitcast_clamp_fusion.6), kind=kCustom, calls=%fused_computation.2.clone.clone.1 | custom fusion | bytes 57344 | tf_op jit(solution)/shard_map/while/body/eval_jaxpr/jit(_take)/gather | solution.py:99
  967.1 24.8 %gather_fusion = f32[2048,3]{1,0:T(8,128)} fusion(f32[3,110593]{0,1:T(8,128)} %get-tuple-element.741, s32[2048]{0:T(1024)S(1)} %bitcast_clamp_fusion.6), kind=kCustom, calls=%fused_computation.clone.clone.1 | custom fusion | bytes 57344 | tf_op jit(solution)/shard_map/while/body/eval_jaxpr/jit(_take)/gather | solution.py:98
  992.6 24.8 %gather_fusion.1 = f32[2048,3]{1,0:T(8,128)} fusion(f32[3,110593]{0,1:T(8,128)} %get-tuple-element.743, s32[2048]{0:T(1024)S(1)} %bitcast_clamp_fusion.6), kind=kCustom, calls=%fused_computation.2.clone.clone.1 | custom fusion | bytes 57344 | tf_op jit(solution)/shard_map/while/body/eval_jaxpr/jit(_take)/gather | solution.py:99
  1028.4 24.8 %gather_fusion = f32[2048,3]{1,0:T(8,128)} fusion(f32[3,110593]{0,1:T(8,128)} %get-tuple-element.741, s32[2048]{0:T(1024)S(1)} %bitcast_clamp_fusion.6), kind=kCustom, calls=%fused_computation.clone.clone.1 | custom fusion | bytes 57344 | tf_op jit(solution)/shard_map/while/body/eval_jaxpr/jit(_take)/gather | solution.py:98
  1053.9 24.8 %gather_fusion.1 = f32[2048,3]{1,0:T(8,128)} fusion(f32[3,110593]{0,1:T(8,128)} %get-tuple-element.743, s32[2048]{0:T(1024)S(1)} %bitcast_clamp_fusion.6), kind=kCustom, calls=%fused_computation.2.clone.clone.1 | custom fusion | bytes 57344 | tf_op jit(solution)/shard_map/while/body/eval_jaxpr/jit(_take)/gather | solution.py:99
  1089.7 24.8 %gather_fusion = f32[2048,3]{1,0:T(8,128)} fusion(f32[3,110593]{0,1:T(8,128)} %get-tuple-element.741, s32[2048]{0:T(1024)S(1)} %bitcast_clamp_fusion.6), kind=kCustom, calls=%fused_computation.clone.clone.1 | custom fusion | bytes 57344 | tf_op jit(solution)/shard_map/while/body/eval_jaxpr/jit(_take)/gather | solution.py:98
  1115.2 24.8 %gather_fusion.1 = f32[2048,3]{1,0:T(8,128)} fusion(f32[3,110593]{0,1:T(8,128)} %get-tuple-element.743, s32[2048]{0:T(1024)S(1)} %bitcast_clamp_fusion.6), kind=kCustom, calls=%fused_computation.2.clone.clone.1 | custom fusion | bytes 57344 | tf_op jit(solution)/shard_map/while/body/eval_jaxpr/jit(_take)/gather | solution.py:99
  1151.0 24.8 %gather_fusion = f32[2048,3]{1,0:T(8,128)} fusion(f32[3,110593]{0,1:T(8,128)} %get-tuple-element.741, s32[2048]{0:T(1024)S(1)} %bitcast_clamp_fusion.6), kind=kCustom, calls=%fused_computation.clone.clone.1 | custom fusion | bytes 57344 | tf_op jit(solution)/shard_map/while/body/eval_jaxpr/jit(_take)/gather | solution.py:98
  1212.4 24.8 %gather_fusion = f32[2048,3]{1,0:T(8,128)} fusion(f32[3,110593]{0,1:T(8,128)} %get-tuple-element.741, s32[2048]{0:T(1024)S(1)} %bitcast_clamp_fusion.6), kind=kCustom, calls=%fused_computation.clone.clone.1 | custom fusion | bytes 57344 | tf_op jit(solution)/shard_map/while/body/eval_jaxpr/jit(_take)/gather | solution.py:98
  1237.9 24.8 %gather_fusion.1 = f32[2048,3]{1,0:T(8,128)} fusion(f32[3,110593]{0,1:T(8,128)} %get-tuple-element.743, s32[2048]{0:T(1024)S(1)} %bitcast_clamp_fusion.6), kind=kCustom, calls=%fused_computation.2.clone.clone.1 | custom fusion | bytes 57344 | tf_op jit(solution)/shard_map/while/body/eval_jaxpr/jit(_take)/gather | solution.py:99
  1273.7 24.8 %gather_fusion = f32[2048,3]{1,0:T(8,128)} fusion(f32[3,110593]{0,1:T(8,128)} %get-tuple-element.741, s32[2048]{0:T(1024)S(1)} %bitcast_clamp_fusion.6), kind=kCustom, calls=%fused_computation.clone.clone.1 | custom fusion | bytes 57344 | tf_op jit(solution)/shard_map/while/body/eval_jaxpr/jit(_take)/gather | solution.py:98
  1299.2 24.8 %gather_fusion.1 = f32[2048,3]{1,0:T(8,128)} fusion(f32[3,110593]{0,1:T(8,128)} %get-tuple-element.743, s32[2048]{0:T(1024)S(1)} %bitcast_clamp_fusion.6), kind=kCustom, calls=%fused_computation.2.clone.clone.1 | custom fusion | bytes 57344 | tf_op jit(solution)/shard_map/while/body/eval_jaxpr/jit(_take)/gather | solution.py:99
  1335.0 24.8 %gather_fusion = f32[2048,3]{1,0:T(8,128)} fusion(f32[3,110593]{0,1:T(8,128)} %get-tuple-element.741, s32[2048]{0:T(1024)S(1)} %bitcast_clamp_fusion.6), kind=kCustom, calls=%fused_computation.clone.clone.1 | custom fusion | bytes 57344 | tf_op jit(solution)/shard_map/while/body/eval_jaxpr/jit(_take)/gather | solution.py:98
  1396.4 24.8 %gather_fusion = f32[2048,3]{1,0:T(8,128)} fusion(f32[3,110593]{0,1:T(8,128)} %get-tuple-element.741, s32[2048]{0:T(1024)S(1)} %bitcast_clamp_fusion.6), kind=kCustom, calls=%fused_computation.clone.clone.1 | custom fusion | bytes 57344 | tf_op jit(solution)/shard_map/while/body/eval_jaxpr/jit(_take)/gather | solution.py:98
  1421.9 24.8 %gather_fusion.1 = f32[2048,3]{1,0:T(8,128)} fusion(f32[3,110593]{0,1:T(8,128)} %get-tuple-element.743, s32[2048]{0:T(1024)S(1)} %bitcast_clamp_fusion.6), kind=kCustom, calls=%fused_computation.2.clone.clone.1 | custom fusion | bytes 57344 | tf_op jit(solution)/shard_map/while/body/eval_jaxpr/jit(_take)/gather | solution.py:99
  1457.7 24.8 %gather_fusion = f32[2048,3]{1,0:T(8,128)} fusion(f32[3,110593]{0,1:T(8,128)} %get-tuple-element.741, s32[2048]{0:T(1024)S(1)} %bitcast_clamp_fusion.6), kind=kCustom, calls=%fused_computation.clone.clone.1 | custom fusion | bytes 57344 | tf_op jit(solution)/shard_map/while/body/eval_jaxpr/jit(_take)/gather | solution.py:98
  1483.2 24.8 %gather_fusion.1 = f32[2048,3]{1,0:T(8,128)} fusion(f32[3,110593]{0,1:T(8,128)} %get-tuple-element.743, s32[2048]{0:T(1024)S(1)} %bitcast_clamp_fusion.6), kind=kCustom, calls=%fused_computation.2.clone.clone.1 | custom fusion | bytes 57344 | tf_op jit(solution)/shard_map/while/body/eval_jaxpr/jit(_take)/gather | solution.py:99
  1519.0 24.8 %gather_fusion = f32[2048,3]{1,0:T(8,128)} fusion(f32[3,110593]{0,1:T(8,128)} %get-tuple-element.741, s32[2048]{0:T(1024)S(1)} %bitcast_clamp_fusion.6), kind=kCustom, calls=%fused_computation.clone.clone.1 | custom fusion | bytes 57344 | tf_op jit(solution)/shard_map/while/body/eval_jaxpr/jit(_take)/gather | solution.py:98
  1580.4 24.8 %gather_fusion = f32[2048,3]{1,0:T(8,128)} fusion(f32[3,110593]{0,1:T(8,128)} %get-tuple-element.741, s32[2048]{0:T(1024)S(1)} %bitcast_clamp_fusion.6), kind=kCustom, calls=%fused_computation.clone.clone.1 | custom fusion | bytes 57344 | tf_op jit(solution)/shard_map/while/body/eval_jaxpr/jit(_take)/gather | solution.py:98
  1605.9 24.8 %gather_fusion.1 = f32[2048,3]{1,0:T(8,128)} fusion(f32[3,110593]{0,1:T(8,128)} %get-tuple-element.743, s32[2048]{0:T(1024)S(1)} %bitcast_clamp_fusion.6), kind=kCustom, calls=%fused_computation.2.clone.clone.1 | custom fusion | bytes 57344 | tf_op jit(solution)/shard_map/while/body/eval_jaxpr/jit(_take)/gather | solution.py:99
  1641.7 24.8 %gather_fusion = f32[2048,3]{1,0:T(8,128)} fusion(f32[3,110593]{0,1:T(8,128)} %get-tuple-element.741, s32[2048]{0:T(1024)S(1)} %bitcast_clamp_fusion.6), kind=kCustom, calls=%fused_computation.clone.clone.1 | custom fusion | bytes 57344 | tf_op jit(solution)/shard_map/while/body/eval_jaxpr/jit(_take)/gather | solution.py:98
  1667.2 24.8 %gather_fusion.1 = f32[2048,3]{1,0:T(8,128)} fusion(f32[3,110593]{0,1:T(8,128)} %get-tuple-element.743, s32[2048]{0:T(1024)S(1)} %bitcast_clamp_fusion.6), kind=kCustom, calls=%fused_computation.2.clone.clone.1 | custom fusion | bytes 57344 | tf_op jit(solution)/shard_map/while/body/eval_jaxpr/jit(_take)/gather | solution.py:99
  1703.0 24.8 %gather_fusion = f32[2048,3]{1,0:T(8,128)} fusion(f32[3,110593]{0,1:T(8,128)} %get-tuple-element.741, s32[2048]{0:T(1024)S(1)} %bitcast_clamp_fusion.6), kind=kCustom, calls=%fused_computation.clone.clone.1 | custom fusion | bytes 57344 | tf_op jit(solution)/shard_map/while/body/eval_jaxpr/jit(_take)/gather | solution.py:98
  1728.6 24.8 %gather_fusion.1 = f32[2048,3]{1,0:T(8,128)} fusion(f32[3,110593]{0,1:T(8,128)} %get-tuple-element.743, s32[2048]{0:T(1024)S(1)} %bitcast_clamp_fusion.6), kind=kCustom, calls=%fused_computation.2.clone.clone.1 | custom fusion | bytes 57344 | tf_op jit(solution)/shard_map/while/body/eval_jaxpr/jit(_take)/gather | solution.py:99
  1764.4 24.8 %gather_fusion = f32[2048,3]{1,0:T(8,128)} fusion(f32[3,110593]{0,1:T(8,128)} %get-tuple-element.741, s32[2048]{0:T(1024)S(1)} %bitcast_clamp_fusion.6), kind=kCustom, calls=%fused_computation.clone.clone.1 | custom fusion | bytes 57344 | tf_op jit(solution)/shard_map/while/body/eval_jaxpr/jit(_take)/gather | solution.py:98
  1789.9 24.8 %gather_fusion.1 = f32[2048,3]{1,0:T(8,128)} fusion(f32[3,110593]{0,1:T(8,128)} %get-tuple-element.743, s32[2048]{0:T(1024)S(1)} %bitcast_clamp_fusion.6), kind=kCustom, calls=%fused_computation.2.clone.clone.1 | custom fusion | bytes 57344 | tf_op jit(solution)/shard_map/while/body/eval_jaxpr/jit(_take)/gather | solution.py:99
  1825.7 24.8 %gather_fusion = f32[2048,3]{1,0:T(8,128)} fusion(f32[3,110593]{0,1:T(8,128)} %get-tuple-element.741, s32[2048]{0:T(1024)S(1)} %bitcast_clamp_fusion.6), kind=kCustom, calls=%fused_computation.clone.clone.1 | custom fusion | bytes 57344 | tf_op jit(solution)/shard_map/while/body/eval_jaxpr/jit(_take)/gather | solution.py:98
  1887.0 24.8 %gather_fusion = f32[2048,3]{1,0:T(8,128)} fusion(f32[3,110593]{0,1:T(8,128)} %get-tuple-element.741, s32[2048]{0:T(1024)S(1)} %bitcast_clamp_fusion.6), kind=kCustom, calls=%fused_computation.clone.clone.1 | custom fusion | bytes 57344 | tf_op jit(solution)/shard_map/while/body/eval_jaxpr/jit(_take)/gather | solution.py:98
  1912.5 24.8 %gather_fusion.1 = f32[2048,3]{1,0:T(8,128)} fusion(f32[3,110593]{0,1:T(8,128)} %get-tuple-element.743, s32[2048]{0:T(1024)S(1)} %bitcast_clamp_fusion.6), kind=kCustom, calls=%fused_computation.2.clone.clone.1 | custom fusion | bytes 57344 | tf_op jit(solution)/shard_map/while/body/eval_jaxpr/jit(_take)/gather | solution.py:99
  1948.4 24.8 %gather_fusion = f32[2048,3]{1,0:T(8,128)} fusion(f32[3,110593]{0,1:T(8,128)} %get-tuple-element.741, s32[2048]{0:T(1024)S(1)} %bitcast_clamp_fusion.6), kind=kCustom, calls=%fused_computation.clone.clone.1 | custom fusion | bytes 57344 | tf_op jit(solution)/shard_map/while/body/eval_jaxpr/jit(_take)/gather | solution.py:98
  2009.7 24.8 %gather_fusion = f32[2048,3]{1,0:T(8,128)} fusion(f32[3,110593]{0,1:T(8,128)} %get-tuple-element.741, s32[2048]{0:T(1024)S(1)} %bitcast_clamp_fusion.6), kind=kCustom, calls=%fused_computation.clone.clone.1 | custom fusion | bytes 57344 | tf_op jit(solution)/shard_map/while/body/eval_jaxpr/jit(_take)/gather | solution.py:98
  2071.0 24.8 %gather_fusion = f32[2048,3]{1,0:T(8,128)} fusion(f32[3,110593]{0,1:T(8,128)} %get-tuple-element.741, s32[2048]{0:T(1024)S(1)} %bitcast_clamp_fusion.6), kind=kCustom, calls=%fused_computation.clone.clone.1 | custom fusion | bytes 57344 | tf_op jit(solution)/shard_map/while/body/eval_jaxpr/jit(_take)/gather | solution.py:98
  2132.3 24.8 %gather_fusion = f32[2048,3]{1,0:T(8,128)} fusion(f32[3,110593]{0,1:T(8,128)} %get-tuple-element.741, s32[2048]{0:T(1024)S(1)} %bitcast_clamp_fusion.6), kind=kCustom, calls=%fused_computation.clone.clone.1 | custom fusion | bytes 57344 | tf_op jit(solution)/shard_map/while/body/eval_jaxpr/jit(_take)/gather | solution.py:98
  (589 shorter events, 974.8 us)
Async XLA Ops:
  0.6 21.5 copy-start
  1.9 8.0 copy-start.3
  1.9 8.1 copy-start.8
  1.9 8.2 copy-start.5
  2.8 12.1 collective-permute-start
  5.9 10.3 collective-permute-start.1
  10.1 4.8 copy-start.10
  17.2 22.0 collective-permute-start.3
  22.2 22.3 %collective-permute-start.2 = (f32[3,1,6,12288]{3,1,2,0:T(1,128)S(1)}, f32[3,1,6,12288]{3,1,2,0:T(1,128)}, u32[]{:S(2)}, u32[]{:S(2)}) collective-permute-start(f32[3,1,6,12288]{3,1,2,0:T(1,128)S(1)} %constant_dynamic-update-slice_fusion), channel_id=1, source_target_pairs={{0,1},{1,2},{2,3},{3,4},{4,5},{5,6},{6,7},{7,8},{8,9},{9,10},{10,1... | collective-permute-start | bytes 2654216 | tf_op jit(solution)/shard_map/ppermute | solution.py:36
  688.6 32.1 %copy-start.4 = (f32[3,12288]{1,0:T(4,128)S(1)}, f32[3,12288]{1,0:T(4,128)}, u32[]{:S(2)}) copy-start(f32[3,12288]{1,0:T(4,128)} %param.21) | copy-start | bytes 442372
  717.8 2.9 copy-start.2
  719.2 1477.5 %collective-permute-start.5 = (f32[3,3,12288]{2,1,0:T(4,128)}, f32[3,3,12288]{2,1,0:T(4,128)}, u32[]{:S(2)}, u32[]{:S(2)}) collective-permute-start(f32[3,3,12288]{2,1,0:T(4,128)} %get-tuple-element.560), channel_id=1, source_target_pairs={{0,15},{1,0},{2,1},{3,2},{4,3},{5,4},{6,5},{7,6},{8,7},{9,8},{10,9... | collective-permute-start | bytes 1327112 | tf_op jit(solution)/shard_map/ppermute | solution.py:27
  719.5 1477.2 %collective-permute-start.4 = (f32[3,3,12288]{2,1,0:T(4,128)}, f32[3,3,12288]{2,1,0:T(4,128)}, u32[]{:S(2)}, u32[]{:S(2)}) collective-permute-start(f32[3,3,12288]{2,1,0:T(4,128)} %get-tuple-element.559), channel_id=1, source_target_pairs={{0,1},{1,2},{2,3},{3,4},{4,5},{5,6},{6,7},{7,8},{8,9},{9,10},{10,1... | collective-permute-start | bytes 1327112 | tf_op jit(solution)/shard_map/ppermute | solution.py:27
  2192.9 10.8 copy-start.6
  2192.9 10.8 copy-start.7
  2193.0 15.2 copy-start.1
  2196.7 10.7 copy-start.9
  2198.4 8.9 collective-permute-start.7
  2202.2 5.2 collective-permute-start.6
where the time goes:
time: 2220 us; the launch traced here: 2210 us
  local copies, waits for them, and re-layouts  1730 us (78%)
  other arithmetic  431 us (19%)
    gather x24, local copies, waits for them, and re-layouts, solvent_add_group(): right_pos = jnp.take(flat_pos, chosen, axis=1)  596 us
    gather x24, local copies, waits for them, and re-layouts, solvent_add_group(): right_vel = jnp.take(flat_vel, chosen, axis=1)  596 us
    gather x4, local copies, waits for them, and re-layouts, contact_add_group(): right_pos = jnp.take(flat_pos, chosen_partner, axis=1)  99.2 us
    gather x4, local copies, waits for them, and re-layouts, contact_add_group(): right_vel = jnp.take(flat_vel, chosen_partner, axis=1)  99.2 us
    scatter-add x1, other arithmetic, dense_reaction(): jnp.zeros((3, flat_width), jnp.float32).at[:, mem_partner.reshape(-1)]  66.6 us
    scatter-add x4, other arithmetic, contact_add_group(): vertex_force.at[:, chosen_vertex.reshape(-1)]  61 us
    reduce_sum x28, other arithmetic, pair_terms(): jnp.sum(direction_unit * (left_vel[..., :, None] - right_vel[..., None, :...  56.7 us
    unnamed x26, local copies, waits for them, and re-layouts  52.3 us
  transfers between devices with their start and end apart: 8, of which 3 were waited for; matrix products, arithmetic and copies ran while one was open for 67% of the time, Pallas kernels for 0%

commit v1 on v0

v1 whole, which is shorter than its diff:
```python
import functools
from jax.sharding import PartitionSpec as P
import jax, jax.numpy as jnp
from jax import lax
from jax.experimental import pallas as pl
from jax.experimental.pallas import tpu as pltpu

f32, bf16 = jnp.float32, jnp.bfloat16
BOXES, TILE, PAIRS = 96, 128, 4
GROUP = 8

def split3(v):
    p1 = v.astype(bf16).astype(f32)
    rest = v - p1
    p2 = rest.astype(bf16).astype(f32)
    return p1, p2, rest - p2

NT = (((1,), (1,)), ((), ()))

def row_of(blk):
    return blk + (blk // BOXES) * (5 * BOXES)

def gather_block(tab_ref, blk, low, high, held, row):
    n = blk // BOXES
    dx = ((n // 3) - 1).astype(f32) * 4.0
    dy = ((n % 3) - 1).astype(f32) * 4.0
    block = tab_ref[pl.ds(row_of(blk), 6, stride=BOXES), :]
    got = jnp.take_along_axis(block, low, axis=1, mode="promise_in_bounds")
    got = got + jnp.where(row == 0, dx, jnp.where(row == 1, dy, 0.0))
    return jnp.where(high == blk, got, held)

def solvent_kernel(lo_ref, hi_ref, idx_ref, theta_ref, tab_ref, out_ref, held_ref):
    step = pl.program_id(0)
    tiles = GROUP * PAIRS
    row6 = lax.broadcasted_iota(jnp.int32, (6, TILE), 0)
    row8 = lax.broadcasted_iota(jnp.int32, (8, TILE), 0)
    far = jnp.where(row6 < 3, 1000.0, 0.0)

    @pl.loop(0, tiles // 8)
    def _(part):
        spread = jnp.int32(0)
        for k in range(8):
            t = part * 8 + k
            first = lo_ref[step * tiles + t]
            spread = jnp.maximum(spread, hi_ref[step * tiles + t] - first)
            index = jnp.broadcast_to(idx_ref[pl.ds(t, 1), :], (6, TILE))
            held_ref[t, 0:6, :] = gather_block(tab_ref, first, index & 127, index >> 7, far, row6)

        @pl.when(spread > 0)
        def _():
            @pl.loop(0, 8)
            def _(k):
                t = part * 8 + k
                index = jnp.broadcast_to(idx_ref[pl.ds(t, 1), :], (6, TILE))

                @pl.loop(lo_ref[step * tiles + t] + 1, hi_ref[step * tiles + t] + 1)
                def _(blk):
                    held_ref[t, 0:6, :] = gather_block(tab_ref, blk, index & 127, index >> 7, held_ref[t, 0:6, :], row6)

    @pl.loop(0, GROUP)
    def _(k):
        box = step * GROUP + k
        cx = (box % 2).astype(f32) * 2.0 + 1.0
        cy = (box // 2 % 2).astype(f32) * 2.0 + 1.0
        cz = (box // 4).astype(f32) * 2.0 + 1.0
        centre = jnp.where(row8 == 0, cx, jnp.where(row8 == 1, cy, jnp.where(row8 == 2, cz, 0.0)))
        own = tab_ref[pl.ds(row_of(4 * BOXES + box), 6, stride=BOXES), :] - centre[0:6]
        a, u = own[0:3], own[3:6] * 4.5
        aa = jnp.sum(a * a, axis=0, keepdims=True)
        au = jnp.sum(a * u, axis=0, keepdims=True)
        zero = jnp.zeros((3, TILE), f32)
        one = jnp.ones((1, TILE), f32)
        def left(q, const):
            q1, q2, q3 = split3(q)
            c1, c2, c3 = split3(const)
            last = jnp.where(row8 == 0, c1, jnp.where(row8 == 1, c2, jnp.where(row8 == 2, c3, 0.0)))
            return jnp.concatenate([q1, q1, q1, q2, q2, q3, last, jnp.zeros_like(last)], axis=0)
        ql = left(jnp.concatenate([-2.0 * a, zero, one, 0.0 * one], axis=0), aa)
        qs = left(jnp.concatenate([-u, -4.5 * a, 0.0 * one, 4.5 * one], axis=0), au)
        lhs = jnp.concatenate([ql.T, qs.T], axis=0).astype(bf16)
        vs, ws = [], []
        for j in range(PAIRS):
            held = held_ref[k * PAIRS + j] - centre
            b, w = held[0:3], held[3:6]
            bb = jnp.sum(b * b, axis=0, keepdims=True)
            bw = jnp.sum(b * w, axis=0, keepdims=True)
            full = jnp.where(row8 == 6, bb, jnp.where(row8 == 7, bw, held))
            p1, p2, p3 = split3(full)
            ones = jnp.ones_like(p1)
            vs.append(jnp.concatenate([p1, p2, p3, p1, p2, p1, ones, ones], axis=0).astype(bf16))
            v1 = jnp.where(row8 == 3, 1.0, p1)
            zz = jnp.zeros_like(p1)
            ws.append(jnp.concatenate([v1, jnp.where(row8 < 3, p2, 0.0), jnp.where(row8 < 3, p3, 0.0), zz], axis=0).astype(bf16))
        acc = jnp.zeros((32, TILE), f32)
        for h in range(2):
            rhs = jnp.concatenate(vs[2 * h:2 * h + 2], axis=1)
            out = jnp.dot(lhs, rhs, preferred_element_type=f32)
            r2, s = out[:TILE], out[TILE:]
            th = jnp.concatenate([theta_ref[k * PAIRS + 2 * h], theta_ref[k * PAIRS + 2 * h + 1]], axis=1).astype(f32)
            r2 = jnp.maximum(r2, 1e-12)
            q = lax.rsqrt(r2)
            g = jnp.maximum(jnp.minimum(q, 10.0) * (1.0 - r2 * q), 0.0)
            force = g * (25.0 + 30.0 * th - g * s)
            fh = force.astype(bf16)
            fl = (force - fh.astype(f32)).astype(bf16)
            wv = jnp.concatenate(ws[2 * h:2 * h + 2], axis=1)
            acc += lax.dot_general(wv, fh, NT, preferred_element_type=f32)
            acc += lax.dot_general(wv, fl, NT, preferred_element_type=f32)
        total = acc[0:8] + acc[8:16] + acc[16:24]
        res = a * acc[3:4] - total[0:3]
        out_ref[:, pl.ds(k, 1), :] = res[:, None, :]

def solvent(tab, idx, theta):
    tiles = idx.shape[0]
    hi = idx >> 7
    full = idx >= 9 * BOXES * TILE
    first = jnp.min(jnp.where(full, 9 * BOXES - 1, hi), axis=1)
    last = jnp.max(jnp.where(full, 0, hi), axis=1)
    last = jnp.maximum(first, last)
    return pl.pallas_call(
        solvent_kernel,
        out_shape=jax.ShapeDtypeStruct((3, BOXES, TILE), f32),
        grid=(BOXES // GROUP,),
        in_specs=[
            pl.BlockSpec(memory_space=pltpu.SMEM),
            pl.BlockSpec(memory_space=pltpu.SMEM),
            pl.BlockSpec((GROUP * PAIRS, TILE), lambda i: (i, 0)),
            pl.BlockSpec((GROUP * PAIRS, TILE, TILE), lambda i: (i, 0, 0)),
            pl.BlockSpec((9 * 6 * BOXES, TILE), lambda i: (0, 0), pipeline_mode=pl.Buffered(1)),
        ],
        out_specs=pl.BlockSpec((3, GROUP, TILE), lambda i: (0, i, 0)),
        scratch_shapes=[pltpu.VMEM((GROUP * PAIRS, 8, TILE), f32)],
        compiler_params=pltpu.CompilerParams(vmem_limit_bytes=40 * 2**20),
        cost_estimate=pl.CostEstimate(flops=10**10, bytes_accessed=2 * 10**7, transcendentals=0),
        name="solvent",
    )(first, last, idx, theta, tab.reshape(9 * 6 * BOXES, TILE))


V = 642
MEM_TILES = 64
MB = 96
WIN = 8
SPAN = 16

def gather_window(tab_ref, base, low, high, held):
    for k in range(WIN):
        block = tab_ref[pl.ds(base + k, 6, stride=MB), :]
        got = jnp.take_along_axis(block, low, axis=1, mode="promise_in_bounds")
        held = jnp.where(high == base + k, got, held)
    return held

def scatter_vertex(con_ref, base, low, high, pieces, rowt, row16):
    onehot = (rowt == low).astype(f32).astype(bf16)
    hit = high == row16 + base
    left = jnp.concatenate([jnp.where(hit, p[c:c + 1], 0.0) for p in pieces for c in range(3)], axis=0).astype(bf16)
    out = lax.dot_general(left, onehot, NT, preferred_element_type=f32)
    out = out[:3 * SPAN] + out[3 * SPAN:]
    for c in range(3):
        con_ref[c, pl.ds(base, SPAN), :] += out[c * SPAN:(c + 1) * SPAN]

def scatter_partner(rea_ref, blk, low, high, pieces, rowt):
    onehot = ((rowt == low) & (high == blk)).astype(f32).astype(bf16)
    out = lax.dot_general(pieces, onehot, NT, preferred_element_type=f32)
    out = (out[0:8] + out[8:16])[0:3]
    rea_ref[pl.ds(blk + (blk // BOXES) * (2 * BOXES), 3, stride=BOXES), :] += out

def contact_kernel(plo, phi, vlo, vhi, count, par_ref, ver_ref, tab_ref, mem_ref, con_ref, rea_ref, lh_ref, rh_ref, fo_ref):
    row6 = lax.broadcasted_iota(jnp.int32, (6, TILE), 0)
    row8 = lax.broadcasted_iota(jnp.int32, (8, TILE), 0)
    rowt = lax.broadcasted_iota(jnp.int32, (TILE, TILE), 0)
    row16 = lax.broadcasted_iota(jnp.int32, (SPAN, TILE), 0)
    far = jnp.where(row6 < 3, 1000.0, 0.0)
    alive_end = count[0] * V
    con_ref[...] = jnp.zeros_like(con_ref)
    rea_ref[...] = jnp.zeros_like(rea_ref)

    @pl.loop(0, MEM_TILES // 8)
    def _(part):
        spread = jnp.int32(0)
        vspread = jnp.int32(0)
        for k in range(8):
            t = part * 8 + k
            first = plo[t]
            spread = jnp.maximum(spread, phi[t] - first)
            vspread = jnp.maximum(vspread, vhi[t] - vlo[t])
            index = jnp.broadcast_to(par_ref[pl.ds(t, 1), :], (6, TILE))
            rh_ref[t, 0:6, :] = gather_block(tab_ref, first, index & 127, index >> 7, far, row6)
            vert = jnp.broadcast_to(ver_ref[pl.ds(t, 1), :], (6, TILE))
            high = jnp.where(vert < alive_end, vert >> 7, -1)
            lh_ref[t, 0:6, :] = gather_window(mem_ref, vlo[t], vert & 127, high, far)

        @pl.when(spread > 0)
        def _():
            @pl.loop(0, 8)
            def _(k):
                t = part * 8 + k
                index = jnp.broadcast_to(par_ref[pl.ds(t, 1), :], (6, TILE))

                @pl.loop(plo[t] + 1, phi[t] + 1)
                def _(blk):
                    rh_ref[t, 0:6, :] = gather_block(tab_ref, blk, index & 127, index >> 7, rh_ref[t, 0:6, :], row6)

        @pl.when(vspread >= WIN)
        def _():
            @pl.loop(0, 8)
            def _(k):
                t = part * 8 + k
                vert = jnp.broadcast_to(ver_ref[pl.ds(t, 1), :], (6, TILE))
                high = jnp.where(vert < alive_end, vert >> 7, -1)

                @pl.loop(1, (vhi[t] - vlo[t]) // WIN + 1)
                def _(j):
                    lh_ref[t, 0:6, :] = gather_window(mem_ref, vlo[t] + j * WIN, vert & 127, high, lh_ref[t, 0:6, :])

    unit = [jnp.where(row8 == c, 1.0, 0.0) for c in range(6)]
    scale = jnp.where(row8 < 3, 1.0, 4.5)

    @pl.loop(0, MEM_TILES)
    def _(t):
        blk = plo[t]
        n, box = blk // BOXES, blk % BOXES
        cx = (n // 3 - 1).astype(f32) * 4.0 + (box % 2).astype(f32) * 2.0 + 1.0
        cy = (n % 3 - 1).astype(f32) * 4.0 + (box // 2 % 2).astype(f32) * 2.0 + 1.0
        cz = (box // 4).astype(f32) * 2.0 + 1.0
        centre = jnp.where(row8 == 0, cx, jnp.where(row8 == 1, cy, jnp.where(row8 == 2, cz, 0.0)))
        live6 = row8 < 6
        lv = jnp.where(live6, lh_ref[t] - centre, 0.0)
        rv = jnp.where(live6, rh_ref[t] - centre, 0.0)
        a1, a2, a3 = split3(lv * scale)
        b1, b2, b3 = split3(rv * scale)
        one = jnp.ones_like(a1)
        zero = jnp.zeros_like(a1)
        left = jnp.concatenate([a1, a2, a3, one, one, one], axis=0).T.astype(bf16)
        diffs = []
        for c in range(6):
            rhs = jnp.concatenate([unit[c], unit[c], unit[c], -b1 * unit[c], -b2 * unit[c], -b3 * unit[c]], axis=0).astype(bf16)
            diffs.append(jnp.dot(left, rhs, preferred_element_type=f32))
        dx, dy, dz, du, dv, dw = diffs
        r2 = dx * dx + dy * dy + dz * dz
        s = dx * du + dy * dv + dz * dw
        r2 = jnp.maximum(r2, 1e-12)
        q = lax.rsqrt(r2)
        g = jnp.maximum(jnp.minimum(q, 10.0) * (1.0 - r2 * q), 0.0)
        force = g * (25.0 - g * s)
        fh = force.astype(bf16)
        fl = (force - fh.astype(f32)).astype(bf16)
        def sums(p1, p2, p3):
            one3 = jnp.where(row8 == 3, 1.0, jnp.where(row8 < 3, p1, 0.0))
            return jnp.concatenate([one3, jnp.where(row8 < 3, p2, 0.0), jnp.where(row8 < 3, p3, 0.0), zero], axis=0).astype(bf16)
        wb, wa = sums(b1, b2, b3), sums(a1, a2, a3)
        oc = lax.dot_general(wb, fh, NT, preferred_element_type=f32) + lax.dot_general(wb, fl, NT, preferred_element_type=f32)
        orr = jnp.dot(wa, fh, preferred_element_type=f32) + jnp.dot(wa, fl, preferred_element_type=f32)
        oc = oc[0:8] + oc[8:16] + oc[16:24]
        orr = orr[0:8] + orr[8:16] + orr[16:24]
        fo_ref[t, 0:8, :] = lv * oc[3:4] - oc
        fo_ref[t, 8:16, :] = rv * orr[3:4] - orr

    @pl.loop(0, MEM_TILES // 4)
    def _(part):
        for k in range(4):
            t = part * 4 + k
            con, rea = fo_ref[t, 0:8, :], fo_ref[t, 8:16, :]
            c1 = con.astype(bf16).astype(f32)
            vert = ver_ref[pl.ds(t, 1), :]
            base = pl.multiple_of(vlo[t] // 8 * 8, 8)
            scatter_vertex(con_ref, base, vert & 127, vert >> 7, (c1, con - c1), rowt, row16)

            @pl.loop(1, (vhi[t] - base) // SPAN + 1)
            def _(j):
                scatter_vertex(con_ref, pl.multiple_of(base + j * SPAN, 8), vert & 127, vert >> 7, (c1, con - c1), rowt, row16)

            rea = jnp.where(row8 < 3, rea, 0.0)
            r1 = rea.astype(bf16).astype(f32)
            pieces = jnp.concatenate([r1, rea - r1], axis=0).astype(bf16)
            index = par_ref[pl.ds(t, 1), :]
            scatter_partner(rea_ref, plo[t], index & 127, index >> 7, pieces, rowt)

            @pl.loop(plo[t] + 1, phi[t] + 1)
            def _(blk):
                scatter_partner(rea_ref, blk, index & 127, index >> 7, pieces, rowt)

def contact(tab, mpos, mvel, vertex, partner, count):
    mem = jnp.concatenate([mpos, mvel], axis=0)
    mem = jnp.pad(mem, ((0, 0), (0, MB * TILE - mem.shape[1]))).reshape(6 * MB, TILE)
    smem = pl.BlockSpec(memory_space=pltpu.SMEM)
    vmem = pl.BlockSpec(memory_space=pltpu.VMEM)
    con, rea = pl.pallas_call(
        contact_kernel,
        out_shape=(jax.ShapeDtypeStruct((3, MB, TILE), f32), jax.ShapeDtypeStruct((3 * 9 * BOXES, TILE), f32)),
        in_specs=[smem] * 5 + [vmem] * 4,
        out_specs=(vmem, vmem),
        scratch_shapes=[pltpu.VMEM((MEM_TILES, 8, TILE), f32), pltpu.VMEM((MEM_TILES, 8, TILE), f32), pltpu.VMEM((MEM_TILES, 16, TILE), f32)],
        compiler_params=pltpu.CompilerParams(vmem_limit_bytes=40 * 2**20),
        name="contact",
    )(jnp.min(partner, 1) >> 7, jnp.max(partner, 1) >> 7, jnp.min(vertex, 1) >> 7, jnp.max(vertex, 1) >> 7, count,
      partner, vertex, tab.reshape(9 * 6 * BOXES, TILE), mem)
    return con, rea.reshape(9, 3, BOXES, TILE)

TIME_STEP = 0.01
BENDING_MODULUS = 20.0
AREA_MODULUS = 40.0
SOLVENT_PUSH = 0.5

def moved(array, by_x, by_y):
    nx, ny = lax.axis_size("gx"), lax.axis_size("gy")
    pairs = [(i * ny + j, (i + by_x) % nx * ny + (j + by_y) % ny) for i in range(nx) for j in range(ny)]
    return lax.ppermute(array, ("gx", "gy"), pairs)

def membrane_forces(mem_pos, bending, rest_size, alive_mask):
    cells_here = rest_size.shape[0]
    shaped = mem_pos.reshape(3, cells_here, V)
    centre = jnp.mean(shaped, axis=2, keepdims=True)
    relative = shaped - centre
    bent_once = jnp.einsum("knv,uv->knu", relative, bending, precision=lax.Precision.HIGHEST)
    bent_twice = jnp.einsum("knv,uv->knu", bent_once, bending, precision=lax.Precision.HIGHEST)
    spread = jnp.sum(relative * relative, axis=(0, 2)) / V
    stretch = AREA_MODULUS * (spread / rest_size - 1.0)
    internal = -(BENDING_MODULUS * bent_twice + stretch[None, :, None] * relative) * alive_mask[None, :, None]
    return internal.reshape(3, cells_here * V)

def on_device(solvent_pos, solvent_vel, pair_index, random_pairs, membrane_pos, membrane_vel, mem_vertex, mem_partner,
              bending, rest_size, cell_count):
    vel = solvent_vel.reshape(3, BOXES, TILE)
    own = jnp.concatenate([solvent_pos.reshape(3, BOXES, TILE), vel], axis=0)[None]
    column = jnp.concatenate([moved(own, 0, 1), own, moved(own, 0, -1)], axis=0)
    tab = jnp.concatenate([moved(column, 1, 0), column, moved(column, -1, 0)], axis=0)
    alive_mask = (jnp.arange(rest_size.shape[0], dtype=jnp.int32) < cell_count[0]).astype(f32)
    internal = membrane_forces(membrane_pos, bending, rest_size, alive_mask)
    con, rea = contact(tab, membrane_pos, membrane_vel, mem_vertex, mem_partner, cell_count)
    back = [rea[3 * p + q] if (p, q) == (1, 1) else moved(rea[3 * p + q], p - 1, q - 1) for p in range(3) for q in range(3)]
    force = solvent(tab, pair_index, random_pairs)
    returned = sum(back[1:], back[0])
    push = jnp.array([SOLVENT_PUSH, 0.0, 0.0], f32)[:, None, None]
    solvent_velocity = (vel + TIME_STEP * (force + returned + push)).reshape(3, BOXES * TILE)
    touch = con.reshape(3, MB * TILE)[:, :membrane_pos.shape[1]]
    membrane_velocity = membrane_vel + TIME_STEP * (internal + touch)
    return solvent_velocity, membrane_velocity

def solution(mesh):
    both = ("gx", "gy")
    flat, tiles = P(None, both), P(both, None)
    return jax.shard_map(
        on_device,
        mesh=mesh,
        in_specs=(flat, flat, tiles, P(both, None, None), flat, flat, tiles, tiles, P(), P(both), P(both)),
        out_specs=(flat, flat),
        check_vma=False,
    )
```

time: 2220 us -> 173 us (0.08)
  local copies, waits for them, and re-layouts: 1730 us -> 7.7 us
  other arithmetic: 431 us -> 5.52 us
  Pallas kernels: 0 us -> 113 us
    gather x64 -> x0, local copies, waits for them, and re-layouts: 1470 us -> none  [the longest x24 596 us: solvent_add_group(): right_pos = jnp.take(flat_pos, chosen, axis=1)]
    reduce_sum x108 -> x0, other arithmetic: 142 us -> none  [the longest x28 56.7 us: pair_terms(): jnp.sum(direction_unit * (left_vel[..., :, None] - right_vel[..., None, :...]
    scatter-add x5 -> x0, other arithmetic: 128 us -> none  [the longest x1 66.6 us: dense_reaction(): jnp.zeros((3, flat_width), jnp.float32).at[:, mem_partner.reshape(-1)]]
    pallas_call x0 -> x2, Pallas kernels: none -> 113 us  [the longest x1 59 us: solvent(): pl.pallas_call(solvent_kernel, out_shape=jax.ShapeDtypeStruct((3, BOXES,...]
    concatenate x3 -> x1, local copies, waits for them, and re-layouts: 76.9 us -> 0.06 us  [on_device(): jnp.concatenate([moved(column, 1, 0), column, moved(column, -1, 0)], axis=0)]
    select_n x37 -> x0, other arithmetic: 64.3 us -> none  [the longest x24 45 us: solvent_add_group(): right_pos = jnp.take(flat_pos, chosen, axis=1)]
    unnamed x26 -> x21, local copies, waits for them, and re-layouts: 52.3 us -> 2.95 us
    mul x29 -> x0, other arithmetic: 40.2 us -> none  [the longest x28 40.2 us: pair_terms(): weight * (REPEL_STRENGTH - FRICTION * weight * approach + NOISE_SCALE * n...]
  transfers between devices with their start and end apart: 8 -> 12, of which waited for: 3 -> 2; matrix products, arithmetic and copies ran while one was open for 67% -> 9% of each run, Pallas kernels for 0% -> 34%
where the time goes in v1:
time: 173 us
  Pallas kernels  113 us (65%)
  starting transfers between devices  28.8 us (17%)
  waiting for transfers between devices  10.4 us (6%)
  local copies, waits for them, and re-layouts  7.7 us (4%)
  matrix products  5.89 us (3%)
  other arithmetic  5.52 us (3%)
    pallas_call x1, Pallas kernels, solvent(): pl.pallas_call(solvent_kernel, out_shape=jax.ShapeDtypeStruct((3, BOXES,...  59 us
    pallas_call x1, Pallas kernels, contact(): pl.pallas_call(contact_kernel, out_shape=(jax.ShapeDtypeStruct((3, MB, TI...  53.7 us
    ppermute x12, starting transfers between devices, moved(): return lax.ppermute(array, ('gx', 'gy'), pairs)  28.8 us
    ppermute x12, waiting for transfers between devices, moved(): return lax.ppermute(array, ('gx', 'gy'), pairs)  10.4 us
  transfers between devices with their start and end apart: 12, of which 2 were waited for; matrix products, arithmetic and copies ran while one was open for 9% of the time, Pallas kernels for 34%

profile of v1, /device:TPU:1, one launch (start us, length us, event | category | flops | bytes accessed | tf_op | source)
XLA Modules:
  0.0 172.7 jit_solution(17223417036653503576)
XLA Ops:
  0.6 0.0 copy-start
  0.6 0.0 copy-start.4
  0.7 1.2 copy_bitcast_fusion.2
  1.9 0.0 copy-start.7
  1.9 0.7 maximum_bitcast_fusion
  2.6 2.1 %collective-permute-start = (f32[1,6,96,128]{3,2,1,0:T(8,128)}, f32[1,6,96,128]{3,2,1,0:T(8,128)}, u32[]{:S(2)}, u32[]{:S(2)}) collective-permute-start(f32[1,6,96,128]{3,2,1,0:T(8,128)} %maximum_bitcast_fusion), channel_id=1, source_target_pairs={{0,1},{1,2},{2,3},{3,4},{4,5},{5,6},{6,7},{7,8},{8,9},{9,10},{10,1... | collective-permute-start | bytes 884744 | tf_op jit(solution)/shard_map/ppermute | solution.py:307
  4.7 3.6 %collective-permute-start.1 = (f32[1,6,96,128]{3,2,1,0:T(8,128)}, f32[1,6,96,128]{3,2,1,0:T(8,128)}, u32[]{:S(2)}, u32[]{:S(2)}) collective-permute-start(f32[1,6,96,128]{3,2,1,0:T(8,128)} %maximum_bitcast_fusion), channel_id=1, source_target_pairs={{0,15},{1,0},{2,1},{3,2},{4,3},{5,4},{6,5},{7,6},{8,7},{9,8},{10,9... | collective-permute-start | bytes 884744 | tf_op jit(solution)/shard_map/ppermute | solution.py:307
  9.0 1.1 reshape.66
  10.1 1.1 select_maximum_fusion
  11.2 0.1 reduce_sum.21
  11.3 2.5 %fusion.2 = f32[3,16,642]{2,1,0:T(8,128)} fusion(f32[642,642]{1,0:T(8,128)S(1)} %copy-done, f32[3,16,642]{2,1,0:T(8,128)S(1)} %reshape.66, f32[3,16]{1,0:T(4,128)S(1)} %broadcast_multiply_fusion), kind=kOutput, calls=%fused_computation.2 | convolution fusion | flops 237437280 | bytes 1895376 | tf_op jit(solution)/shard_map/knv,uv->knu/dot_general | solution.py:314
  13.8 0.1 sub.16
  13.9 0.9 sub.18
  14.7 1.0 multiply_reduce_fusion
  15.8 0.1 reduce_sum.27
  15.9 0.1 reduce_sum.28
  16.0 3.4 %fusion.13 = f32[3,16,642]{2,1,0:T(8,128)} fusion(f32[3,16,642]{2,1,0:T(8,128)} %fusion.2, f32[642,642]{1,0:T(8,128)S(1)} %copy-done, f32[3,16,642]{2,1,0:T(8,128)S(1)} %reshape.66, f32[16]{0:T(128)S(1)} %compare_convert_fusion, f32[16]{0:T(128)S(1)} %add_multiply_fusion, f32[3,16]{1,0:T(4,128)S(1)} %broadcast_multiply_fusion), kind=kOutput, calls=%fused_computation.7 | convolution fusion | flops 237591360 | bytes 2018768 | tf_op jit(solution)/shard_map/knv,uv->knu/dot_general | solution.py:315
  19.4 0.2 reshape.64.mem_ref
  19.6 1.1 reshape.67
  20.7 0.2 select_reduce_fusion
  20.9 0.1 fusion.20
  21.1 0.0 collective-permute-done.1
  21.1 1.2 pad_maximum_fusion
  22.3 2.6 %collective-permute-start.2 = (f32[3,6,96,128]{3,2,1,0:T(8,128)S(1)}, f32[3,6,96,128]{3,2,1,0:T(8,128)S(1)}, u32[]{:S(2)}, u32[]{:S(2)}) collective-permute-start(f32[3,6,96,128]{3,2,1,0:T(8,128)S(1)} %pad_maximum_fusion), channel_id=1, source_target_pairs={{0,16},{1,17},{2,18},{3,19},{4,20},{5,21},{6,22},{7,23},{8,24},{9,... | collective-permute-start | bytes 2654216 | tf_op jit(solution)/shard_map/ppermute | solution.py:307
  24.9 0.0 collective-permute-start.3
  24.9 10.0 %collective-permute-done.2 = f32[3,6,96,128]{3,2,1,0:T(8,128)S(1)} collective-permute-done((f32[3,6,96,128]{3,2,1,0:T(8,128)S(1)}, f32[3,6,96,128]{3,2,1,0:T(8,128)S(1)}, u32[]{:S(2)}, u32[]{:S(2)}) %collective-permute-start.2) | collective-permute-done | bytes 884768 | tf_op jit(solution)/shard_map/ppermute | solution.py:307
  34.9 0.1 constant_dynamic-update-slice_fusion.4
  35.0 1.0 constant_dynamic-update-slice_fusion.3
  36.0 1.0 constant_dynamic-update-slice_fusion.1
  37.0 0.4 collective-permute-done.3
  37.4 0.1 constant_dynamic-update-slice_fusion
  37.5 0.0 copy-start.5
  37.5 53.7 %contact.1 = (f32[3,96,128]{2,1,0:T(8,128)S(1)}, f32[2592,128]{1,0:T(8,128)S(1)}) custom-call(s32[64]{0:T(128)S(1)} %broadcast_shift-right-arithmetic_fusion.3.plo, s32[64]{0:T(128)S(1)} %broadcast_shift-right-arithmetic_fusion.2.phi, s32[64]{0:T(128)S(1)} %broadcast_shift-right-arithmetic_fusion.1.vlo, s32[64]{0:T(128)S(1)} %broadcast_shift-right-arithmetic_fusion.vhi, ...), custom_call_target="tpu_custom_call" | custom-call | tf_op jit(solution)/shard_map/contact/pallas_call | solution.py:287
  91.2 0.1 fusion.22
  91.3 2.1 %collective-permute-start.10 = (f32[3,96,128]{2,1,0:T(8,128)S(1)}, f32[3,96,128]{2,1,0:T(8,128)S(1)}, u32[]{:S(2)}, u32[]{:S(2)}) collective-permute-start(f32[3,96,128]{2,1,0:T(8,128)S(1)} %bitcast.60), channel_id=1, source_target_pairs={{0,16},{1,17},{2,18},{3,19},{4,20},{5,21},{6,22},{7,23},{8,24},{9,... | collective-permute-start | bytes 442376 | tf_op jit(solution)/shard_map/ppermute | solution.py:307
  93.4 0.0 collective-permute-start.11
  93.4 5.1 %collective-permute-start.4 = (f32[3,96,128]{2,1,0:T(8,128)S(1)}, f32[3,96,128]{2,1,0:T(8,128)S(1)}, u32[]{:S(2)}, u32[]{:S(2)}) collective-permute-start(f32[3,96,128]{2,1,0:T(8,128)S(1)} %bitcast.58), channel_id=1, source_target_pairs={{0,127},{1,112},{2,113},{3,114},{4,115},{5,116},{6,117},{7,118},{8... | collective-permute-start | bytes 442376 | tf_op jit(solution)/shard_map/ppermute | solution.py:307
  98.5 2.0 %collective-permute-start.5 = (f32[3,96,128]{2,1,0:T(8,128)S(1)}, f32[3,96,128]{2,1,0:T(8,128)S(1)}, u32[]{:S(2)}, u32[]{:S(2)}) collective-permute-start(f32[3,96,128]{2,1,0:T(8,128)S(1)} %bitcast.57), channel_id=1, source_target_pairs={{0,112},{1,113},{2,114},{3,115},{4,116},{5,117},{6,118},{7,119},{8... | collective-permute-start | bytes 442376 | tf_op jit(solution)/shard_map/ppermute | solution.py:307
  100.5 0.1 copy.22
  100.6 0.7 fusion.17
  101.3 0.0 collective-permute-done.10
  101.3 5.4 %collective-permute-start.7 = (f32[3,96,128]{2,1,0:T(8,128)S(1)}, f32[3,96,128]{2,1,0:T(8,128)S(1)}, u32[]{:S(2)}, u32[]{:S(2)}) collective-permute-start(f32[3,96,128]{2,1,0:T(8,128)S(1)} %bitcast.55), channel_id=1, source_target_pairs={{0,15},{1,0},{2,1},{3,2},{4,3},{5,4},{6,5},{7,6},{8,7},{9,8},{10,9... | collective-permute-start | bytes 442376 | tf_op jit(solution)/shard_map/ppermute | solution.py:307
  106.8 0.0 collective-permute-done.11
  106.8 0.0 copy-start.6
  106.8 5.9 %collective-permute-start.9 = (f32[3,96,128]{2,1,0:T(8,128)S(1)}, f32[3,96,128]{2,1,0:T(8,128)S(1)}, u32[]{:S(2)}, u32[]{:S(2)}) collective-permute-start(f32[3,96,128]{2,1,0:T(8,128)S(1)} %bitcast.53), channel_id=1, source_target_pairs={{0,31},{1,16},{2,17},{3,18},{4,19},{5,20},{6,21},{7,22},{8,23},{9,... | collective-permute-start | bytes 442376 | tf_op jit(solution)/shard_map/ppermute | solution.py:307
  112.6 59.0 %solvent.1 = f32[3,96,128]{2,1,0:T(8,128)S(1)} custom-call(s32[384]{0:T(512)S(1)} %get-tuple-element.7.lo_ref, s32[384]{0:T(512)S(1)} %max.3.hi_ref, s32[384,128]{1,0:T(8,128)S(1)} %copy-done.1, bf16[384,128,128]{2,1,0:T(8,128)(2,1)} %theta_ref.1, f32[5184,128]{1,0:T(8,128)S(1)} %bitcast.46), custom_call_target="tpu_custom_call" | custom-call | flops 10000000000 | bytes 20000000 | tf_op jit(solution)/shard_map/solvent/pallas_call | solution.py:120
  171.8 0.1 add_bitcast_fusion
  171.9 0.8 copy.23
  (29 shorter events, 0.1 us)
Async XLA Ops:
  0.6 10.6 %copy-start = (f32[642,642]{1,0:T(8,128)S(1)}, f32[642,642]{1,0:T(8,128)}, u32[]{:S(2)}) copy-start(f32[642,642]{1,0:T(8,128)} %param.20) | copy-start | bytes 4945972
  0.6 14.1 %copy-start.4 = (f32[3,10272]{1,0:T(4,128)S(1)}, f32[3,10272]{1,0:T(4,128)}, u32[]{:S(2)}) copy-start(f32[3,10272]{1,0:T(4,128)} %param.16) | copy-start | bytes 369796
  1.9 14.1 %copy-start.7 = (f32[16]{0:T(128)S(1)}, f32[16]{0:T(128)}, u32[]{:S(2)}) copy-start(f32[16]{0:T(128)} %param.21) | copy-start | bytes 196
  2.6 18.5 %collective-permute-start = (f32[1,6,96,128]{3,2,1,0:T(8,128)}, f32[1,6,96,128]{3,2,1,0:T(8,128)}, u32[]{:S(2)}, u32[]{:S(2)}) collective-permute-start(f32[1,6,96,128]{3,2,1,0:T(8,128)} %maximum_bitcast_fusion), channel_id=1, source_target_pairs={{0,1},{1,2},{2,3},{3,4},{4,5},{5,6},{6,7},{7,8},{8,9},{9,10},{10,1... | collective-permute-start | bytes 884744 | tf_op jit(solution)/shard_map/ppermute | solution.py:307
  4.7 16.4 %collective-permute-start.1 = (f32[1,6,96,128]{3,2,1,0:T(8,128)}, f32[1,6,96,128]{3,2,1,0:T(8,128)}, u32[]{:S(2)}, u32[]{:S(2)}) collective-permute-start(f32[1,6,96,128]{3,2,1,0:T(8,128)} %maximum_bitcast_fusion), channel_id=1, source_target_pairs={{0,15},{1,0},{2,1},{3,2},{4,3},{5,4},{6,5},{7,6},{8,7},{9,8},{10,9... | collective-permute-start | bytes 884744 | tf_op jit(solution)/shard_map/ppermute | solution.py:307
  13.8 6.9 %copy-start.1 = (s32[384,128]{1,0:T(8,128)S(1)}, s32[384,128]{1,0:T(8,128)}, u32[]{:S(2)}) copy-start(s32[384,128]{1,0:T(8,128)} %idx_ref.1) | copy-start | bytes 589828
  13.8 7.1 %copy-start.2 = (s32[64,128]{1,0:T(8,128)S(1)}, s32[64,128]{1,0:T(8,128)}, u32[]{:S(2)}) copy-start(s32[64,128]{1,0:T(8,128)} %ver_ref.1) | copy-start | bytes 98308
  13.8 7.1 %copy-start.3 = (s32[64,128]{1,0:T(8,128)S(1)}, s32[64,128]{1,0:T(8,128)}, u32[]{:S(2)}) copy-start(s32[64,128]{1,0:T(8,128)} %par_ref.1) | copy-start | bytes 98308
  22.3 12.6 %collective-permute-start.2 = (f32[3,6,96,128]{3,2,1,0:T(8,128)S(1)}, f32[3,6,96,128]{3,2,1,0:T(8,128)S(1)}, u32[]{:S(2)}, u32[]{:S(2)}) collective-permute-start(f32[3,6,96,128]{3,2,1,0:T(8,128)S(1)} %pad_maximum_fusion), channel_id=1, source_target_pairs={{0,16},{1,17},{2,18},{3,19},{4,20},{5,21},{6,22},{7,23},{8,24},{9,... | collective-permute-start | bytes 2654216 | tf_op jit(solution)/shard_map/ppermute | solution.py:307
  24.9 12.5 %collective-permute-start.3 = (f32[3,6,96,128]{3,2,1,0:T(8,128)S(1)}, f32[3,6,96,128]{3,2,1,0:T(8,128)S(1)}, u32[]{:S(2)}, u32[]{:S(2)}) collective-permute-start(f32[3,6,96,128]{3,2,1,0:T(8,128)S(1)} %pad_maximum_fusion), channel_id=1, source_target_pairs={{0,112},{1,113},{2,114},{3,115},{4,116},{5,117},{6,118},{7,119},{8... | collective-permute-start | bytes 2654216 | tf_op jit(solution)/shard_map/ppermute | solution.py:307
  37.5 63.1 %copy-start.5 = (f32[3,10272]{1,0:T(4,128)S(1)}, f32[3,10272]{1,0:T(4,128)}, u32[]{:S(2)}) copy-start(f32[3,10272]{1,0:T(4,128)} %param.17) | copy-start | bytes 369796
  91.3 10.0 %collective-permute-start.10 = (f32[3,96,128]{2,1,0:T(8,128)S(1)}, f32[3,96,128]{2,1,0:T(8,128)S(1)}, u32[]{:S(2)}, u32[]{:S(2)}) collective-permute-start(f32[3,96,128]{2,1,0:T(8,128)S(1)} %bitcast.60), channel_id=1, source_target_pairs={{0,16},{1,17},{2,18},{3,19},{4,20},{5,21},{6,22},{7,23},{8,24},{9,... | collective-permute-start | bytes 442376 | tf_op jit(solution)/shard_map/ppermute | solution.py:307
  93.4 13.4 %collective-permute-start.11 = (f32[3,96,128]{2,1,0:T(8,128)S(1)}, f32[3,96,128]{2,1,0:T(8,128)S(1)}, u32[]{:S(2)}, u32[]{:S(2)}) collective-permute-start(f32[3,96,128]{2,1,0:T(8,128)S(1)} %bitcast.59), channel_id=1, source_target_pairs={{0,17},{1,18},{2,19},{3,20},{4,21},{5,22},{6,23},{7,24},{8,25},{9,... | collective-permute-start | bytes 442376 | tf_op jit(solution)/shard_map/ppermute | solution.py:307
  93.4 13.4 %collective-permute-start.4 = (f32[3,96,128]{2,1,0:T(8,128)S(1)}, f32[3,96,128]{2,1,0:T(8,128)S(1)}, u32[]{:S(2)}, u32[]{:S(2)}) collective-permute-start(f32[3,96,128]{2,1,0:T(8,128)S(1)} %bitcast.58), channel_id=1, source_target_pairs={{0,127},{1,112},{2,113},{3,114},{4,115},{5,116},{6,117},{7,118},{8... | collective-permute-start | bytes 442376 | tf_op jit(solution)/shard_map/ppermute | solution.py:307
  98.5 73.2 %collective-permute-start.5 = (f32[3,96,128]{2,1,0:T(8,128)S(1)}, f32[3,96,128]{2,1,0:T(8,128)S(1)}, u32[]{:S(2)}, u32[]{:S(2)}) collective-permute-start(f32[3,96,128]{2,1,0:T(8,128)S(1)} %bitcast.57), channel_id=1, source_target_pairs={{0,112},{1,113},{2,114},{3,115},{4,116},{5,117},{6,118},{7,119},{8... | collective-permute-start | bytes 442376 | tf_op jit(solution)/shard_map/ppermute | solution.py:307
  100.5 71.2 %collective-permute-start.6 = (f32[3,96,128]{2,1,0:T(8,128)S(1)}, f32[3,96,128]{2,1,0:T(8,128)S(1)}, u32[]{:S(2)}, u32[]{:S(2)}) collective-permute-start(f32[3,96,128]{2,1,0:T(8,128)S(1)} %bitcast.56), channel_id=1, source_target_pairs={{0,113},{1,114},{2,115},{3,116},{4,117},{5,118},{6,119},{7,120},{8... | collective-permute-start | bytes 442376 | tf_op jit(solution)/shard_map/ppermute | solution.py:307
  101.3 70.4 %collective-permute-start.7 = (f32[3,96,128]{2,1,0:T(8,128)S(1)}, f32[3,96,128]{2,1,0:T(8,128)S(1)}, u32[]{:S(2)}, u32[]{:S(2)}) collective-permute-start(f32[3,96,128]{2,1,0:T(8,128)S(1)} %bitcast.55), channel_id=1, source_target_pairs={{0,15},{1,0},{2,1},{3,2},{4,3},{5,4},{6,5},{7,6},{8,7},{9,8},{10,9... | collective-permute-start | bytes 442376 | tf_op jit(solution)/shard_map/ppermute | solution.py:307
  106.8 65.0 %collective-permute-start.8 = (f32[3,96,128]{2,1,0:T(8,128)S(1)}, f32[3,96,128]{2,1,0:T(8,128)S(1)}, u32[]{:S(2)}, u32[]{:S(2)}) collective-permute-start(f32[3,96,128]{2,1,0:T(8,128)S(1)} %bitcast.54), channel_id=1, source_target_pairs={{0,1},{1,2},{2,3},{3,4},{4,5},{5,6},{6,7},{7,8},{8,9},{9,10},{10,1... | collective-permute-start | bytes 442376 | tf_op jit(solution)/shard_map/ppermute | solution.py:307
  106.8 65.0 %copy-start.6 = (f32[3]{0:T(128)S(1)}, f32[3]{0:T(128)}, u32[]{:S(2)}) copy-start(f32[3]{0:T(128)} %constant.33.clone) | copy-start | bytes 40
  106.8 64.9 %collective-permute-start.9 = (f32[3,96,128]{2,1,0:T(8,128)S(1)}, f32[3,96,128]{2,1,0:T(8,128)S(1)}, u32[]{:S(2)}, u32[]{:S(2)}) collective-permute-start(f32[3,96,128]{2,1,0:T(8,128)S(1)} %bitcast.53), channel_id=1, source_target_pairs={{0,31},{1,16},{2,17},{3,18},{4,19},{5,20},{6,21},{7,22},{8,23},{9,... | collective-permute-start | bytes 442376 | tf_op jit(solution)/shard_map/ppermute | solution.py:307

commit v2 on v1

v2 whole, which is shorter than its diff:
```python
import functools
from jax.sharding import PartitionSpec as P
import jax, jax.numpy as jnp
from jax import lax
from jax.experimental import pallas as pl
from jax.experimental.pallas import tpu as pltpu

f32, bf16 = jnp.float32, jnp.bfloat16
BOXES, TILE, PAIRS = 96, 128, 4
GROUP = 8
AHEAD = 1

def split3(v):
    p1 = v.astype(bf16).astype(f32)
    rest = v - p1
    p2 = rest.astype(bf16).astype(f32)
    return p1, p2, rest - p2

NT = (((1,), (1,)), ((), ()))

def part_of(blk):
    return (blk * 683) >> 16

def row_of(blk):
    return blk + part_of(blk) * (5 * BOXES)

def gather_block(tab_ref, blk, low, high, held, row):
    n = part_of(blk)
    p = (n * 11) >> 5
    dx = (p - 1).astype(f32) * 4.0
    dy = (n - 3 * p - 1).astype(f32) * 4.0
    block = tab_ref[pl.ds(blk + n * (5 * BOXES), 6, stride=BOXES), :]
    got = jnp.take_along_axis(block, low, axis=1, mode="promise_in_bounds")
    got = got + jnp.where(row == 0, dx, jnp.where(row == 1, dy, 0.0))
    return jnp.where(high == blk, got, held)

def box_centre(box, row8):
    cx = (box & 1).astype(f32) * 2.0 + 1.0
    cy = ((box >> 1) & 1).astype(f32) * 2.0 + 1.0
    cz = (box >> 2).astype(f32) * 2.0 + 1.0
    return jnp.where(row8 == 0, cx, jnp.where(row8 == 1, cy, jnp.where(row8 == 2, cz, 0.0)))

def own_features(own, row8):
    a, u = own[0:3], own[3:6] * 4.5
    aa = jnp.sum(a * a, axis=0, keepdims=True)
    au = jnp.sum(a * u, axis=0, keepdims=True)
    zero = jnp.zeros((3, TILE), f32)
    one = jnp.ones((1, TILE), f32)
    def left(q, const):
        q1, q2, q3 = split3(q)
        c1, c2, c3 = split3(const)
        last = jnp.where(row8 == 0, c1, jnp.where(row8 == 1, c2, jnp.where(row8 == 2, c3, 0.0)))
        return jnp.concatenate([q1, q1, q1, q2, q2, q3, last, jnp.zeros_like(last)], axis=0)
    ql = left(jnp.concatenate([-2.0 * a, zero, one, 0.0 * one], axis=0), aa)
    qs = left(jnp.concatenate([-u, -4.5 * a, 0.0 * one, 4.5 * one], axis=0), au)
    return jnp.concatenate([ql.T, qs.T], axis=0).astype(bf16)

def right_features(held, centre, row8):
    held = jnp.concatenate([held, held[0:2]], axis=0) - centre
    b, w = held[0:3], held[3:6]
    bb = jnp.sum(b * b, axis=0, keepdims=True)
    bw = jnp.sum(b * w, axis=0, keepdims=True)
    full = jnp.where(row8 == 6, bb, jnp.where(row8 == 7, bw, held))
    p1, p2, p3 = split3(full)
    ones = jnp.ones_like(p1)
    v1 = jnp.where(row8 == 3, 1.0, p1)
    return (jnp.concatenate([p1, p2, p3, p1, p2, p1, ones, ones], axis=0).astype(bf16),
            jnp.concatenate([v1, p2, p3, p3], axis=0).astype(bf16))

def pair_force(out, theta_ref, k, h):
    r2, s = out[:TILE], out[TILE:]
    th = jnp.concatenate([theta_ref[k * PAIRS + 2 * h], theta_ref[k * PAIRS + 2 * h + 1]], axis=1).astype(f32)
    r2 = jnp.maximum(r2, 1e-12)
    q = lax.rsqrt(r2)
    g = jnp.maximum(jnp.minimum(q, 10.0) * (1.0 - r2 * q), 0.0)
    force = g * (25.0 + 30.0 * th - g * s)
    fh = force.astype(bf16)
    return fh, (force - fh.astype(f32)).astype(bf16)

def solvent_kernel(lo_ref, hi_ref, idx_ref, theta1_ref, theta2_ref, tab_ref, out_ref, *held_refs):
    step = pl.program_id(0)
    steps = BOXES // GROUP // 2
    tiles = GROUP * PAIRS
    row6 = lax.broadcasted_iota(jnp.int32, (6, TILE), 0)
    row8 = lax.broadcasted_iota(jnp.int32, (8, TILE), 0)
    far = jnp.where(row6 < 3, 1000.0, 0.0)
    even, odd = held_refs[:3], held_refs[3:]

    def section(group, row, made, used, before, theta_ref):
        lhs_ref, rhs_ref, sum_ref = made
        spread = jnp.int32(0)
        products, forces = {}, {}

        def product(unit):
            k, h = divmod(unit, 2)
            at = pl.ds(h * 2 * TILE, 2 * TILE)
            products[unit] = jnp.dot(used[0][k], used[1][k, :, at], preferred_element_type=f32)

        def finish(k):
            acc = jnp.zeros((32, TILE), f32)
            for h in range(2):
                sums = used[2][k, :, pl.ds(h * 2 * TILE, 2 * TILE)]
                for force in forces.pop(2 * k + h):
                    acc += lax.dot_general(sums, force, NT, preferred_element_type=f32)
            total = acc[0:8] + acc[8:16] + acc[16:24]
            last = before * GROUP + k
            a = tab_ref[pl.ds(4 * 6 * BOXES + last, 6, stride=BOXES), :] - box_centre(last, row8)[0:6]
            out_ref[:, pl.ds(last, 1), :] = (a[0:3] * acc[3:4] - total[0:3])[:, None, :]

        for ahead in range(AHEAD):
            product(ahead)
        for k in range(GROUP):
            for h in range(2):
                unit = 2 * k + h
                if unit + AHEAD < 2 * GROUP:
                    product(unit + AHEAD)
                forces[unit] = pair_force(products.pop(unit), theta_ref, k, h)
            if k > 0:
                finish(k - 1)

            box = group * GROUP + k
            centre = box_centre(box, row8)
            own = tab_ref[pl.ds(4 * 6 * BOXES + box, 6, stride=BOXES), :]
            lhs_ref[k] = own_features(own - centre[0:6], row8)
            for j in range(PAIRS):
                t = k * PAIRS + j
                first = lo_ref[group * tiles + t]
                spread = jnp.maximum(spread, hi_ref[group * tiles + t] - first)
                index = jnp.broadcast_to(idx_ref[pl.ds(row + t, 1), :], (6, TILE))
                held = gather_block(tab_ref, first, index & 127, index >> 7, far, row6)
                at = pl.ds(j * TILE, TILE)
                rhs_ref[k, :, at], sum_ref[k, :, at] = right_features(held, centre, row8)
        finish(GROUP - 1)

        @pl.when(spread > 0)
        def _():
            for j in range(PAIRS):
                @pl.loop(0, GROUP)
                def _(k):
                    t = k * PAIRS + j
                    index = jnp.broadcast_to(idx_ref[pl.ds(row + t, 1), :], (6, TILE))
                    held = lax.fori_loop(
                        lo_ref[group * tiles + t], hi_ref[group * tiles + t] + 1,
                        lambda blk, held: gather_block(tab_ref, blk, index & 127, index >> 7, held, row6), far)
                    at = pl.ds(j * TILE, TILE)
                    rhs_ref[k, :, at], sum_ref[k, :, at] = right_features(held, box_centre(group * GROUP + k, row8), row8)

    @pl.when(step == 0)
    def _():
        for ref in odd:
            ref[...] = jnp.zeros_like(ref)

    section(jnp.minimum(step, steps - 1) * 2, 0, even, odd, jnp.maximum(2 * step - 1, 0), theta1_ref)

    @pl.when(step < steps)
    def _():
        section(step * 2 + 1, tiles, odd, even, step * 2, theta2_ref)

def solvent(tab, idx, theta):
    hi = idx >> 7
    full = idx >= 9 * BOXES * TILE
    first = jnp.min(jnp.where(full, 9 * BOXES - 1, hi), axis=1)
    last = jnp.max(jnp.where(full, 0, hi), axis=1)
    last = jnp.maximum(first, last)
    steps = BOXES // GROUP // 2
    return pl.pallas_call(
        solvent_kernel,
        out_shape=jax.ShapeDtypeStruct((3, BOXES, TILE), f32),
        grid=(BOXES // GROUP // 2 + 1,),
        in_specs=[
            pl.BlockSpec(memory_space=pltpu.SMEM),
            pl.BlockSpec(memory_space=pltpu.SMEM),
            pl.BlockSpec((2 * GROUP * PAIRS, TILE), lambda i: (jnp.minimum(i, steps - 1), 0)),
            pl.BlockSpec((GROUP * PAIRS, TILE, TILE), lambda i: (jnp.maximum(2 * i - 1, 0), 0, 0)),
            pl.BlockSpec((GROUP * PAIRS, TILE, TILE), lambda i: (jnp.minimum(2 * i, 2 * steps - 2), 0, 0)),
            pl.BlockSpec((9 * 6 * BOXES, TILE), lambda i: (0, 0), pipeline_mode=pl.Buffered(1)),
        ],
        out_specs=pl.BlockSpec((3, BOXES, TILE), lambda i: (0, 0, 0)),
        scratch_shapes=[pltpu.VMEM((GROUP, 256, 64), bf16), pltpu.VMEM((GROUP, 64, 512), bf16), pltpu.VMEM((GROUP, 32, 512), bf16)] * 2,
        compiler_params=pltpu.CompilerParams(vmem_limit_bytes=40 * 2**20),
        cost_estimate=pl.CostEstimate(flops=10**10, bytes_accessed=2 * 10**7, transcendentals=0),
        name="solvent",
    )(first, last, idx, theta, theta, tab.reshape(9 * 6 * BOXES, TILE))


V = 642
MEM_TILES = 64
MB = 96
WIN = 8
SPAN = 16
UNG, UNC, UNS = 16, 8, 16

def gather_window(tab_ref, base, low, high, held):
    for k in range(WIN):
        block = tab_ref[pl.ds(base + k, 6, stride=MB), :]
        got = jnp.take_along_axis(block, low, axis=1, mode="promise_in_bounds")
        held = jnp.where(high == base + k, got, held)
    return held

def vertex_sums(base, low, high, pieces, rowt, row16):
    onehot = (rowt == low).astype(f32).astype(bf16)
    hit = high == row16 + base
    left = jnp.concatenate([jnp.where(hit, p[c:c + 1], 0.0) for p in pieces for c in range(3)], axis=0).astype(bf16)
    out = lax.dot_general(left, onehot, NT, preferred_element_type=f32)
    return out[:3 * SPAN] + out[3 * SPAN:]

def add_vertex(con_ref, base, out):
    for c in range(3):
        con_ref[c, pl.ds(base, SPAN), :] += out[c * SPAN:(c + 1) * SPAN]

def partner_sums(blk, low, high, pieces, rowt):
    onehot = ((rowt == low) & (high == blk)).astype(f32).astype(bf16)
    out = lax.dot_general(pieces, onehot, NT, preferred_element_type=f32)
    return (out[0:8] + out[8:16])[0:3]

def add_partner(rea_ref, blk, out):
    rea_ref[pl.ds(blk + part_of(blk) * (2 * BOXES), 3, stride=BOXES), :] += out

def contact_kernel(plo, phi, vlo, vhi, count, par_ref, ver_ref, tab_ref, mem_ref, con_ref, rea_ref, lh_ref, rh_ref, fo_ref):
    row6 = lax.broadcasted_iota(jnp.int32, (6, TILE), 0)
    row8 = lax.broadcasted_iota(jnp.int32, (8, TILE), 0)
    rowt = lax.broadcasted_iota(jnp.int32, (TILE, TILE), 0)
    row16 = lax.broadcasted_iota(jnp.int32, (SPAN, TILE), 0)
    far = jnp.where(row6 < 3, 1000.0, 0.0)
    alive_end = count[0] * V
    con_ref[...] = jnp.zeros_like(con_ref)
    rea_ref[...] = jnp.zeros_like(rea_ref)

    @pl.loop(0, MEM_TILES // UNG)
    def _(part):
        spread = jnp.int32(0)
        vspread = jnp.int32(0)
        for k in range(UNG):
            t = part * UNG + k
            first = plo[t]
            spread = jnp.maximum(spread, phi[t] - first)
            vspread = jnp.maximum(vspread, vhi[t] - vlo[t])
            index = jnp.broadcast_to(par_ref[pl.ds(t, 1), :], (6, TILE))
            rh_ref[t, 0:6, :] = gather_block(tab_ref, first, index & 127, index >> 7, far, row6)
            vert = jnp.broadcast_to(ver_ref[pl.ds(t, 1), :], (6, TILE))
            high = jnp.where(vert < alive_end, vert >> 7, -1)
            lh_ref[t, 0:6, :] = gather_window(mem_ref, vlo[t], vert & 127, high, far)

        @pl.when(spread > 0)
        def _():
            @pl.loop(0, UNG)
            def _(k):
                t = part * UNG + k
                index = jnp.broadcast_to(par_ref[pl.ds(t, 1), :], (6, TILE))

                @pl.loop(plo[t] + 1, phi[t] + 1)
                def _(blk):
                    rh_ref[t, 0:6, :] = gather_block(tab_ref, blk, index & 127, index >> 7, rh_ref[t, 0:6, :], row6)

        @pl.when(vspread >= WIN)
        def _():
            @pl.loop(0, UNG)
            def _(k):
                t = part * UNG + k
                vert = jnp.broadcast_to(ver_ref[pl.ds(t, 1), :], (6, TILE))
                high = jnp.where(vert < alive_end, vert >> 7, -1)

                @pl.loop(1, (vhi[t] - vlo[t]) // WIN + 1)
                def _(j):
                    lh_ref[t, 0:6, :] = gather_window(mem_ref, vlo[t] + j * WIN, vert & 127, high, lh_ref[t, 0:6, :])

    def centre_of(blk):
        n = part_of(blk)
        box = blk - BOXES * n
        p = (n * 11) >> 5
        cx = ((p - 1) * 4 + (box & 1) * 2 + 1).astype(f32)
        cy = ((n - 3 * p - 1) * 4 + ((box >> 1) & 1) * 2 + 1).astype(f32)
        cz = ((box >> 2) * 2 + 1).astype(f32)
        return jnp.where(row8 == 0, cx, jnp.where(row8 == 1, cy, jnp.where(row8 == 2, cz, 0.0)))

    def store_forces(t, r2, s, centre, wa, wb):
        r2 = jnp.maximum(r2, 1e-12)
        q = lax.rsqrt(r2)
        g = jnp.maximum(jnp.minimum(q, 10.0) * (1.0 - r2 * q), 0.0)
        force = g * (25.0 - g * s)
        fh = force.astype(bf16)
        fl = (force - fh.astype(f32)).astype(bf16)
        con = lax.dot_general(wb, fh, NT, preferred_element_type=f32) + lax.dot_general(wb, fl, NT, preferred_element_type=f32)
        rea = jnp.dot(wa, fh, preferred_element_type=f32) + jnp.dot(wa, fl, preferred_element_type=f32)
        fo_ref[t, 0:8, :] = (lh_ref[t] - centre) * con[3:4] - (con[0:8] + con[8:16] + con[16:24])
        fo_ref[t, 8:16, :] = (rh_ref[t] - centre) * rea[3:4] - (rea[0:8] + rea[8:16] + rea[16:24])

    unit = [jnp.where(row8 == c, 1.0, 0.0) for c in range(6)]
    scale = jnp.where(row8 < 3, 1.0, 4.5)

    @pl.loop(0, MEM_TILES // UNC)
    def _(part):
        spread = jnp.int32(0)
        for k in range(UNC):
            t = part * UNC + k
            spread = jnp.maximum(spread, phi[t] - plo[t])
            centre = centre_of(plo[t])
            left, right = lh_ref[t, 0:6, :], rh_ref[t, 0:6, :]
            lhs = own_features(left - centre[0:6], row8)
            rhs, wb = right_features(right, centre, row8)
            wa = right_features(left, centre, row8)[1]
            out = jnp.dot(lhs, rhs, preferred_element_type=f32)
            store_forces(t, out[:TILE], out[TILE:], centre, wa, wb)

        @pl.when(spread > 0)
        def _():
            @pl.loop(0, UNC)
            def _(k):
                t = part * UNC + k
                centre = centre_of(plo[t])
                left, right = lh_ref[t, 0:6, :], rh_ref[t, 0:6, :]
                wb, wa = right_features(right, centre, row8)[1], right_features(left, centre, row8)[1]
                live6 = row8 < 6
                a1, a2, a3 = split3(jnp.where(live6, lh_ref[t] - centre, 0.0) * scale)
                b1, b2, b3 = split3(jnp.where(live6, rh_ref[t] - centre, 0.0) * scale)
                one = jnp.ones_like(a1)
                left = jnp.concatenate([a1, a2, a3, one, one, one], axis=0).T.astype(bf16)
                diffs = []
                for c in range(6):
                    rhs = jnp.concatenate([unit[c], unit[c], unit[c], -b1 * unit[c], -b2 * unit[c], -b3 * unit[c]], axis=0).astype(bf16)
                    diffs.append(jnp.dot(left, rhs, preferred_element_type=f32))
                dx, dy, dz, du, dv, dw = diffs
                store_forces(t, dx * dx + dy * dy + dz * dz, dx * du + dy * dv + dz * dw, centre, wa, wb)

    def pieces_of(t):
        con, rea = fo_ref[t, 0:8, :], jnp.where(row8 < 3, fo_ref[t, 8:16, :], 0.0)
        c1 = con.astype(bf16).astype(f32)
        r1 = rea.astype(bf16).astype(f32)
        return (c1, con - c1), jnp.concatenate([r1, rea - r1], axis=0).astype(bf16)

    @pl.loop(0, MEM_TILES // UNS)
    def _(part):
        more = jnp.int32(0)
        sums = []
        for k in range(UNS):
            t = part * UNS + k
            con, rea = pieces_of(t)
            vert, index = ver_ref[pl.ds(t, 1), :], par_ref[pl.ds(t, 1), :]
            base = pl.multiple_of((vlo[t] >> 3) << 3, 8)
            more = jnp.maximum(more, jnp.maximum(phi[t] - plo[t], (vhi[t] - base) >> 4))
            sums.append((base, vertex_sums(base, vert & 127, vert >> 7, con, rowt, row16),
                         plo[t], partner_sums(plo[t], index & 127, index >> 7, rea, rowt)))
        for base, con, blk, rea in sums:
            add_vertex(con_ref, base, con)
            add_partner(rea_ref, blk, rea)

        @pl.when(more > 0)
        def _():
            @pl.loop(0, UNS)
            def _(k):
                t = part * UNS + k
                con, rea = pieces_of(t)
                vert, index = ver_ref[pl.ds(t, 1), :], par_ref[pl.ds(t, 1), :]
                base = (vlo[t] >> 3) << 3

                @pl.loop(1, ((vhi[t] - base) >> 4) + 1)
                def _(j):
                    at = pl.multiple_of(base + j * SPAN, 8)
                    add_vertex(con_ref, at, vertex_sums(at, vert & 127, vert >> 7, con, rowt, row16))

                @pl.loop(plo[t] + 1, phi[t] + 1)
                def _(blk):
                    add_partner(rea_ref, blk, partner_sums(blk, index & 127, index >> 7, rea, rowt))

def contact(tab, mpos, mvel, vertex, partner, count):
    mem = jnp.concatenate([mpos, mvel], axis=0)
    mem = jnp.pad(mem, ((0, 0), (0, MB * TILE - mem.shape[1]))).reshape(6 * MB, TILE)
    smem = pl.BlockSpec(memory_space=pltpu.SMEM)
    vmem = pl.BlockSpec(memory_space=pltpu.VMEM)
    con, rea = pl.pallas_call(
        contact_kernel,
        out_shape=(jax.ShapeDtypeStruct((3, MB, TILE), f32), jax.ShapeDtypeStruct((3 * 9 * BOXES, TILE), f32)),
        in_specs=[smem] * 5 + [vmem] * 4,
        out_specs=(vmem, vmem),
        scratch_shapes=[pltpu.VMEM((MEM_TILES, 8, TILE), f32), pltpu.VMEM((MEM_TILES, 8, TILE), f32), pltpu.VMEM((MEM_TILES, 16, TILE), f32)],
        compiler_params=pltpu.CompilerParams(vmem_limit_bytes=40 * 2**20),
        name="contact",
    )(jnp.min(partner, 1) >> 7, jnp.max(partner, 1) >> 7, jnp.min(vertex, 1) >> 7, jnp.max(vertex, 1) >> 7, count,
      partner, vertex, tab.reshape(9 * 6 * BOXES, TILE), mem)
    return con, rea.reshape(9, 3, BOXES, TILE)

TIME_STEP = 0.01
BENDING_MODULUS = 20.0
AREA_MODULUS = 40.0
SOLVENT_PUSH = 0.5

MESH = pl.DeviceIdType.MESH
CHUNKS = 3

def halo_kernel(nx, ny, own_ref, x_ref, bend_ref, cell_ref, tab_ref, internal_ref, send_sem, recv_sem, own_sem):
    gx, gy = lax.axis_index("gx"), lax.axis_index("gy")
    up, down = (lax.rem(gx + 1, nx), gy), (lax.rem(gx + nx - 1, nx), gy)
    right, left = (gx, lax.rem(gy + 1, ny)), (gx, lax.rem(gy + ny - 1, ny))
    size = own_ref.shape[0]
    part = size // CHUNKS

    barrier = pltpu.get_barrier_semaphore()
    for device in (up, down, right, left):
        pl.semaphore_signal(barrier, inc=1, device_id=device, device_id_type=MESH)
    pl.semaphore_wait(barrier, 4)

    def slot(n, c):
        return tab_ref.at[pl.ds(n * size + c * part, part)]

    def copy(source, n, c, device):
        src = own_ref.at[pl.ds(c * part, part)] if source is None else slot(source, c)
        return pltpu.make_async_remote_copy(
            src_ref=src, dst_ref=slot(n, c), send_sem=send_sem.at[n, c], recv_sem=recv_sem.at[n, c],
            device_id=device, device_id_type=MESH)

    keep = pltpu.make_async_copy(own_ref, tab_ref.at[pl.ds(4 * size, size)], own_sem)
    keep.start()
    first = [[copy(None, 3, c, right), copy(None, 5, c, left)] for c in range(CHUNKS)]
    along = [[copy(None, 1, c, up), copy(None, 7, c, down)] for c in range(CHUNKS)]
    on = [[copy(3, 0, c, up), copy(3, 6, c, down), copy(5, 2, c, up), copy(5, 8, c, down)] for c in range(CHUNKS)]
    for c in range(CHUNKS):
        for one in first[c] + along[c]:
            one.start()

    x = x_ref[...]
    cells = x.shape[0] // 3
    relative = x - jnp.sum(x, axis=1, keepdims=True) * (1.0 / V)
    once = lax.dot_general(relative, bend_ref[...], NT, precision=lax.Precision.HIGHEST, preferred_element_type=f32)
    twice = lax.dot_general(once, bend_ref[...], NT, precision=lax.Precision.HIGHEST, preferred_element_type=f32)
    square = jnp.sum(relative * relative, axis=1, keepdims=True)
    spread = (square[:cells] + square[cells:2 * cells] + square[2 * cells:]) * (1.0 / V)
    stretch = AREA_MODULUS * (spread / cell_ref[:, 0:1] - 1.0)
    alive = cell_ref[:, 1:2]
    for d in range(3):
        rows = slice(d * cells, (d + 1) * cells)
        internal_ref[rows] = -(BENDING_MODULUS * twice[rows] + stretch * relative[rows]) * alive

    for c in range(CHUNKS):
        for k in range(2):
            first[c][k].wait_recv()
            on[c][2 * k].start()
            on[c][2 * k + 1].start()
    keep.wait()
    for c in range(CHUNKS):
        for one in first[c]:
            one.wait_send()
        for one in along[c] + on[c]:
            one.wait()

def halo(own, x, bending, cell):
    size = own.shape[0]
    nx, ny = lax.axis_size("gx"), lax.axis_size("gy")
    vmem, anywhere = pl.BlockSpec(memory_space=pltpu.VMEM), pl.BlockSpec(memory_space=pl.ANY)
    return pl.pallas_call(
        functools.partial(halo_kernel, nx, ny),
        out_shape=(jax.ShapeDtypeStruct((9 * size, TILE), f32), jax.ShapeDtypeStruct(x.shape, f32)),
        in_specs=[anywhere, vmem, vmem, vmem],
        out_specs=(anywhere, vmem),
        scratch_shapes=[pltpu.SemaphoreType.DMA((9, CHUNKS)), pltpu.SemaphoreType.DMA((9, CHUNKS)), pltpu.SemaphoreType.DMA],
        compiler_params=pltpu.CompilerParams(collective_id=0, has_side_effects=True, vmem_limit_bytes=30 * 2**20),
        name="halo",
    )(own, x, bending, cell)

def moved(array, by_x, by_y):
    nx, ny = lax.axis_size("gx"), lax.axis_size("gy")
    pairs = [(i * ny + j, (i + by_x) % nx * ny + (j + by_y) % ny) for i in range(nx) for j in range(ny)]
    return lax.ppermute(array, ("gx", "gy"), pairs)

def on_device(solvent_pos, solvent_vel, pair_index, random_pairs, membrane_pos, membrane_vel, mem_vertex, mem_partner,
              bending, rest_size, cell_count):
    cells = rest_size.shape[0]
    vel = solvent_vel.reshape(3, BOXES, TILE)
    own = jnp.concatenate([solvent_pos.reshape(3, BOXES, TILE), vel], axis=0).reshape(6 * BOXES, TILE)
    alive = (jnp.arange(cells, dtype=jnp.int32) < cell_count[0]).astype(f32)
    tab, internal = halo(own, membrane_pos.reshape(3 * cells, V), bending, jnp.stack([rest_size, alive], axis=1))
    con, rea = contact(tab, membrane_pos, membrane_vel, mem_vertex, mem_partner, cell_count)
    back = [rea[3 * p + q] if (p, q) == (1, 1) else moved(rea[3 * p + q], p - 1, q - 1) for p in range(3) for q in range(3)]
    force = solvent(tab, pair_index, random_pairs)
    returned = sum(back[1:], back[0])
    push = jnp.array([SOLVENT_PUSH, 0.0, 0.0], f32)[:, None, None]
    solvent_velocity = (vel + TIME_STEP * (force + returned + push)).reshape(3, BOXES * TILE)
    touch = con.reshape(3, MB * TILE)[:, :membrane_pos.shape[1]]
    membrane_velocity = membrane_vel + TIME_STEP * (internal.reshape(membrane_pos.shape) + touch)
    return solvent_velocity, membrane_velocity

def solution(mesh):
    both = ("gx", "gy")
    flat, tiles = P(None, both), P(both, None)
    return jax.shard_map(
        on_device,
        mesh=mesh,
        in_specs=(flat, flat, tiles, P(both, None, None), flat, flat, tiles, tiles, P(), P(both), P(both)),
        out_specs=(flat, flat),
        check_vma=False,
    )
```

time: 173 us -> 99.9 us (0.58)
  Pallas kernels: 113 us -> 66.4 us
  waiting for transfers between devices: 10.4 us -> 0.02 us
  starting transfers between devices: 28.8 us -> 18.9 us
  matrix products: 5.89 us -> 0 us
    pallas_call x1, Pallas kernels: 53.7 us -> 19.8 us  [contact(): pl.pallas_call(contact_kernel, out_shape=(jax.ShapeDtypeStruct((3, MB, TI...]
    pallas_call x1, Pallas kernels: 59 us -> 26.1 us  [solvent(): pl.pallas_call(solvent_kernel, out_shape=jax.ShapeDtypeStruct((3, BOXES,...]
    pallas_call x0 -> x1, Pallas kernels: none -> 20.5 us  [halo(): pl.pallas_call(functools.partial(halo_kernel, nx, ny), out_shape=(jax.Sha...]
    ppermute x12 -> x8, waiting for transfers between devices: 10.4 us -> 0.02 us  [moved(): return lax.ppermute(array, ('gx', 'gy'), pairs)]
    ppermute x12 -> x8, starting transfers between devices: 28.8 us -> 18.9 us  [moved(): return lax.ppermute(array, ('gx', 'gy'), pairs)]
    dot_general x2 -> x0, matrix products: 5.89 us -> none  [the longest x1 3.4 us: membrane_forces(): jnp.einsum('knv,uv->knu', bent_once, bending, precision=lax.Precision.HIG...]
  transfers between devices with their start and end apart: 12 -> 8, of which waited for: 2 -> 0; matrix products, arithmetic and copies ran while one was open for 9% -> 3% of each run, Pallas kernels for 34% -> 26%
where the time goes in v2:
time: 99.9 us; the launch traced here: 99.6 us
  Pallas kernels  66.4 us (66%)
  starting transfers between devices  18.9 us (19%)
  local copies, waits for them, and re-layouts  6.75 us (7%)
  other arithmetic  5.94 us (6%)
  between operations  1.52 us (2%)
    pallas_call x1, Pallas kernels, solvent(): pl.pallas_call(solvent_kernel, out_shape=jax.ShapeDtypeStruct((3, BOXES,...  26.1 us
    pallas_call x1, Pallas kernels, halo(): pl.pallas_call(functools.partial(halo_kernel, nx, ny), out_shape=(jax.Sha...  20.5 us
    pallas_call x1, Pallas kernels, contact(): pl.pallas_call(contact_kernel, out_shape=(jax.ShapeDtypeStruct((3, MB, TI...  19.8 us
    ppermute x8, starting transfers between devices, moved(): return lax.ppermute(array, ('gx', 'gy'), pairs)  18.9 us
    unnamed x14, local copies, waits for them, and re-layouts  2.46 us
  transfers between devices with their start and end apart: 8, of which 0 were waited for; matrix products, arithmetic and copies ran while one was open for 3% of the time, Pallas kernels for 26%

profile of v2, /device:TPU:1, one launch (start us, length us, event | category | flops | bytes accessed | tf_op | source)
XLA Modules:
  0.0 99.6 jit_solution(17829152067199275466)
XLA Ops:
  0.6 1.1 %reshape.61.x_ref = f32[48,642]{1,0:T(8,128)S(1)} reshape(f32[3,10272]{1,0:T(4,128)} %param.16) | data formatting | bytes 246528 | tf_op jit(solution)/shard_map/reshape | solution.py:470
  2.4 0.7 pad_maximum_fusion.1
  3.0 0.1 copy.15.cell_ref
  3.1 0.9 fusion.2
  4.1 1.1 %select_maximum_fusion = f32[6,12288]{1,0:T(8,128)S(1)} fusion(f32[3,10272]{1,0:T(4,128)} %param.17, f32[3,10272]{1,0:T(4,128)} %param.16), kind=kLoop, calls=%fused_computation | loop fusion | flops 294912 | bytes 541440 | tf_op jit(solution)/shard_map/concatenate | solution.py:366
  5.2 0.2 reshape.62.mem_ref
  5.3 0.0 copy-start.2
  5.4 0.0 copy-start.3
  5.4 1.1 %copy_bitcast_fusion.2 = (f32[3,96,128]{2,1,0:T(8,128)S(1)}, f32[3,96,128]{2,1,0:T(8,128)S(1)}) fusion(f32[1,3,96,128]{3,1,2,0:T(4,128)} %bitcast.32, f32[1,3,96,128]{3,1,2,0:T(4,128)} %bitcast.33), kind=kLoop, calls=%fused_computation.10 | loop fusion | bytes 589824 | tf_op jit(solution)/shard_map/reshape | solution.py:468
  6.5 0.0 copy-start
  6.5 1.5 %copy-done = f32[642,642]{1,0:T(8,128)S(1)} copy-done((f32[642,642]{1,0:T(8,128)S(1)}, f32[642,642]{1,0:T(8,128)}, u32[]{:S(2)}) %copy-start) | copy-done | bytes 1648680
  8.0 20.5 %halo.1 = (f32[5184,128]{1,0:T(8,128)S(1)}, f32[48,642]{1,0:T(8,128)S(1)}) custom-call(f32[576,128]{1,0:T(8,128)S(1)} %bitcast.28, f32[48,642]{1,0:T(8,128)S(1)} %reshape.61.x_ref, f32[642,642]{1,0:T(8,128)S(1)} %copy-done, f32[16,2]{1,0:T(8,128)S(1)} %copy.15.cell_ref), custom_call_target="tpu_custom_call" | custom-call | tf_op jit(solution)/shard_map/halo/pallas_call | solution.py:449
  28.5 0.0 copy-done.2
  28.5 0.0 copy-done.3
  28.5 19.8 %contact.1 = (f32[3,96,128]{2,1,0:T(8,128)S(1)}, f32[2592,128]{1,0:T(8,128)S(1)}) custom-call(s32[64]{0:T(128)S(1)} %broadcast_shift-right-arithmetic_fusion.3.plo, s32[64]{0:T(128)S(1)} %broadcast_shift-right-arithmetic_fusion.2.phi, s32[64]{0:T(128)S(1)} %broadcast_shift-right-arithmetic_fusion.1.vlo, s32[64]{0:T(128)S(1)} %broadcast_shift-right-arithmetic_fusion.vhi, ...), custom_call_target="tpu_custom_call" | custom-call | tf_op jit(solution)/shard_map/contact/pallas_call | solution.py:370
  48.3 0.0 copy-start.1
  48.3 1.1 %fusion.4 = (f32[288,128]{1,0:T(8,128)}, f32[288,128]{1,0:T(8,128)}, f32[288,128]{1,0:T(8,128)}, f32[288,128]{1,0:T(8,128)}, f32[288,128]{1,0:T(8,128)}, /*index...) fusion(f32[2592,128]{1,0:T(8,128)S(1)} %get-tuple-element.7), kind=kLoop, calls=%fused_computation.22 | loop fusion | bytes 2654208 | tf_op jit(solution)/shard_map/slice | solution.py:472
  49.4 0.8 collective-permute-start.7
  50.2 2.4 %collective-permute-start.6 = (f32[3,96,128]{2,1,0:T(8,128)}, f32[3,96,128]{2,1,0:T(8,128)}, u32[]{:S(2)}, u32[]{:S(2)}) collective-permute-start(f32[3,96,128]{2,1,0:T(8,128)} %bitcast.10), channel_id=1, source_target_pairs={{0,16},{1,17},{2,18},{3,19},{4,20},{5,21},{6,22},{7,23},{8,24},{9,... | collective-permute-start | bytes 442376 | tf_op jit(solution)/shard_map/ppermute | solution.py:462
  52.6 3.7 %collective-permute-start.5 = (f32[3,96,128]{2,1,0:T(8,128)}, f32[3,96,128]{2,1,0:T(8,128)}, u32[]{:S(2)}, u32[]{:S(2)}) collective-permute-start(f32[3,96,128]{2,1,0:T(8,128)} %bitcast.9), channel_id=1, source_target_pairs={{0,31},{1,16},{2,17},{3,18},{4,19},{5,20},{6,21},{7,22},{8,23},{9,... | collective-permute-start | bytes 442376 | tf_op jit(solution)/shard_map/ppermute | solution.py:462
  56.3 0.0 collective-permute-start.4
  56.3 4.8 %collective-permute-start.3 = (f32[3,96,128]{2,1,0:T(8,128)}, f32[3,96,128]{2,1,0:T(8,128)}, u32[]{:S(2)}, u32[]{:S(2)}) collective-permute-start(f32[3,96,128]{2,1,0:T(8,128)} %bitcast.6), channel_id=1, source_target_pairs={{0,15},{1,0},{2,1},{3,2},{4,3},{5,4},{6,5},{7,6},{8,7},{9,8},{10,9... | collective-permute-start | bytes 442376 | tf_op jit(solution)/shard_map/ppermute | solution.py:462
  61.0 0.9 reshape.64
  61.9 0.1 copy.24
  62.0 1.7 %fusion.1 = f32[3,10272]{1,0:T(4,128)} fusion(f32[3,10272]{1,0:T(4,128)} %param.17, f32[3,10272]{1,0:T(4,128)} %reshape.64, f32[3,12288]{1,0:T(4,128)S(1)} %bitcast.30), kind=kLoop, calls=%fused_computation.9 | loop fusion | flops 92448 | bytes 493056 | tf_op jit(solution)/shard_map/add | solution.py:478
  63.7 0.0 copy-done.1
  63.8 0.2 select_reduce_fusion
  63.9 0.0 collective-permute-done.7
  64.0 0.1 collective-permute-start.2
  64.0 0.0 collective-permute-done.6
  64.1 5.4 %collective-permute-start = (f32[3,96,128]{2,1,0:T(8,128)}, f32[3,96,128]{2,1,0:T(8,128)S(1)}, u32[]{:S(2)}, u32[]{:S(2)}) collective-permute-start(f32[3,96,128]{2,1,0:T(8,128)} %bitcast.36), channel_id=1, source_target_pairs={{0,127},{1,112},{2,113},{3,114},{4,115},{5,116},{6,117},{7,118},{8... | collective-permute-start | bytes 442376 | tf_op jit(solution)/shard_map/ppermute | solution.py:462
  69.4 0.0 collective-permute-done.5
  69.4 0.0 copy-start.4
  69.4 0.0 copy-start.5
  69.4 1.8 %collective-permute-start.1 = (f32[3,96,128]{2,1,0:T(8,128)}, f32[3,96,128]{2,1,0:T(8,128)S(1)}, u32[]{:S(2)}, u32[]{:S(2)}) collective-permute-start(f32[3,96,128]{2,1,0:T(8,128)} %bitcast.35), channel_id=1, source_target_pairs={{0,112},{1,113},{2,114},{3,115},{4,116},{5,117},{6,118},{7,119},{8... | collective-permute-start | bytes 442376 | tf_op jit(solution)/shard_map/ppermute | solution.py:462
  71.3 26.1 %solvent.1 = f32[3,96,128]{2,1,0:T(8,128)S(1)} custom-call(s32[384]{0:T(512)S(1)} %get-tuple-element.11.lo_ref, s32[384]{0:T(512)S(1)} %max.3.hi_ref, s32[384,128]{1,0:T(8,128)S(1)} %copy-done.1, bf16[384,128,128]{2,1,0:T(8,128)(2,1)} %theta2_ref.1, bf16[384,128,128]{2,1,0:T(8,128)(2,1)} %theta2_ref.1, f32[5184,128]{1,0:T(8,128)S(1)} %get-tuple-element.6.tab_ref), custom_call_target="tpu_custom_call" | custom-call | flops 10000000000 | bytes 20000000 | tf_op jit(solution)/shard_map/solvent/pallas_call | solution.py:166
  97.4 0.0 collective-permute-done.4
  97.4 0.0 collective-permute-done.3
  97.4 0.0 collective-permute-done.2
  97.4 0.0 collective-permute-done
  97.4 0.0 collective-permute-done.1
  97.5 0.0 copy-done.4
  97.5 0.0 copy-done.5
  97.5 1.3 %add_bitcast_fusion = f32[1,3,96,128]{3,2,1,0:T(8,128)S(1)} fusion(f32[3,96,128]{2,1,0:T(8,128)S(1)} %get-tuple-element.26, f32[3,96,128]{2,1,0:T(8,128)S(1)} %solvent.1, f32[3,96,128]{2,1,0:T(8,128)} %collective-permute-done.7, f32[3,96,128]{2,1,0:T(8,128)} %collective-permute-done.6, f32[3,96,128]{2,1,0:T(8,128)} %collective-permute-done.5, ...), kind=kLoop, calls=%fused_computation.12 | loop fusion | flops 442368 | bytes 1769484
  98.8 0.8 copy.25
  (7 shorter events, 0.0 us)
Async XLA Ops:
  5.3 23.2 %copy-start.2 = (s32[64,128]{1,0:T(8,128)S(1)}, s32[64,128]{1,0:T(8,128)}, u32[]{:S(2)}) copy-start(s32[64,128]{1,0:T(8,128)} %ver_ref.1) | copy-start | bytes 98308
  5.4 23.2 %copy-start.3 = (s32[64,128]{1,0:T(8,128)S(1)}, s32[64,128]{1,0:T(8,128)}, u32[]{:S(2)}) copy-start(s32[64,128]{1,0:T(8,128)} %par_ref.1) | copy-start | bytes 98308
  6.5 1.6 %copy-start = (f32[642,642]{1,0:T(8,128)S(1)}, f32[642,642]{1,0:T(8,128)}, u32[]{:S(2)}) copy-start(f32[642,642]{1,0:T(8,128)} %bend_ref.1) | copy-start | bytes 4945972
  48.3 15.4 %copy-start.1 = (s32[384,128]{1,0:T(8,128)S(1)}, s32[384,128]{1,0:T(8,128)}, u32[]{:S(2)}) copy-start(s32[384,128]{1,0:T(8,128)} %idx_ref.1) | copy-start | bytes 589828
  49.4 14.6 %collective-permute-start.7 = (f32[3,96,128]{2,1,0:T(8,128)}, f32[3,96,128]{2,1,0:T(8,128)}, u32[]{:S(2)}, u32[]{:S(2)}) collective-permute-start(f32[3,96,128]{2,1,0:T(8,128)} %bitcast.11), channel_id=1, source_target_pairs={{0,17},{1,18},{2,19},{3,20},{4,21},{5,22},{6,23},{7,24},{8,25},{9,... | collective-permute-start | bytes 442376 | tf_op jit(solution)/shard_map/ppermute | solution.py:462
  50.2 13.8 %collective-permute-start.6 = (f32[3,96,128]{2,1,0:T(8,128)}, f32[3,96,128]{2,1,0:T(8,128)}, u32[]{:S(2)}, u32[]{:S(2)}) collective-permute-start(f32[3,96,128]{2,1,0:T(8,128)} %bitcast.10), channel_id=1, source_target_pairs={{0,16},{1,17},{2,18},{3,19},{4,20},{5,21},{6,22},{7,23},{8,24},{9,... | collective-permute-start | bytes 442376 | tf_op jit(solution)/shard_map/ppermute | solution.py:462
  52.6 16.9 %collective-permute-start.5 = (f32[3,96,128]{2,1,0:T(8,128)}, f32[3,96,128]{2,1,0:T(8,128)}, u32[]{:S(2)}, u32[]{:S(2)}) collective-permute-start(f32[3,96,128]{2,1,0:T(8,128)} %bitcast.9), channel_id=1, source_target_pairs={{0,31},{1,16},{2,17},{3,18},{4,19},{5,20},{6,21},{7,22},{8,23},{9,... | collective-permute-start | bytes 442376 | tf_op jit(solution)/shard_map/ppermute | solution.py:462
  56.3 41.2 %collective-permute-start.4 = (f32[3,96,128]{2,1,0:T(8,128)}, f32[3,96,128]{2,1,0:T(8,128)}, u32[]{:S(2)}, u32[]{:S(2)}) collective-permute-start(f32[3,96,128]{2,1,0:T(8,128)} %bitcast.8), channel_id=1, source_target_pairs={{0,1},{1,2},{2,3},{3,4},{4,5},{5,6},{6,7},{7,8},{8,9},{9,10},{10,1... | collective-permute-start | bytes 442376 | tf_op jit(solution)/shard_map/ppermute | solution.py:462
  56.3 41.2 %collective-permute-start.3 = (f32[3,96,128]{2,1,0:T(8,128)}, f32[3,96,128]{2,1,0:T(8,128)}, u32[]{:S(2)}, u32[]{:S(2)}) collective-permute-start(f32[3,96,128]{2,1,0:T(8,128)} %bitcast.6), channel_id=1, source_target_pairs={{0,15},{1,0},{2,1},{3,2},{4,3},{5,4},{6,5},{7,6},{8,7},{9,8},{10,9... | collective-permute-start | bytes 442376 | tf_op jit(solution)/shard_map/ppermute | solution.py:462
  64.0 33.5 %collective-permute-start.2 = (f32[3,96,128]{2,1,0:T(8,128)}, f32[3,96,128]{2,1,0:T(8,128)S(1)}, u32[]{:S(2)}, u32[]{:S(2)}) collective-permute-start(f32[3,96,128]{2,1,0:T(8,128)} %bitcast.37), channel_id=1, source_target_pairs={{0,113},{1,114},{2,115},{3,116},{4,117},{5,118},{6,119},{7,120},{8... | collective-permute-start | bytes 442376 | tf_op jit(solution)/shard_map/ppermute | solution.py:462
  64.1 33.4 %collective-permute-start = (f32[3,96,128]{2,1,0:T(8,128)}, f32[3,96,128]{2,1,0:T(8,128)S(1)}, u32[]{:S(2)}, u32[]{:S(2)}) collective-permute-start(f32[3,96,128]{2,1,0:T(8,128)} %bitcast.36), channel_id=1, source_target_pairs={{0,127},{1,112},{2,113},{3,114},{4,115},{5,116},{6,117},{7,118},{8... | collective-permute-start | bytes 442376 | tf_op jit(solution)/shard_map/ppermute | solution.py:462
  69.4 28.0 %copy-start.4 = (f32[288,128]{1,0:T(8,128)S(1)}, f32[288,128]{1,0:T(8,128)}, u32[]{:S(2)}) copy-start(f32[288,128]{1,0:T(8,128)} %get-tuple-element.21) | copy-start | bytes 442372
  69.4 28.0 %copy-start.5 = (f32[3]{0:T(128)S(1)}, f32[3]{0:T(128)}, u32[]{:S(2)}) copy-start(f32[3]{0:T(128)} %constant.20.clone) | copy-start | bytes 40
  69.4 28.0 %collective-permute-start.1 = (f32[3,96,128]{2,1,0:T(8,128)}, f32[3,96,128]{2,1,0:T(8,128)S(1)}, u32[]{:S(2)}, u32[]{:S(2)}) collective-permute-start(f32[3,96,128]{2,1,0:T(8,128)} %bitcast.35), channel_id=1, source_target_pairs={{0,112},{1,113},{2,114},{3,115},{4,116},{5,117},{6,118},{7,119},{8... | collective-permute-start | bytes 442376 | tf_op jit(solution)/shard_map/ppermute | solution.py:462

commit v3 on v2

--- a/solution.py
+++ b/solution.py
@@ -8,7 +8,9 @@
 f32, bf16 = jnp.float32, jnp.bfloat16
 BOXES, TILE, PAIRS = 96, 128, 4
 GROUP = 8
-AHEAD = 1
+TIME_STEP = 0.01
+SOLVENT_PUSH = 0.5
+MESH = pl.DeviceIdType.MESH
 
 def split3(v):
     p1 = v.astype(bf16).astype(f32)
@@ -77,110 +79,86 @@
     fh = force.astype(bf16)
     return fh, (force - fh.astype(f32)).astype(bf16)
 
-def solvent_kernel(lo_ref, hi_ref, idx_ref, theta1_ref, theta2_ref, tab_ref, out_ref, *held_refs):
+def pair_kernel(nx, ny, held_ref, theta_ref, own_ref, rea_ref, out_ref, back_ref, send_sem, recv_sem, own_sem):
     step = pl.program_id(0)
-    steps = BOXES // GROUP // 2
-    tiles = GROUP * PAIRS
-    row6 = lax.broadcasted_iota(jnp.int32, (6, TILE), 0)
     row8 = lax.broadcasted_iota(jnp.int32, (8, TILE), 0)
-    far = jnp.where(row6 < 3, 1000.0, 0.0)
-    even, odd = held_refs[:3], held_refs[3:]
-
-    def section(group, row, made, used, before, theta_ref):
-        lhs_ref, rhs_ref, sum_ref = made
-        spread = jnp.int32(0)
-        products, forces = {}, {}
-
-        def product(unit):
-            k, h = divmod(unit, 2)
-            at = pl.ds(h * 2 * TILE, 2 * TILE)
-            products[unit] = jnp.dot(used[0][k], used[1][k, :, at], preferred_element_type=f32)
-
-        def finish(k):
-            acc = jnp.zeros((32, TILE), f32)
-            for h in range(2):
-                sums = used[2][k, :, pl.ds(h * 2 * TILE, 2 * TILE)]
-                for force in forces.pop(2 * k + h):
-                    acc += lax.dot_general(sums, force, NT, preferred_element_type=f32)
-            total = acc[0:8] + acc[8:16] + acc[16:24]
-            last = before * GROUP + k
-            a = tab_ref[pl.ds(4 * 6 * BOXES + last, 6, stride=BOXES), :] - box_centre(last, row8)[0:6]
-            out_ref[:, pl.ds(last, 1), :] = (a[0:3] * acc[3:4] - total[0:3])[:, None, :]
-
-        for ahead in range(AHEAD):
-            product(ahead)
-        for k in range(GROUP):
-            for h in range(2):
-                unit = 2 * k + h
-                if unit + AHEAD < 2 * GROUP:
-                    product(unit + AHEAD)
-                forces[unit] = pair_force(products.pop(unit), theta_ref, k, h)
-            if k > 0:
-                finish(k - 1)
-
-            box = group * GROUP + k
-            centre = box_centre(box, row8)
-            own = tab_ref[pl.ds(4 * 6 * BOXES + box, 6, stride=BOXES), :]
-            lhs_ref[k] = own_features(own - centre[0:6], row8)
-            for j in range(PAIRS):
-                t = k * PAIRS + j
-                first = lo_ref[group * tiles + t]
-                spread = jnp.maximum(spread, hi_ref[group * tiles + t] - first)
-                index = jnp.broadcast_to(idx_ref[pl.ds(row + t, 1), :], (6, TILE))
-                held = gather_block(tab_ref, first, index & 127, index >> 7, far, row6)
-                at = pl.ds(j * TILE, TILE)
-                rhs_ref[k, :, at], sum_ref[k, :, at] = right_features(held, centre, row8)
-        finish(GROUP - 1)
-
-        @pl.when(spread > 0)
-        def _():
-            for j in range(PAIRS):
-                @pl.loop(0, GROUP)
-                def _(k):
-                    t = k * PAIRS + j
-                    index = jnp.broadcast_to(idx_ref[pl.ds(row + t, 1), :], (6, TILE))
-                    held = lax.fori_loop(
-                        lo_ref[group * tiles + t], hi_ref[group * tiles + t] + 1,
-                        lambda blk, held: gather_block(tab_ref, blk, index & 127, index >> 7, held, row6), far)
-                    at = pl.ds(j * TILE, TILE)
-                    rhs_ref[k, :, at], sum_ref[k, :, at] = right_features(held, box_centre(group * GROUP + k, row8), row8)
+    gx, gy = lax.axis_index("gx"), lax.axis_index("gy")
+    size = 3 * BOXES
+
+    def slot(ref, n):
+        return ref.at[pl.ds(n * size, size)]
+
+    def device(n):
+        return (lax.rem(gx + n // 3 - 1 + nx, nx), lax.rem(gy + n % 3 - 1 + ny, ny))
+
+    others = [n for n in range(9) if n != 4]
+    sends = [pltpu.make_async_remote_copy(
+        src_ref=slot(rea_ref, n), dst_ref=slot(back_ref, n), send_sem=send_sem.at[n], recv_sem=recv_sem.at[n],
+        device_id=device(n), device_id_type=MESH) for n in others]
+    keep = pltpu.make_async_copy(slot(rea_ref, 4), slot(back_ref, 4), own_sem)
 
     @pl.when(step == 0)
     def _():
-        for ref in odd:
-            ref[...] = jnp.zeros_like(ref)
-
-    section(jnp.minimum(step, steps - 1) * 2, 0, even, odd, jnp.maximum(2 * step - 1, 0), theta1_ref)
-
-    @pl.when(step < steps)
+        barrier = pltpu.get_barrier_semaphore()
+        for n in others:
+            pl.semaphore_signal(barrier, inc=1, device_id=device(n), device_id_type=MESH)
+        pl.semaphore_wait(barrier, 8)
+        keep.start()
+        for send in sends:
+            send.start()
+
+    @pl.loop(0, GROUP, unroll=GROUP)
+    def _(k):
+        box = step * GROUP + k
+        centre = box_centre(box, row8)
+        own = own_ref[pl.ds(box, 6, stride=BOXES), :] - centre[0:6]
+        lhs = own_features(own, row8)
+        acc = jnp.zeros((32, TILE), f32)
+        for h in range(2):
+            feats = [right_features(held_ref[k * PAIRS + 2 * h + j, 0:6, :], centre, row8) for j in range(2)]
+            rhs, sums = [jnp.concatenate(parts, axis=1) for parts in zip(*feats)]
+            out = jnp.dot(lhs, rhs, preferred_element_type=f32)
+            for force in pair_force(out, theta_ref, k, h):
+                acc += lax.dot_general(sums, force, NT, preferred_element_type=f32)
+        out_ref[pl.ds(box, 3, stride=BOXES), :] = own[0:3] * acc[3:4] - (acc[0:8] + acc[8:16] + acc[16:24])[0:3]
+
+    @pl.when(step == BOXES // GROUP - 1)
     def _():
-        section(step * 2 + 1, tiles, odd, even, step * 2, theta2_ref)
-
-def solvent(tab, idx, theta):
-    hi = idx >> 7
-    full = idx >= 9 * BOXES * TILE
-    first = jnp.min(jnp.where(full, 9 * BOXES - 1, hi), axis=1)
-    last = jnp.max(jnp.where(full, 0, hi), axis=1)
-    last = jnp.maximum(first, last)
-    steps = BOXES // GROUP // 2
+        keep.wait()
+        for send in sends:
+            send.wait()
+        total = out_ref[...]
+        for n in range(9):
+            total += back_ref[pl.ds(n * size, size), :]
+        row = lax.broadcasted_iota(jnp.int32, (size, TILE), 0)
+        total += jnp.where(row < BOXES, SOLVENT_PUSH, 0.0)
+        out_ref[...] = own_ref[pl.ds(size, size), :] + TIME_STEP * total
+
+def pairs(held, theta, own, rea):
+    nx, ny = lax.axis_size("gx"), lax.axis_size("gy")
+    size = 3 * BOXES
     return pl.pallas_call(
-        solvent_kernel,
-        out_shape=jax.ShapeDtypeStruct((3, BOXES, TILE), f32),
-        grid=(BOXES // GROUP // 2 + 1,),
+        functools.partial(pair_kernel, nx, ny),
+        out_shape=jax.ShapeDtypeStruct((size, TILE), f32),
+        grid=(BOXES // GROUP,),
         in_specs=[
-            pl.BlockSpec(memory_space=pltpu.SMEM),
-            pl.BlockSpec(memory_space=pltpu.SMEM),
-            pl.BlockSpec((2 * GROUP * PAIRS, TILE), lambda i: (jnp.minimum(i, steps - 1), 0)),
-            pl.BlockSpec((GROUP * PAIRS, TILE, TILE), lambda i: (jnp.maximum(2 * i - 1, 0), 0, 0)),
-            pl.BlockSpec((GROUP * PAIRS, TILE, TILE), lambda i: (jnp.minimum(2 * i, 2 * steps - 2), 0, 0)),
-            pl.BlockSpec((9 * 6 * BOXES, TILE), lambda i: (0, 0), pipeline_mode=pl.Buffered(1)),
+            pl.BlockSpec((GROUP * PAIRS, 8, TILE), lambda i: (i, 0, 0)),
+            pl.BlockSpec((GROUP * PAIRS, TILE, TILE), lambda i: (i, 0, 0)),
+            pl.BlockSpec((2 * size, TILE), lambda i: (0, 0)),
+            pl.BlockSpec(memory_space=pl.ANY),
         ],
-        out_specs=pl.BlockSpec((3, BOXES, TILE), lambda i: (0, 0, 0)),
-        scratch_shapes=[pltpu.VMEM((GROUP, 256, 64), bf16), pltpu.VMEM((GROUP, 64, 512), bf16), pltpu.VMEM((GROUP, 32, 512), bf16)] * 2,
-        compiler_params=pltpu.CompilerParams(vmem_limit_bytes=40 * 2**20),
-        cost_estimate=pl.CostEstimate(flops=10**10, bytes_accessed=2 * 10**7, transcendentals=0),
-        name="solvent",
-    )(first, last, idx, theta, theta, tab.reshape(9 * 6 * BOXES, TILE))
+        out_specs=pl.BlockSpec((size, TILE), lambda i: (0, 0)),
+        scratch_shapes=[pltpu.VMEM((9 * size, TILE), f32), pltpu.SemaphoreType.DMA((9,)), pltpu.SemaphoreType.DMA((9,)), pltpu.SemaphoreType.DMA],
+        compiler_params=pltpu.CompilerParams(collective_id=1, has_side_effects=True, vmem_limit_bytes=40 * 2**20),
+        name="pairs",
+    )(held, theta, own, rea)
+
+def block_range(index, unused):
+    high = index >> 7
+    full = index >= unused
+    first = jnp.min(jnp.where(full, (unused >> 7) - 1, high), axis=1)
+    last = jnp.max(jnp.where(full, 0, high), axis=1)
+    return first, jnp.maximum(first, last)
 
 
 V = 642
@@ -216,7 +194,7 @@
 def add_partner(rea_ref, blk, out):
     rea_ref[pl.ds(blk + part_of(blk) * (2 * BOXES), 3, stride=BOXES), :] += out
 
-def contact_kernel(plo, phi, vlo, vhi, count, par_ref, ver_ref, tab_ref, mem_ref, con_ref, rea_ref, lh_ref, rh_ref, fo_ref):
+def contact_kernel(plo, phi, vlo, vhi, slo, shi, count, par_ref, ver_ref, idx_ref, tab_ref, mem_ref, con_ref, rea_ref, held_ref, lh_ref, rh_ref, fo_ref):
     row6 = lax.broadcasted_iota(jnp.int32, (6, TILE), 0)
     row8 = lax.broadcasted_iota(jnp.int32, (8, TILE), 0)
     rowt = lax.broadcasted_iota(jnp.int32, (TILE, TILE), 0)
@@ -225,6 +203,27 @@
     alive_end = count[0] * V
     con_ref[...] = jnp.zeros_like(con_ref)
     rea_ref[...] = jnp.zeros_like(rea_ref)
+
+    @pl.loop(0, idx_ref.shape[0] // UNG)
+    def _(part):
+        spread = jnp.int32(0)
+        for k in range(UNG):
+            t = part * UNG + k
+            first = slo[t]
+            spread = jnp.maximum(spread, shi[t] - first)
+            index = jnp.broadcast_to(idx_ref[pl.ds(t, 1), :], (6, TILE))
+            held_ref[t, 0:6, :] = gather_block(tab_ref, first, index & 127, index >> 7, far, row6)
+
+        @pl.when(spread > 0)
+        def _():
+            @pl.loop(0, UNG)
+            def _(k):
+                t = part * UNG + k
+                index = jnp.broadcast_to(idx_ref[pl.ds(t, 1), :], (6, TILE))
+
+                @pl.loop(slo[t] + 1, shi[t] + 1)
+                def _(blk):
+                    held_ref[t, 0:6, :] = gather_block(tab_ref, blk, index & 127, index >> 7, held_ref[t, 0:6, :], row6)
 
     @pl.loop(0, MEM_TILES // UNG)
     def _(part):
@@ -362,29 +361,28 @@
                 def _(blk):
                     add_partner(rea_ref, blk, partner_sums(blk, index & 127, index >> 7, rea, rowt))
 
-def contact(tab, mpos, mvel, vertex, partner, count):
-    mem = jnp.concatenate([mpos, mvel], axis=0)
-    mem = jnp.pad(mem, ((0, 0), (0, MB * TILE - mem.shape[1]))).reshape(6 * MB, TILE)
-    smem = pl.BlockSpec(memory_space=pltpu.SMEM)
-    vmem = pl.BlockSpec(memory_space=pltpu.VMEM)
-    con, rea = pl.pallas_call(
+def contact(tab, mem, vertex, partner, index, count):
+    smem, vmem = pl.BlockSpec(memory_space=pltpu.SMEM), pl.BlockSpec(memory_space=pltpu.VMEM)
+    unused = 9 * BOXES * TILE
+    tile = pltpu.VMEM((MEM_TILES, 8, TILE), f32)
+    return pl.pallas_call(
         contact_kernel,
-        out_shape=(jax.ShapeDtypeStruct((3, MB, TILE), f32), jax.ShapeDtypeStruct((3 * 9 * BOXES, TILE), f32)),
-        in_specs=[smem] * 5 + [vmem] * 4,
-        out_specs=(vmem, vmem),
-        scratch_shapes=[pltpu.VMEM((MEM_TILES, 8, TILE), f32), pltpu.VMEM((MEM_TILES, 8, TILE), f32), pltpu.VMEM((MEM_TILES, 16, TILE), f32)],
+        out_shape=(
+            jax.ShapeDtypeStruct((3, MB, TILE), f32),
+            jax.ShapeDtypeStruct((9 * 3 * BOXES, TILE), f32),
+            jax.ShapeDtypeStruct((index.shape[0], 8, TILE), f32),
+        ),
+        in_specs=[smem] * 7 + [vmem] * 5,
+        out_specs=(vmem, vmem, vmem),
+        scratch_shapes=[tile, tile, pltpu.VMEM((MEM_TILES, 16, TILE), f32)],
         compiler_params=pltpu.CompilerParams(vmem_limit_bytes=40 * 2**20),
         name="contact",
-    )(jnp.min(partner, 1) >> 7, jnp.max(partner, 1) >> 7, jnp.min(vertex, 1) >> 7, jnp.max(vertex, 1) >> 7, count,
-      partner, vertex, tab.reshape(9 * 6 * BOXES, TILE), mem)
-    return con, rea.reshape(9, 3, BOXES, TILE)
-
-TIME_STEP = 0.01
+    )(*block_range(partner, unused), *block_range(vertex, MB * TILE), *block_range(index, unused), count,
+      partner, vertex, index, tab, mem)
+
 BENDING_MODULUS = 20.0
 AREA_MODULUS = 40.0
-SOLVENT_PUSH = 0.5
-
-MESH = pl.DeviceIdType.MESH
+
 CHUNKS = 3
 
 def halo_kernel(nx, ny, own_ref, x_ref, bend_ref, cell_ref, tab_ref, internal_ref, send_sem, recv_sem, own_sem):
@@ -456,24 +454,16 @@
         name="halo",
     )(own, x, bending, cell)
 
-def moved(array, by_x, by_y):
-    nx, ny = lax.axis_size("gx"), lax.axis_size("gy")
-    pairs = [(i * ny + j, (i + by_x) % nx * ny + (j + by_y) % ny) for i in range(nx) for j in range(ny)]
-    return lax.ppermute(array, ("gx", "gy"), pairs)
-
 def on_device(solvent_pos, solvent_vel, pair_index, random_pairs, membrane_pos, membrane_vel, mem_vertex, mem_partner,
               bending, rest_size, cell_count):
     cells = rest_size.shape[0]
-    vel = solvent_vel.reshape(3, BOXES, TILE)
-    own = jnp.concatenate([solvent_pos.reshape(3, BOXES, TILE), vel], axis=0).reshape(6 * BOXES, TILE)
+    own = jnp.concatenate([solvent_pos, solvent_vel], axis=0).reshape(6 * BOXES, TILE)
     alive = (jnp.arange(cells, dtype=jnp.int32) < cell_count[0]).astype(f32)
     tab, internal = halo(own, membrane_pos.reshape(3 * cells, V), bending, jnp.stack([rest_size, alive], axis=1))
-    con, rea = contact(tab, membrane_pos, membrane_vel, mem_vertex, mem_partner, cell_count)
-    back = [rea[3 * p + q] if (p, q) == (1, 1) else moved(rea[3 * p + q], p - 1, q - 1) for p in range(3) for q in range(3)]
-    force = solvent(tab, pair_index, random_pairs)
-    returned = sum(back[1:], back[0])
-    push = jnp.array([SOLVENT_PUSH, 0.0, 0.0], f32)[:, None, None]
-    solvent_velocity = (vel + TIME_STEP * (force + returned + push)).reshape(3, BOXES * TILE)
+    mem = jnp.concatenate([membrane_pos, membrane_vel], axis=0)
+    mem = jnp.pad(mem, ((0, 0), (0, MB * TILE - mem.shape[1]))).reshape(6 * MB, TILE)
+    con, rea, held = contact(tab, mem, mem_vertex, mem_partner, pair_index, cell_count)
+    solvent_velocity = pairs(held, random_pairs, own, rea).reshape(3, BOXES * TILE)
     touch = con.reshape(3, MB * TILE)[:, :membrane_pos.shape[1]]
     membrane_velocity = membrane_vel + TIME_STEP * (internal.reshape(membrane_pos.shape) + touch)
     return solvent_velocity, membrane_velocity

time: 99.9 us -> 81.1 us (0.81)
  starting transfers between devices: 18.9 us -> 0 us
  Pallas kernels: 66.4 us -> 70.3 us
  local copies, waits for them, and re-layouts: 6.75 us -> 3.55 us
    ppermute x8 -> x0, starting transfers between devices: 18.9 us -> none  [moved(): return lax.ppermute(array, ('gx', 'gy'), pairs)]
    pallas_call x1, Pallas kernels: 19.8 us -> 23.1 us  [contact(): pl.pallas_call(contact_kernel, out_shape=(jax.ShapeDtypeStruct((3, MB, TI...]
    unnamed x14 -> x13, local copies, waits for them, and re-layouts: 2.46 us -> 0.14 us
    unnamed x1 -> x0, other arithmetic: 1.3 us -> none
    slice x1 -> x0, local copies, waits for them, and re-layouts: 1.06 us -> none  [on_device(): rea[3 * p + q]]
    reshape x2 -> x3, local copies, waits for them, and re-layouts: 1.2 us -> 2.05 us  [the longest x1 1.15 us: on_device(): jnp.pad(mem, ((0, 0), (0, MB * TILE - mem.shape[1]))).reshape(6 * MB, TILE)]
  transfers between devices with their start and end apart: 8 -> 0, of which waited for: 0 -> 0; matrix products, arithmetic and copies ran while one was open for 3% -> 0% of each run, Pallas kernels for 26% -> 0%
where the time goes in v3:
time: 81.1 us; the launch traced here: 80.8 us
  Pallas kernels  70.3 us (87%)
  other arithmetic  5.39 us (7%)
  local copies, waits for them, and re-layouts  3.55 us (4%)
  between operations  1.61 us (2%)
    pallas_call x1, Pallas kernels, pairs(): pl.pallas_call(functools.partial(pair_kernel, nx, ny), out_shape=jax.Shap...  26.6 us
    pallas_call x1, Pallas kernels, contact(): pl.pallas_call(contact_kernel, out_shape=(jax.ShapeDtypeStruct((3, MB, TI...  23.1 us
    pallas_call x1, Pallas kernels, halo(): pl.pallas_call(functools.partial(halo_kernel, nx, ny), out_shape=(jax.Sha...  20.6 us
    reduce_max x2, other arithmetic, block_range(): last = jnp.max(jnp.where(full, 0, high), axis=1)  2.05 us

profile of v3, /device:TPU:1, one launch (start us, length us, event | category | flops | bytes accessed | tf_op | source)
XLA Modules:
  0.0 80.8 jit_solution(16253285154529184175)
XLA Ops:
  0.6 0.0 copy-start.5
  0.6 0.0 copy-start.4
  0.7 0.0 copy-start
  1.5 0.7 pad_maximum_fusion.1
  2.1 0.9 %select_reduce_fusion.2 = (s32[64]{0:T(128)S(1)}, s32[64]{0:T(128)S(1)}, s32[64]{0:T(128)S(1)}, s32[64]{0:T(128)S(1)}) fusion(s32[64,128]{1,0:T(8,128)} %ver_ref.1, s32[64,128]{1,0:T(8,128)} %par_ref.1), kind=kLoop, calls=%fused_computation.10 | loop fusion | flops 98048 | bytes 66560 | tf_op jit(solution)/shard_map/reduce_max | solution.py:160
  3.1 1.1 %select_reduce_fusion = (s32[384]{0:T(512)S(1)}, s32[384]{0:T(512)S(1)}) fusion(s32[384,128]{1,0:T(8,128)} %idx_ref.1), kind=kLoop, calls=%fused_computation.4 | loop fusion | flops 294144 | bytes 199680 | tf_op jit(solution)/shard_map/reduce_max | solution.py:160
  4.2 0.1 copy.14.cell_ref
  4.3 1.1 %reshape.33.x_ref = f32[48,642]{1,0:T(8,128)S(1)} reshape(f32[3,10272]{1,0:T(4,128)} %param.15) | data formatting | bytes 246528 | tf_op jit(solution)/shard_map/reshape | solution.py:462
  5.4 1.1 %pad_maximum_fusion = f32[6,12288]{1,0:T(8,128)S(1)} fusion(f32[3,12288]{1,0:T(4,128)} %param.12, f32[3,12288]{1,0:T(4,128)} %param.11), kind=kLoop, calls=%fused_computation.2 | loop fusion | flops 73728 | bytes 589824 | tf_op jit(solution)/shard_map/concatenate | solution.py:460
  6.5 0.2 reshape.32.own_ref
  6.7 0.0 copy-done.5
  6.7 0.0 copy-done.4
  6.7 0.0 copy-start.1
  6.7 0.0 copy-start.2
  6.7 0.0 copy-start.3
  6.7 0.8 %select_maximum_fusion = f32[6,12288]{1,0:T(8,128)} fusion(f32[3,10272]{1,0:T(4,128)S(1)} %copy-done.5, f32[3,10272]{1,0:T(4,128)S(1)} %copy-done.4), kind=kLoop, calls=%fused_computation | loop fusion | flops 294912 | bytes 541440 | tf_op jit(solution)/shard_map/concatenate | solution.py:463
  7.5 1.1 %reshape.34.mem_ref = f32[576,128]{1,0:T(8,128)S(1)} reshape(f32[6,12288]{1,0:T(8,128)} %select_maximum_fusion) | data formatting | bytes 589824 | tf_op jit(solution)/shard_map/reshape | solution.py:464
  8.7 0.0 copy-done
  8.7 20.6 %halo.1 = (f32[5184,128]{1,0:T(8,128)S(1)}, f32[48,642]{1,0:T(8,128)S(1)}) custom-call(f32[576,128]{1,0:T(8,128)S(1)} %reshape.32.own_ref, f32[48,642]{1,0:T(8,128)S(1)} %reshape.33.x_ref, f32[642,642]{1,0:T(8,128)S(1)} %copy-done, f32[16,2]{1,0:T(8,128)S(1)} %copy.14.cell_ref), custom_call_target="tpu_custom_call" | custom-call | tf_op jit(solution)/shard_map/halo/pallas_call | solution.py:447
  29.3 0.0 copy-done.1
  29.3 0.0 copy-done.2
  29.3 0.0 copy-done.3
  29.3 23.1 %contact.1 = (f32[3,96,128]{2,1,0:T(8,128)S(1)}, f32[2592,128]{1,0:T(8,128)S(1)}, f32[384,8,128]{2,1,0:T(8,128)S(1)}) custom-call(s32[64]{0:T(128)S(1)} %get-tuple-element.18.plo, s32[64]{0:T(128)S(1)} %max.9.phi, s32[64]{0:T(128)S(1)} %get-tuple-element.15.vlo, s32[64]{0:T(128)S(1)} %max.10.vhi, s32[384]{0:T(512)S(1)} %get-tuple-element.13.slo, ...), custom_call_target="tpu_custom_call" | custom-call | tf_op jit(solution)/shard_map/contact/pallas_call | solution.py:368
  52.4 26.6 %pairs.1 = f32[288,128]{1,0:T(8,128)S(1)} custom-call(f32[384,8,128]{2,1,0:T(8,128)S(1)} %get-tuple-element.8.held_ref, bf16[384,128,128]{2,1,0:T(8,128)(2,1)} %theta_ref.1, f32[576,128]{1,0:T(8,128)S(1)} %reshape.32.own_ref, f32[2592,128]{1,0:T(8,128)S(1)} %get-tuple-element.9.rea_ref), custom_call_target="tpu_custom_call" | custom-call | tf_op jit(solution)/shard_map/pairs/pallas_call | solution.py:140
  79.0 0.8 reshape.35
  79.8 0.2 reshape.36
  80.0 0.1 copy.17
  80.1 0.7 fusion.1
  (4 shorter events, 0.0 us)
Async XLA Ops:
  0.6 6.0 %copy-start.5 = (f32[3,10272]{1,0:T(4,128)S(1)}, f32[3,10272]{1,0:T(4,128)}, u32[]{:S(2)}) copy-start(f32[3,10272]{1,0:T(4,128)} %param.16) | copy-start | bytes 369796
  0.6 6.0 %copy-start.4 = (f32[3,10272]{1,0:T(4,128)S(1)}, f32[3,10272]{1,0:T(4,128)}, u32[]{:S(2)}) copy-start(f32[3,10272]{1,0:T(4,128)} %param.15) | copy-start | bytes 369796
  0.7 8.0 %copy-start = (f32[642,642]{1,0:T(8,128)S(1)}, f32[642,642]{1,0:T(8,128)}, u32[]{:S(2)}) copy-start(f32[642,642]{1,0:T(8,128)} %bend_ref.1) | copy-start | bytes 4945972
  6.7 22.6 %copy-start.1 = (s32[384,128]{1,0:T(8,128)S(1)}, s32[384,128]{1,0:T(8,128)}, u32[]{:S(2)}) copy-start(s32[384,128]{1,0:T(8,128)} %idx_ref.1) | copy-start | bytes 589828
  6.7 22.6 %copy-start.2 = (s32[64,128]{1,0:T(8,128)S(1)}, s32[64,128]{1,0:T(8,128)}, u32[]{:S(2)}) copy-start(s32[64,128]{1,0:T(8,128)} %ver_ref.1) | copy-start | bytes 98308
  6.7 22.6 %copy-start.3 = (s32[64,128]{1,0:T(8,128)S(1)}, s32[64,128]{1,0:T(8,128)}, u32[]{:S(2)}) copy-start(s32[64,128]{1,0:T(8,128)} %par_ref.1) | copy-start | bytes 98308

commit v4 on v3

--- a/solution.py
+++ b/solution.py
@@ -79,33 +79,42 @@
     fh = force.astype(bf16)
     return fh, (force - fh.astype(f32)).astype(bf16)
 
-def pair_kernel(nx, ny, held_ref, theta_ref, own_ref, rea_ref, out_ref, back_ref, send_sem, recv_sem, own_sem):
+def pair_kernel(nx, ny, held_ref, theta_ref, own_ref, rea_ref, out_ref, row_ref, far_ref, back_ref, send_sem, recv_sem, own_sem):
     step = pl.program_id(0)
     row8 = lax.broadcasted_iota(jnp.int32, (8, TILE), 0)
     gx, gy = lax.axis_index("gx"), lax.axis_index("gy")
     size = 3 * BOXES
-
-    def slot(ref, n):
-        return ref.at[pl.ds(n * size, size)]
-
-    def device(n):
-        return (lax.rem(gx + n // 3 - 1 + nx, nx), lax.rem(gy + n % 3 - 1 + ny, ny))
-
-    others = [n for n in range(9) if n != 4]
-    sends = [pltpu.make_async_remote_copy(
-        src_ref=slot(rea_ref, n), dst_ref=slot(back_ref, n), send_sem=send_sem.at[n], recv_sem=recv_sem.at[n],
-        device_id=device(n), device_id_type=MESH) for n in others]
-    keep = pltpu.make_async_copy(slot(rea_ref, 4), slot(back_ref, 4), own_sem)
+    down, up = (lax.rem(gx + nx - 1, nx), gy), (lax.rem(gx + 1, nx), gy)
+    left, right = (gx, lax.rem(gy + ny - 1, ny)), (gx, lax.rem(gy + 1, ny))
+
+    def send(src, dst, k, device):
+        return pltpu.make_async_remote_copy(
+            src_ref=src, dst_ref=dst, send_sem=send_sem.at[k], recv_sem=recv_sem.at[k], device_id=device, device_id_type=MESH)
+
+    keep = pltpu.make_async_copy(rea_ref.at[pl.ds(3 * size, 3 * size)], row_ref, own_sem)
+    rows = [send(rea_ref.at[pl.ds(0, 3 * size)], far_ref.at[0], 0, down),
+            send(rea_ref.at[pl.ds(6 * size, 3 * size)], far_ref.at[1], 1, up)]
+    columns = [send(row_ref.at[pl.ds(0, size)], back_ref.at[0], 2, left),
+               send(row_ref.at[pl.ds(2 * size, size)], back_ref.at[1], 3, right)]
 
     @pl.when(step == 0)
     def _():
         barrier = pltpu.get_barrier_semaphore()
-        for n in others:
-            pl.semaphore_signal(barrier, inc=1, device_id=device(n), device_id_type=MESH)
-        pl.semaphore_wait(barrier, 8)
+        for device in (down, up, left, right):
+            pl.semaphore_signal(barrier, inc=1, device_id=device, device_id_type=MESH)
+        pl.semaphore_wait(barrier, 4)
         keep.start()
-        for send in sends:
-            send.start()
+        for one in rows:
+            one.start()
+
+    @pl.when(step == BOXES // GROUP // 2)
+    def _():
+        keep.wait()
+        for one in rows:
+            one.wait()
+        row_ref[...] += far_ref[0] + far_ref[1]
+        for one in columns:
+            one.start()
 
     @pl.loop(0, GROUP, unroll=GROUP)
     def _(k):
@@ -124,17 +133,14 @@
 
     @pl.when(step == BOXES // GROUP - 1)
     def _():
-        keep.wait()
-        for send in sends:
-            send.wait()
-        total = out_ref[...]
-        for n in range(9):
-            total += back_ref[pl.ds(n * size, size), :]
+        for one in columns:
+            one.wait()
+        total = out_ref[...] + row_ref[pl.ds(size, size), :] + back_ref[0] + back_ref[1]
         row = lax.broadcasted_iota(jnp.int32, (size, TILE), 0)
         total += jnp.where(row < BOXES, SOLVENT_PUSH, 0.0)
         out_ref[...] = own_ref[pl.ds(size, size), :] + TIME_STEP * total
 
-def pairs(held, theta, own, rea):
+def pairs(held, theta, tab, rea):
     nx, ny = lax.axis_size("gx"), lax.axis_size("gy")
     size = 3 * BOXES
     return pl.pallas_call(
@@ -144,21 +150,15 @@
         in_specs=[
             pl.BlockSpec((GROUP * PAIRS, 8, TILE), lambda i: (i, 0, 0)),
             pl.BlockSpec((GROUP * PAIRS, TILE, TILE), lambda i: (i, 0, 0)),
-            pl.BlockSpec((2 * size, TILE), lambda i: (0, 0)),
+            pl.BlockSpec((2 * size, TILE), lambda i: (4, 0)),
             pl.BlockSpec(memory_space=pl.ANY),
         ],
         out_specs=pl.BlockSpec((size, TILE), lambda i: (0, 0)),
-        scratch_shapes=[pltpu.VMEM((9 * size, TILE), f32), pltpu.SemaphoreType.DMA((9,)), pltpu.SemaphoreType.DMA((9,)), pltpu.SemaphoreType.DMA],
+        scratch_shapes=[pltpu.VMEM((3 * size, TILE), f32), pltpu.VMEM((2, 3 * size, TILE), f32), pltpu.VMEM((2, size, TILE), f32),
+                        pltpu.SemaphoreType.DMA((4,)), pltpu.SemaphoreType.DMA((4,)), pltpu.SemaphoreType.DMA],
         compiler_params=pltpu.CompilerParams(collective_id=1, has_side_effects=True, vmem_limit_bytes=40 * 2**20),
         name="pairs",
-    )(held, theta, own, rea)
-
-def block_range(index, unused):
-    high = index >> 7
-    full = index >= unused
-    first = jnp.min(jnp.where(full, (unused >> 7) - 1, high), axis=1)
-    last = jnp.max(jnp.where(full, 0, high), axis=1)
-    return first, jnp.maximum(first, last)
+    )(held, theta, tab, rea)
 
 
 V = 642
@@ -167,6 +167,7 @@
 WIN = 8
 SPAN = 16
 UNG, UNC, UNS = 16, 8, 16
+P_LOW, P_HIGH, V_LOW, V_HIGH = 6, 7, 8, 9
 
 def gather_window(tab_ref, base, low, high, held):
     for k in range(WIN):
@@ -194,7 +195,7 @@
 def add_partner(rea_ref, blk, out):
     rea_ref[pl.ds(blk + part_of(blk) * (2 * BOXES), 3, stride=BOXES), :] += out
 
-def contact_kernel(plo, phi, vlo, vhi, slo, shi, count, par_ref, ver_ref, idx_ref, tab_ref, mem_ref, con_ref, rea_ref, held_ref, lh_ref, rh_ref, fo_ref):
+def contact_kernel(range_ref, count, par_ref, ver_ref, idx_ref, tab_ref, mem_ref, internal_ref, vel_ref, rea_ref, held_ref, out_ref, con_ref, lh_ref, rh_ref, fo_ref, force_ref, sum_ref):
     row6 = lax.broadcasted_iota(jnp.int32, (6, TILE), 0)
     row8 = lax.broadcasted_iota(jnp.int32, (8, TILE), 0)
     rowt = lax.broadcasted_iota(jnp.int32, (TILE, TILE), 0)
@@ -209,8 +210,8 @@
         spread = jnp.int32(0)
         for k in range(UNG):
             t = part * UNG + k
-            first = slo[t]
-            spread = jnp.maximum(spread, shi[t] - first)
+            first = range_ref[t >> 7, t & 127]
+            spread = jnp.maximum(spread, range_ref[(t >> 7) + 3, t & 127] - first)
             index = jnp.broadcast_to(idx_ref[pl.ds(t, 1), :], (6, TILE))
             held_ref[t, 0:6, :] = gather_block(tab_ref, first, index & 127, index >> 7, far, row6)
 
@@ -221,7 +222,7 @@
                 t = part * UNG + k
                 index = jnp.broadcast_to(idx_ref[pl.ds(t, 1), :], (6, TILE))
 
-                @pl.loop(slo[t] + 1, shi[t] + 1)
+                @pl.loop(range_ref[t >> 7, t & 127] + 1, range_ref[(t >> 7) + 3, t & 127] + 1)
                 def _(blk):
                     held_ref[t, 0:6, :] = gather_block(tab_ref, blk, index & 127, index >> 7, held_ref[t, 0:6, :], row6)
 
@@ -231,14 +232,14 @@
         vspread = jnp.int32(0)
         for k in range(UNG):
             t = part * UNG + k
-            first = plo[t]
-            spread = jnp.maximum(spread, phi[t] - first)
-            vspread = jnp.maximum(vspread, vhi[t] - vlo[t])
+            first = range_ref[P_LOW, t]
+            spread = jnp.maximum(spread, range_ref[P_HIGH, t] - first)
+            vspread = jnp.maximum(vspread, range_ref[V_HIGH, t] - range_ref[V_LOW, t])
             index = jnp.broadcast_to(par_ref[pl.ds(t, 1), :], (6, TILE))
             rh_ref[t, 0:6, :] = gather_block(tab_ref, first, index & 127, index >> 7, far, row6)
             vert = jnp.broadcast_to(ver_ref[pl.ds(t, 1), :], (6, TILE))
             high = jnp.where(vert < alive_end, vert >> 7, -1)
-            lh_ref[t, 0:6, :] = gather_window(mem_ref, vlo[t], vert & 127, high, far)
+            lh_ref[t, 0:6, :] = gather_window(mem_ref, range_ref[V_LOW, t], vert & 127, high, far)
 
         @pl.when(spread > 0)
         def _():
@@ -247,7 +248,7 @@
                 t = part * UNG + k
                 index = jnp.broadcast_to(par_ref[pl.ds(t, 1), :], (6, TILE))
 
-                @pl.loop(plo[t] + 1, phi[t] + 1)
+                @pl.loop(range_ref[P_LOW, t] + 1, range_ref[P_HIGH, t] + 1)
                 def _(blk):
                     rh_ref[t, 0:6, :] = gather_block(tab_ref, blk, index & 127, index >> 7, rh_ref[t, 0:6, :], row6)
 
@@ -259,9 +260,9 @@
                 vert = jnp.broadcast_to(ver_ref[pl.ds(t, 1), :], (6, TILE))
                 high = jnp.where(vert < alive_end, vert >> 7, -1)
 
-                @pl.loop(1, (vhi[t] - vlo[t]) // WIN + 1)
+                @pl.loop(1, (range_ref[V_HIGH, t] - range_ref[V_LOW, t]) // WIN + 1)
                 def _(j):
-                    lh_ref[t, 0:6, :] = gather_window(mem_ref, vlo[t] + j * WIN, vert & 127, high, lh_ref[t, 0:6, :])
+                    lh_ref[t, 0:6, :] = gather_window(mem_ref, range_ref[V_LOW, t] + j * WIN, vert & 127, high, lh_ref[t, 0:6, :])
 
     def centre_of(blk):
         n = part_of(blk)
@@ -272,17 +273,15 @@
         cz = ((box >> 2) * 2 + 1).astype(f32)
         return jnp.where(row8 == 0, cx, jnp.where(row8 == 1, cy, jnp.where(row8 == 2, cz, 0.0)))
 
-    def store_forces(t, r2, s, centre, wa, wb):
+    def store_forces(t, r2, s, wa, wb):
         r2 = jnp.maximum(r2, 1e-12)
         q = lax.rsqrt(r2)
         g = jnp.maximum(jnp.minimum(q, 10.0) * (1.0 - r2 * q), 0.0)
         force = g * (25.0 - g * s)
-        fh = force.astype(bf16)
-        fl = (force - fh.astype(f32)).astype(bf16)
-        con = lax.dot_general(wb, fh, NT, preferred_element_type=f32) + lax.dot_general(wb, fl, NT, preferred_element_type=f32)
-        rea = jnp.dot(wa, fh, preferred_element_type=f32) + jnp.dot(wa, fl, preferred_element_type=f32)
-        fo_ref[t, 0:8, :] = (lh_ref[t] - centre) * con[3:4] - (con[0:8] + con[8:16] + con[16:24])
-        fo_ref[t, 8:16, :] = (rh_ref[t] - centre) * rea[3:4] - (rea[0:8] + rea[8:16] + rea[16:24])
+        force_ref[0, t] = force.astype(bf16)
+        force_ref[1, t] = (force - force_ref[0, t].astype(f32)).astype(bf16)
+        sum_ref[0, t] = wa
+        sum_ref[1, t] = wb
 
     unit = [jnp.where(row8 == c, 1.0, 0.0) for c in range(6)]
     scale = jnp.where(row8 < 3, 1.0, 4.5)
@@ -292,21 +291,21 @@
         spread = jnp.int32(0)
         for k in range(UNC):
             t = part * UNC + k
-            spread = jnp.maximum(spread, phi[t] - plo[t])
-            centre = centre_of(plo[t])
+            spread = jnp.maximum(spread, range_ref[P_HIGH, t] - range_ref[P_LOW, t])
+            centre = centre_of(range_ref[P_LOW, t])
             left, right = lh_ref[t, 0:6, :], rh_ref[t, 0:6, :]
             lhs = own_features(left - centre[0:6], row8)
             rhs, wb = right_features(right, centre, row8)
             wa = right_features(left, centre, row8)[1]
             out = jnp.dot(lhs, rhs, preferred_element_type=f32)
-            store_forces(t, out[:TILE], out[TILE:], centre, wa, wb)
+            store_forces(t, out[:TILE], out[TILE:], wa, wb)
 
         @pl.when(spread > 0)
         def _():
             @pl.loop(0, UNC)
             def _(k):
                 t = part * UNC + k
-                centre = centre_of(plo[t])
+                centre = centre_of(range_ref[P_LOW, t])
                 left, right = lh_ref[t, 0:6, :], rh_ref[t, 0:6, :]
                 wb, wa = right_features(right, centre, row8)[1], right_features(left, centre, row8)[1]
                 live6 = row8 < 6
@@ -319,7 +318,19 @@
                     rhs = jnp.concatenate([unit[c], unit[c], unit[c], -b1 * unit[c], -b2 * unit[c], -b3 * unit[c]], axis=0).astype(bf16)
                     diffs.append(jnp.dot(left, rhs, preferred_element_type=f32))
                 dx, dy, dz, du, dv, dw = diffs
-                store_forces(t, dx * dx + dy * dy + dz * dz, dx * du + dy * dv + dz * dw, centre, wa, wb)
+                store_forces(t, dx * dx + dy * dy + dz * dz, dx * du + dy * dv + dz * dw, wa, wb)
+
+    @pl.loop(0, MEM_TILES, unroll=UNC)
+    def _(t):
+        wb = sum_ref[1, t]
+        con = lax.dot_general(wb, force_ref[0, t], NT, preferred_element_type=f32) + lax.dot_general(wb, force_ref[1, t], NT, preferred_element_type=f32)
+        fo_ref[t, 0:8, :] = (lh_ref[t] - centre_of(range_ref[P_LOW, t])) * con[3:4] - (con[0:8] + con[8:16] + con[16:24])
+
+    @pl.loop(0, MEM_TILES, unroll=UNC)
+    def _(t):
+        wa = sum_ref[0, t]
+        rea = jnp.dot(wa, force_ref[0, t], preferred_element_type=f32) + jnp.dot(wa, force_ref[1, t], preferred_element_type=f32)
+        fo_ref[t, 8:16, :] = (rh_ref[t] - centre_of(range_ref[P_LOW, t])) * rea[3:4] - (rea[0:8] + rea[8:16] + rea[16:24])
 
     def pieces_of(t):
         con, rea = fo_ref[t, 0:8, :], jnp.where(row8 < 3, fo_ref[t, 8:16, :], 0.0)
@@ -335,10 +346,10 @@
             t = part * UNS + k
             con, rea = pieces_of(t)
             vert, index = ver_ref[pl.ds(t, 1), :], par_ref[pl.ds(t, 1), :]
-            base = pl.multiple_of((vlo[t] >> 3) << 3, 8)
-            more = jnp.maximum(more, jnp.maximum(phi[t] - plo[t], (vhi[t] - base) >> 4))
+            base = pl.multiple_of((range_ref[V_LOW, t] >> 3) << 3, 8)
+            more = jnp.maximum(more, jnp.maximum(range_ref[P_HIGH, t] - range_ref[P_LOW, t], (range_ref[V_HIGH, t] - base) >> 4))
             sums.append((base, vertex_sums(base, vert & 127, vert >> 7, con, rowt, row16),
-                         plo[t], partner_sums(plo[t], index & 127, index >> 7, rea, rowt)))
+                         range_ref[P_LOW, t], partner_sums(range_ref[P_LOW, t], index & 127, index >> 7, rea, rowt)))
         for base, con, blk, rea in sums:
             add_vertex(con_ref, base, con)
             add_partner(rea_ref, blk, rea)
@@ -350,42 +361,54 @@
                 t = part * UNS + k
                 con, rea = pieces_of(t)
                 vert, index = ver_ref[pl.ds(t, 1), :], par_ref[pl.ds(t, 1), :]
-                base = (vlo[t] >> 3) << 3
-
-                @pl.loop(1, ((vhi[t] - base) >> 4) + 1)
+                base = (range_ref[V_LOW, t] >> 3) << 3
+
+                @pl.loop(1, ((range_ref[V_HIGH, t] - base) >> 4) + 1)
                 def _(j):
                     at = pl.multiple_of(base + j * SPAN, 8)
                     add_vertex(con_ref, at, vertex_sums(at, vert & 127, vert >> 7, con, rowt, row16))
 
-                @pl.loop(plo[t] + 1, phi[t] + 1)
+                @pl.loop(range_ref[P_LOW, t] + 1, range_ref[P_HIGH, t] + 1)
                 def _(blk):
                     add_partner(rea_ref, blk, partner_sums(blk, index & 127, index >> 7, rea, rowt))
 
-def contact(tab, mem, vertex, partner, index, count):
+    width = out_ref.shape[1]
+    for blk in range(-(-width // TILE)):
+        at = slice(blk * TILE, min((blk + 1) * TILE, width))
+        out_ref[:, at] = vel_ref[:, at] + TIME_STEP * (internal_ref[:, at] + con_ref[:, blk, :at.stop - at.start])
+
+def contact(ranges, tab, mem, internal, vel, vertex, partner, index, count):
     smem, vmem = pl.BlockSpec(memory_space=pltpu.SMEM), pl.BlockSpec(memory_space=pltpu.VMEM)
-    unused = 9 * BOXES * TILE
     tile = pltpu.VMEM((MEM_TILES, 8, TILE), f32)
     return pl.pallas_call(
         contact_kernel,
         out_shape=(
-            jax.ShapeDtypeStruct((3, MB, TILE), f32),
             jax.ShapeDtypeStruct((9 * 3 * BOXES, TILE), f32),
             jax.ShapeDtypeStruct((index.shape[0], 8, TILE), f32),
+            jax.ShapeDtypeStruct(vel.shape, f32),
         ),
-        in_specs=[smem] * 7 + [vmem] * 5,
+        in_specs=[smem] * 2 + [vmem] * 7,
         out_specs=(vmem, vmem, vmem),
-        scratch_shapes=[tile, tile, pltpu.VMEM((MEM_TILES, 16, TILE), f32)],
+        scratch_shapes=[pltpu.VMEM((3, MB, TILE), f32), tile, tile, pltpu.VMEM((MEM_TILES, 16, TILE), f32),
+                        pltpu.VMEM((2, MEM_TILES, TILE, TILE), bf16), pltpu.VMEM((2, MEM_TILES, 32, TILE), bf16)],
         compiler_params=pltpu.CompilerParams(vmem_limit_bytes=40 * 2**20),
         name="contact",
-    )(*block_range(partner, unused), *block_range(vertex, MB * TILE), *block_range(index, unused), count,
-      partner, vertex, index, tab, mem)
+    )(ranges, count, partner, vertex, index, tab, mem, internal, vel)
 
 BENDING_MODULUS = 20.0
 AREA_MODULUS = 40.0
 
 CHUNKS = 3
 
-def halo_kernel(nx, ny, own_ref, x_ref, bend_ref, cell_ref, tab_ref, internal_ref, send_sem, recv_sem, own_sem):
+def block_range(index, unused):
+    high = index >> 7
+    full = index >= unused
+    first = jnp.min(jnp.where(full, (unused >> 7) - 1, high).astype(f32).T, axis=0, keepdims=True)
+    last = jnp.max(jnp.where(full, 0, high).astype(f32).T, axis=0, keepdims=True)
+    return first.astype(jnp.int32), jnp.maximum(first, last).astype(jnp.int32)
+
+def halo_kernel(nx, ny, pos_ref, vel_ref, mpos_ref, mvel_ref, bend_ref, cell_ref, idx_ref, par_ref, ver_ref,
+                tab_ref, mem_ref, internal_ref, range_ref, own_ref, x_ref, send_sem, recv_sem, own_sem):
     gx, gy = lax.axis_index("gx"), lax.axis_index("gy")
     up, down = (lax.rem(gx + 1, nx), gy), (lax.rem(gx + nx - 1, nx), gy)
     right, left = (gx, lax.rem(gy + 1, ny)), (gx, lax.rem(gy + ny - 1, ny))
@@ -395,6 +418,10 @@
     barrier = pltpu.get_barrier_semaphore()
     for device in (up, down, right, left):
         pl.semaphore_signal(barrier, inc=1, device_id=device, device_id_type=MESH)
+    for blk in range(BOXES):
+        at = slice(blk * TILE, (blk + 1) * TILE)
+        own_ref[pl.ds(blk, 3, stride=BOXES), :] = pos_ref[:, at]
+        own_ref[pl.ds(3 * BOXES + blk, 3, stride=BOXES), :] = vel_ref[:, at]
     pl.semaphore_wait(barrier, 4)
 
     def slot(n, c):
@@ -415,24 +442,49 @@
         for one in first[c] + along[c]:
             one.start()
 
+    def forward(c):
+        for k in range(2):
+            first[c][k].wait_recv()
+            on[c][2 * k].start()
+            on[c][2 * k + 1].start()
+
+    cells = x_ref.shape[0] // 3
+    for d in range(3):
+        for j in range(cells):
+            x_ref[d * cells + j:d * cells + j + 1, :] = mpos_ref[d:d + 1, j * V:(j + 1) * V]
     x = x_ref[...]
-    cells = x.shape[0] // 3
     relative = x - jnp.sum(x, axis=1, keepdims=True) * (1.0 / V)
     once = lax.dot_general(relative, bend_ref[...], NT, precision=lax.Precision.HIGHEST, preferred_element_type=f32)
+    forward(0)
     twice = lax.dot_general(once, bend_ref[...], NT, precision=lax.Precision.HIGHEST, preferred_element_type=f32)
+    forward(1)
     square = jnp.sum(relative * relative, axis=1, keepdims=True)
     spread = (square[:cells] + square[cells:2 * cells] + square[2 * cells:]) * (1.0 / V)
     stretch = AREA_MODULUS * (spread / cell_ref[:, 0:1] - 1.0)
     alive = cell_ref[:, 1:2]
     for d in range(3):
         rows = slice(d * cells, (d + 1) * cells)
-        internal_ref[rows] = -(BENDING_MODULUS * twice[rows] + stretch * relative[rows]) * alive
-
-    for c in range(CHUNKS):
-        for k in range(2):
-            first[c][k].wait_recv()
-            on[c][2 * k].start()
-            on[c][2 * k + 1].start()
+        x_ref[rows] = -(BENDING_MODULUS * twice[rows] + stretch * relative[rows]) * alive
+    forward(2)
+    for d in range(3):
+        for j in range(cells):
+            internal_ref[d:d + 1, j * V:(j + 1) * V] = x_ref[d * cells + j:d * cells + j + 1, :]
+
+    width = mpos_ref.shape[1]
+    rows = mem_ref.shape[0] // 6
+    mem_ref[...] = jnp.zeros_like(mem_ref)
+    for blk in range(-(-width // TILE)):
+        at = slice(blk * TILE, min((blk + 1) * TILE, width))
+        mem_ref[pl.ds(blk, 3, stride=rows), :at.stop - at.start] = mpos_ref[:, at]
+        mem_ref[pl.ds(3 * rows + blk, 3, stride=rows), :at.stop - at.start] = mvel_ref[:, at]
+    range_ref[...] = jnp.zeros_like(range_ref)
+    parts = idx_ref.shape[0] // TILE
+    for k in range(parts):
+        range_ref[k:k + 1, :], range_ref[parts + k:parts + k + 1, :] = block_range(idx_ref[k * TILE:(k + 1) * TILE, :], 9 * BOXES * TILE)
+    for k, ref in ((P_LOW, par_ref), (V_LOW, ver_ref)):
+        low, high = block_range(ref[...], 9 * BOXES * TILE)
+        range_ref[k:k + 1, :low.shape[1]] = low
+        range_ref[k + 1:k + 2, :low.shape[1]] = high
     keep.wait()
     for c in range(CHUNKS):
         for one in first[c]:
@@ -440,32 +492,34 @@
         for one in along[c] + on[c]:
             one.wait()
 
-def halo(own, x, bending, cell):
-    size = own.shape[0]
+def halo(pos, vel, mpos, mvel, bending, cell, index, partner, vertex):
+    size = 6 * BOXES
     nx, ny = lax.axis_size("gx"), lax.axis_size("gy")
     vmem, anywhere = pl.BlockSpec(memory_space=pltpu.VMEM), pl.BlockSpec(memory_space=pl.ANY)
     return pl.pallas_call(
         functools.partial(halo_kernel, nx, ny),
-        out_shape=(jax.ShapeDtypeStruct((9 * size, TILE), f32), jax.ShapeDtypeStruct(x.shape, f32)),
-        in_specs=[anywhere, vmem, vmem, vmem],
-        out_specs=(anywhere, vmem),
-        scratch_shapes=[pltpu.SemaphoreType.DMA((9, CHUNKS)), pltpu.SemaphoreType.DMA((9, CHUNKS)), pltpu.SemaphoreType.DMA],
+        out_shape=(
+            jax.ShapeDtypeStruct((9 * size, TILE), f32),
+            jax.ShapeDtypeStruct((6 * MB, TILE), f32),
+            jax.ShapeDtypeStruct(mpos.shape, f32),
+            jax.ShapeDtypeStruct((16, TILE), jnp.int32),
+        ),
+        in_specs=[vmem] * 9,
+        out_specs=(anywhere, vmem, vmem, vmem),
+        scratch_shapes=[pltpu.VMEM((size, TILE), f32), pltpu.VMEM((3 * cell.shape[0], V), f32),
+                        pltpu.SemaphoreType.DMA((9, CHUNKS)), pltpu.SemaphoreType.DMA((9, CHUNKS)), pltpu.SemaphoreType.DMA],
         compiler_params=pltpu.CompilerParams(collective_id=0, has_side_effects=True, vmem_limit_bytes=30 * 2**20),
         name="halo",
-    )(own, x, bending, cell)
+    )(pos, vel, mpos, mvel, bending, cell, index, partner, vertex)
 
 def on_device(solvent_pos, solvent_vel, pair_index, random_pairs, membrane_pos, membrane_vel, mem_vertex, mem_partner,
               bending, rest_size, cell_count):
     cells = rest_size.shape[0]
-    own = jnp.concatenate([solvent_pos, solvent_vel], axis=0).reshape(6 * BOXES, TILE)
     alive = (jnp.arange(cells, dtype=jnp.int32) < cell_count[0]).astype(f32)
-    tab, internal = halo(own, membrane_pos.reshape(3 * cells, V), bending, jnp.stack([rest_size, alive], axis=1))
-    mem = jnp.concatenate([membrane_pos, membrane_vel], axis=0)
-    mem = jnp.pad(mem, ((0, 0), (0, MB * TILE - mem.shape[1]))).reshape(6 * MB, TILE)
-    con, rea, held = contact(tab, mem, mem_vertex, mem_partner, pair_index, cell_count)
-    solvent_velocity = pairs(held, random_pairs, own, rea).reshape(3, BOXES * TILE)
-    touch = con.reshape(3, MB * TILE)[:, :membrane_pos.shape[1]]
-    membrane_velocity = membrane_vel + TIME_STEP * (internal.reshape(membrane_pos.shape) + touch)
+    tab, mem, internal, ranges = halo(solvent_pos, solvent_vel, membrane_pos, membrane_vel, bending,
+                                      jnp.stack([rest_size, alive], axis=1), pair_index, mem_partner, mem_vertex)
+    rea, held, membrane_velocity = contact(ranges, tab, mem, internal, membrane_vel, mem_vertex, mem_partner, pair_index, cell_count)
+    solvent_velocity = pairs(held, random_pairs, tab, rea).reshape(3, BOXES * TILE)
     return solvent_velocity, membrane_velocity
 
 def solution(mesh):

time: 81.1 us -> 78.8 us (0.972)
  local copies, waits for them, and re-layouts: 3.55 us -> 8.53 us
  other arithmetic: 5.39 us -> 0.67 us
  Pallas kernels: 70.3 us -> 67.8 us
    unnamed x13 -> x22, local copies, waits for them, and re-layouts: 0.14 us -> 7.69 us
    pallas_call x1, Pallas kernels: 23.1 us -> 19.9 us  [contact(): pl.pallas_call(contact_kernel, out_shape=(jax.ShapeDtypeStruct((9 * 3 * B...]
    reshape x5 -> x1, local copies, waits for them, and re-layouts: 3.33 us -> 0.75 us  [on_device(): pairs(held, random_pairs, tab, rea).reshape(3, BOXES * TILE)]
    reduce_max x2 -> x0, other arithmetic: 2.05 us -> none  [block_range(): last = jnp.max(jnp.where(full, 0, high), axis=1)]
    concatenate x2 -> x0, other arithmetic: 1.92 us -> none  [the longest x1 1.11 us: on_device(): jnp.concatenate([solvent_pos, solvent_vel], axis=0).reshape(6 * BOXES, TILE)]
where the time goes in v4:
time: 78.8 us; the launch traced here: 78.4 us
  Pallas kernels  67.8 us (86%)
  local copies, waits for them, and re-layouts  8.53 us (11%)
  between operations  1.33 us (2%)
    pallas_call x1, Pallas kernels, pairs(): pl.pallas_call(functools.partial(pair_kernel, nx, ny), out_shape=jax.Shap...  27.3 us
    pallas_call x1, Pallas kernels, halo(): pl.pallas_call(functools.partial(halo_kernel, nx, ny), out_shape=(jax.Sha...  20.6 us
    pallas_call x1, Pallas kernels, contact(): pl.pallas_call(contact_kernel, out_shape=(jax.ShapeDtypeStruct((9 * 3 * B...  19.9 us
    unnamed x22, local copies, waits for them, and re-layouts  7.69 us

profile of v4, /device:TPU:1, one launch (start us, length us, event | category | flops | bytes accessed | tf_op | source)
XLA Modules:
  0.0 78.4 jit_solution(14414599569789420601)
XLA Ops:
  1.3 0.7 pad_maximum_fusion
  2.0 0.1 copy.14.cell_ref
  2.0 0.0 copy-start
  2.0 1.6 %copy-done = f32[642,642]{1,0:T(8,128)S(1)} copy-done((f32[642,642]{1,0:T(8,128)S(1)}, f32[642,642]{1,0:T(8,128)}, u32[]{:S(2)}) %copy-start) | copy-done | bytes 1648680
  3.6 0.0 copy-start.1
  3.6 0.9 %copy-done.1 = s32[384,128]{1,0:T(8,128)S(1)} copy-done((s32[384,128]{1,0:T(8,128)S(1)}, s32[384,128]{1,0:T(8,128)}, u32[]{:S(2)}) %copy-start.1) | copy-done | bytes 196632
  4.5 0.0 copy-start.3
  4.5 0.9 %copy-done.3 = f32[3,10272]{1,0:T(4,128)S(1)} copy-done((f32[3,10272]{1,0:T(4,128)S(1)}, f32[3,10272]{1,0:T(4,128)}, u32[]{:S(2)}) %copy-start.3) | copy-done | bytes 123288
  5.4 0.0 copy-start.5
  5.4 0.9 %copy-done.5 = f32[3,12288]{1,0:T(4,128)S(1)} copy-done((f32[3,12288]{1,0:T(4,128)S(1)}, f32[3,12288]{1,0:T(4,128)}, u32[]{:S(2)}) %copy-start.5) | copy-done | bytes 147480
  6.4 0.0 copy-start.6
  6.4 0.9 %copy-done.6 = f32[3,12288]{1,0:T(4,128)S(1)} copy-done((f32[3,12288]{1,0:T(4,128)S(1)}, f32[3,12288]{1,0:T(4,128)}, u32[]{:S(2)}) %copy-start.6) | copy-done | bytes 147480
  7.3 0.0 copy-start.7
  7.3 0.9 %copy-done.7 = f32[3,10272]{1,0:T(4,128)S(1)} copy-done((f32[3,10272]{1,0:T(4,128)S(1)}, f32[3,10272]{1,0:T(4,128)}, u32[]{:S(2)}) %copy-start.7) | copy-done | bytes 123288
  8.2 0.0 copy-start.8
  8.2 0.8 copy-done.8
  9.0 0.0 copy-start.10
  9.0 0.8 copy-done.10
  9.7 0.0 copy-start.2
  9.7 0.0 copy-start.4
  9.7 0.0 copy-start.9
  9.7 20.6 %halo.1 = (f32[5184,128]{1,0:T(8,128)S(1)}, f32[576,128]{1,0:T(8,128)S(1)}, f32[3,10272]{1,0:T(4,128)S(1)}, s32[16,128]{1,0:T(8,128)S(1)}) custom-call(f32[3,12288]{1,0:T(4,128)S(1)} %copy-done.5, f32[3,12288]{1,0:T(4,128)S(1)} %copy-done.6, f32[3,10272]{1,0:T(4,128)S(1)} %copy-done.7, f32[3,10272]{1,0:T(4,128)S(1)} %copy-done.3, f32[642,642]{1,0:T(8,128)S(1)} %copy-done, ...), custom_call_target="tpu_custom_call" | custom-call | tf_op jit(solution)/shard_map/halo/pallas_call | solution.py:499
  30.3 0.0 copy-done.2
  30.3 0.0 copy-done.4
  30.3 0.0 copy-done.9
  30.4 19.9 %contact.1 = (f32[2592,128]{1,0:T(8,128)S(1)}, f32[384,8,128]{2,1,0:T(8,128)S(1)}, f32[3,10272]{1,0:T(4,128)}) custom-call(s32[16,128]{1,0:T(8,128)S(1)} %get-tuple-element.9.range_ref, s32[1]{0:T(128)} %copy.15.count, s32[64,128]{1,0:T(8,128)S(1)} %copy-done.9, s32[64,128]{1,0:T(8,128)S(1)} %copy-done.10, s32[384,128]{1,0:T(8,128)S(1)} %copy-done.2, ...), custom_call_target="tpu_custom_call" | custom-call | tf_op jit(solution)/shard_map/contact/pallas_call | solution.py:383
  50.3 27.3 %pairs.1 = f32[288,128]{1,0:T(8,128)S(1)} custom-call(f32[384,8,128]{2,1,0:T(8,128)S(1)} %get-tuple-element.13.held_ref, bf16[384,128,128]{2,1,0:T(8,128)(2,1)} %theta_ref.1, f32[5184,128]{1,0:T(8,128)S(1)} %get-tuple-element.10.tab_ref.own_ref, f32[2592,128]{1,0:T(8,128)S(1)} %get-tuple-element.14.rea_ref), custom_call_target="tpu_custom_call" | custom-call | tf_op jit(solution)/shard_map/pairs/pallas_call | solution.py:146
  77.6 0.8 reshape.17
  (1 shorter events, 0.0 us)
Async XLA Ops:
  2.0 1.6 %copy-start = (f32[642,642]{1,0:T(8,128)S(1)}, f32[642,642]{1,0:T(8,128)}, u32[]{:S(2)}) copy-start(f32[642,642]{1,0:T(8,128)} %bend_ref.1) | copy-start | bytes 4945972
  3.6 0.9 %copy-start.1 = (s32[384,128]{1,0:T(8,128)S(1)}, s32[384,128]{1,0:T(8,128)}, u32[]{:S(2)}) copy-start(s32[384,128]{1,0:T(8,128)} %idx_ref.3) | copy-start | bytes 589828
  4.5 0.9 %copy-start.3 = (f32[3,10272]{1,0:T(4,128)S(1)}, f32[3,10272]{1,0:T(4,128)}, u32[]{:S(2)}) copy-start(f32[3,10272]{1,0:T(4,128)} %vel_ref.3) | copy-start | bytes 369796
  5.4 0.9 %copy-start.5 = (f32[3,12288]{1,0:T(4,128)S(1)}, f32[3,12288]{1,0:T(4,128)}, u32[]{:S(2)}) copy-start(f32[3,12288]{1,0:T(4,128)} %pos_ref.1) | copy-start | bytes 442372
  6.4 0.9 %copy-start.6 = (f32[3,12288]{1,0:T(4,128)S(1)}, f32[3,12288]{1,0:T(4,128)}, u32[]{:S(2)}) copy-start(f32[3,12288]{1,0:T(4,128)} %vel_ref.2) | copy-start | bytes 442372
  7.3 0.9 %copy-start.7 = (f32[3,10272]{1,0:T(4,128)S(1)}, f32[3,10272]{1,0:T(4,128)}, u32[]{:S(2)}) copy-start(f32[3,10272]{1,0:T(4,128)} %mpos_ref.1) | copy-start | bytes 369796
  8.2 0.8 copy-start.8
  9.0 0.8 copy-start.10
  9.7 20.6 %copy-start.2 = (s32[384,128]{1,0:T(8,128)S(1)}, s32[384,128]{1,0:T(8,128)}, u32[]{:S(2)}) copy-start(s32[384,128]{1,0:T(8,128)} %idx_ref.3) | copy-start | bytes 589828
  9.7 20.6 %copy-start.4 = (f32[3,10272]{1,0:T(4,128)S(1)}, f32[3,10272]{1,0:T(4,128)}, u32[]{:S(2)}) copy-start(f32[3,10272]{1,0:T(4,128)} %vel_ref.3) | copy-start | bytes 369796
  9.7 20.6 %copy-start.9 = (s32[64,128]{1,0:T(8,128)S(1)}, s32[64,128]{1,0:T(8,128)}, u32[]{:S(2)}) copy-start(s32[64,128]{1,0:T(8,128)} %par_ref.3) | copy-start | bytes 98308

commit v5 on v4

--- a/solution.py
+++ b/solution.py
@@ -7,7 +7,7 @@
 
 f32, bf16 = jnp.float32, jnp.bfloat16
 BOXES, TILE, PAIRS = 96, 128, 4
-GROUP = 8
+GROUP = 16
 TIME_STEP = 0.01
 SOLVENT_PUSH = 0.5
 MESH = pl.DeviceIdType.MESH
@@ -42,8 +42,8 @@
     cz = (box >> 2).astype(f32) * 2.0 + 1.0
     return jnp.where(row8 == 0, cx, jnp.where(row8 == 1, cy, jnp.where(row8 == 2, cz, 0.0)))
 
-def own_features(own, row8):
-    a, u = own[0:3], own[3:6] * 4.5
+def own_features(own, row8, friction):
+    a, u = own[0:3], own[3:6] * friction
     aa = jnp.sum(a * a, axis=0, keepdims=True)
     au = jnp.sum(a * u, axis=0, keepdims=True)
     zero = jnp.zeros((3, TILE), f32)
@@ -54,7 +54,7 @@
         last = jnp.where(row8 == 0, c1, jnp.where(row8 == 1, c2, jnp.where(row8 == 2, c3, 0.0)))
         return jnp.concatenate([q1, q1, q1, q2, q2, q3, last, jnp.zeros_like(last)], axis=0)
     ql = left(jnp.concatenate([-2.0 * a, zero, one, 0.0 * one], axis=0), aa)
-    qs = left(jnp.concatenate([-u, -4.5 * a, 0.0 * one, 4.5 * one], axis=0), au)
+    qs = left(jnp.concatenate([-u, -friction * a, 0.0 * one, friction * one], axis=0), au)
     return jnp.concatenate([ql.T, qs.T], axis=0).astype(bf16)
 
 def right_features(held, centre, row8):
@@ -75,7 +75,7 @@
     r2 = jnp.maximum(r2, 1e-12)
     q = lax.rsqrt(r2)
     g = jnp.maximum(jnp.minimum(q, 10.0) * (1.0 - r2 * q), 0.0)
-    force = g * (25.0 + 30.0 * th - g * s)
+    force = g * ((th + 25.0 / 30.0) - g * s)
     fh = force.astype(bf16)
     return fh, (force - fh.astype(f32)).astype(bf16)
 
@@ -121,7 +121,7 @@
         box = step * GROUP + k
         centre = box_centre(box, row8)
         own = own_ref[pl.ds(box, 6, stride=BOXES), :] - centre[0:6]
-        lhs = own_features(own, row8)
+        lhs = own_features(own, row8, 4.5 / 30.0)
         acc = jnp.zeros((32, TILE), f32)
         for h in range(2):
             feats = [right_features(held_ref[k * PAIRS + 2 * h + j, 0:6, :], centre, row8) for j in range(2)]
@@ -129,7 +129,7 @@
             out = jnp.dot(lhs, rhs, preferred_element_type=f32)
             for force in pair_force(out, theta_ref, k, h):
                 acc += lax.dot_general(sums, force, NT, preferred_element_type=f32)
-        out_ref[pl.ds(box, 3, stride=BOXES), :] = own[0:3] * acc[3:4] - (acc[0:8] + acc[8:16] + acc[16:24])[0:3]
+        out_ref[pl.ds(box, 3, stride=BOXES), :] = 30.0 * (own[0:3] * acc[3:4] - (acc[0:8] + acc[8:16] + acc[16:24])[0:3])
 
     @pl.when(step == BOXES // GROUP - 1)
     def _():
@@ -156,7 +156,7 @@
         out_specs=pl.BlockSpec((size, TILE), lambda i: (0, 0)),
         scratch_shapes=[pltpu.VMEM((3 * size, TILE), f32), pltpu.VMEM((2, 3 * size, TILE), f32), pltpu.VMEM((2, size, TILE), f32),
                         pltpu.SemaphoreType.DMA((4,)), pltpu.SemaphoreType.DMA((4,)), pltpu.SemaphoreType.DMA],
-        compiler_params=pltpu.CompilerParams(collective_id=1, has_side_effects=True, vmem_limit_bytes=40 * 2**20),
+        compiler_params=pltpu.CompilerParams(collective_id=1, has_side_effects=True, vmem_limit_bytes=56 * 2**20),
         name="pairs",
     )(held, theta, tab, rea)
 
@@ -195,7 +195,14 @@
 def add_partner(rea_ref, blk, out):
     rea_ref[pl.ds(blk + part_of(blk) * (2 * BOXES), 3, stride=BOXES), :] += out
 
-def contact_kernel(range_ref, count, par_ref, ver_ref, idx_ref, tab_ref, mem_ref, internal_ref, vel_ref, rea_ref, held_ref, out_ref, con_ref, lh_ref, rh_ref, fo_ref, force_ref, sum_ref):
+def contact_kernel(count, *refs):
+    arrays, (rea_ref, held_out_ref, out_ref) = refs[:8], refs[8:11]
+    con_ref, held_ref, lh_ref, rh_ref, fo_ref, force_ref, sum_ref, in_sem, out_sem = refs[11:20]
+    range_ref, mem_ref, ver_ref, par_ref, idx_ref, tab_ref, internal_ref, vel_ref = local = refs[20:]
+    loads = [pltpu.make_async_copy(array, ref, in_sem.at[k]) for k, (array, ref) in enumerate(zip(arrays, local))]
+    for load in loads:
+        load.start()
+    held_copy = pltpu.make_async_copy(held_ref, held_out_ref, out_sem)
     row6 = lax.broadcasted_iota(jnp.int32, (6, TILE), 0)
     row8 = lax.broadcasted_iota(jnp.int32, (8, TILE), 0)
     rowt = lax.broadcasted_iota(jnp.int32, (TILE, TILE), 0)
@@ -204,6 +211,8 @@
     alive_end = count[0] * V
     con_ref[...] = jnp.zeros_like(con_ref)
     rea_ref[...] = jnp.zeros_like(rea_ref)
+    for load in loads[:6]:
+        load.wait()
 
     @pl.loop(0, idx_ref.shape[0] // UNG)
     def _(part):
@@ -225,6 +234,8 @@
                 @pl.loop(range_ref[t >> 7, t & 127] + 1, range_ref[(t >> 7) + 3, t & 127] + 1)
                 def _(blk):
                     held_ref[t, 0:6, :] = gather_block(tab_ref, blk, index & 127, index >> 7, held_ref[t, 0:6, :], row6)
+
+    held_copy.start()
 
     @pl.loop(0, MEM_TILES // UNG)
     def _(part):
@@ -294,7 +305,7 @@
             spread = jnp.maximum(spread, range_ref[P_HIGH, t] - range_ref[P_LOW, t])
             centre = centre_of(range_ref[P_LOW, t])
             left, right = lh_ref[t, 0:6, :], rh_ref[t, 0:6, :]
-            lhs = own_features(left - centre[0:6], row8)
+            lhs = own_features(left - centre[0:6], row8, 4.5)
             rhs, wb = right_features(right, centre, row8)
             wa = right_features(left, centre, row8)[1]
             out = jnp.dot(lhs, rhs, preferred_element_type=f32)
@@ -372,28 +383,31 @@
                 def _(blk):
                     add_partner(rea_ref, blk, partner_sums(blk, index & 127, index >> 7, rea, rowt))
 
+    for load in loads[6:]:
+        load.wait()
     width = out_ref.shape[1]
     for blk in range(-(-width // TILE)):
         at = slice(blk * TILE, min((blk + 1) * TILE, width))
         out_ref[:, at] = vel_ref[:, at] + TIME_STEP * (internal_ref[:, at] + con_ref[:, blk, :at.stop - at.start])
+    held_copy.wait()
 
 def contact(ranges, tab, mem, internal, vel, vertex, partner, index, count):
-    smem, vmem = pl.BlockSpec(memory_space=pltpu.SMEM), pl.BlockSpec(memory_space=pltpu.VMEM)
+    arrays = ranges, mem, vertex, partner, index, tab, internal, vel
+    hbm, vmem = pl.BlockSpec(memory_space=pltpu.HBM), pl.BlockSpec(memory_space=pltpu.VMEM)
     tile = pltpu.VMEM((MEM_TILES, 8, TILE), f32)
+    held = jax.ShapeDtypeStruct((index.shape[0], 8, TILE), f32)
     return pl.pallas_call(
         contact_kernel,
-        out_shape=(
-            jax.ShapeDtypeStruct((9 * 3 * BOXES, TILE), f32),
-            jax.ShapeDtypeStruct((index.shape[0], 8, TILE), f32),
-            jax.ShapeDtypeStruct(vel.shape, f32),
-        ),
-        in_specs=[smem] * 2 + [vmem] * 7,
-        out_specs=(vmem, vmem, vmem),
-        scratch_shapes=[pltpu.VMEM((3, MB, TILE), f32), tile, tile, pltpu.VMEM((MEM_TILES, 16, TILE), f32),
-                        pltpu.VMEM((2, MEM_TILES, TILE, TILE), bf16), pltpu.VMEM((2, MEM_TILES, 32, TILE), bf16)],
-        compiler_params=pltpu.CompilerParams(vmem_limit_bytes=40 * 2**20),
+        out_shape=(jax.ShapeDtypeStruct((9 * 3 * BOXES, TILE), f32), held, jax.ShapeDtypeStruct(vel.shape, f32)),
+        in_specs=[pl.BlockSpec(memory_space=pltpu.SMEM)] + [hbm] * 8,
+        out_specs=(vmem, hbm, vmem),
+        scratch_shapes=[pltpu.VMEM((3, MB, TILE), f32), pltpu.VMEM(held.shape, f32), tile, tile, pltpu.VMEM((MEM_TILES, 16, TILE), f32),
+                        pltpu.VMEM((2, MEM_TILES, TILE, TILE), bf16), pltpu.VMEM((2, MEM_TILES, 32, TILE), bf16),
+                        pltpu.SemaphoreType.DMA((8,)), pltpu.SemaphoreType.DMA, pltpu.SMEM(ranges.shape, ranges.dtype)]
+        + [pltpu.VMEM(x.shape, x.dtype) for x in arrays[1:]],
+        compiler_params=pltpu.CompilerParams(vmem_limit_bytes=56 * 2**20),
         name="contact",
-    )(ranges, count, partner, vertex, index, tab, mem, internal, vel)
+    )(count, *arrays)
 
 BENDING_MODULUS = 20.0
 AREA_MODULUS = 40.0
@@ -407,8 +421,10 @@
     last = jnp.max(jnp.where(full, 0, high).astype(f32).T, axis=0, keepdims=True)
     return first.astype(jnp.int32), jnp.maximum(first, last).astype(jnp.int32)
 
-def halo_kernel(nx, ny, pos_ref, vel_ref, mpos_ref, mvel_ref, bend_ref, cell_ref, idx_ref, par_ref, ver_ref,
-                tab_ref, mem_ref, internal_ref, range_ref, own_ref, x_ref, send_sem, recv_sem, own_sem):
+def halo_kernel(nx, ny, *refs):
+    arrays, (rest_ref, count_ref, tab_ref, mem_ref, internal_ref, range_ref) = refs[:8], refs[8:14]
+    own_ref, x_ref, send_sem, recv_sem, own_sem, in_sem = refs[14:20]
+    pos_ref, vel_ref, mpos_ref, mvel_ref, bend_ref, idx_ref, par_ref, ver_ref = local = refs[20:]
     gx, gy = lax.axis_index("gx"), lax.axis_index("gy")
     up, down = (lax.rem(gx + 1, nx), gy), (lax.rem(gx + nx - 1, nx), gy)
     right, left = (gx, lax.rem(gy + 1, ny)), (gx, lax.rem(gy + ny - 1, ny))
@@ -418,6 +434,11 @@
     barrier = pltpu.get_barrier_semaphore()
     for device in (up, down, right, left):
         pl.semaphore_signal(barrier, inc=1, device_id=device, device_id_type=MESH)
+    loads = [pltpu.make_async_copy(array, ref, in_sem.at[k]) for k, (array, ref) in enumerate(zip(arrays, local))]
+    for load in loads:
+        load.start()
+    loads[0].wait()
+    loads[1].wait()
     for blk in range(BOXES):
         at = slice(blk * TILE, (blk + 1) * TILE)
         own_ref[pl.ds(blk, 3, stride=BOXES), :] = pos_ref[:, at]
@@ -448,6 +469,8 @@
             on[c][2 * k].start()
             on[c][2 * k + 1].start()
 
+    for load in loads[2:]:
+        load.wait()
     cells = x_ref.shape[0] // 3
     for d in range(3):
         for j in range(cells):
@@ -460,8 +483,12 @@
     forward(1)
     square = jnp.sum(relative * relative, axis=1, keepdims=True)
     spread = (square[:cells] + square[cells:2 * cells] + square[2 * cells:]) * (1.0 / V)
-    stretch = AREA_MODULUS * (spread / cell_ref[:, 0:1] - 1.0)
-    alive = cell_ref[:, 1:2]
+    slot_row = lax.broadcasted_iota(jnp.int32, (cells, 1), 0)
+    rest = jnp.ones((cells, 1), f32)
+    for j in range(cells):
+        rest = jnp.where(slot_row == j, rest_ref[j], rest)
+    stretch = AREA_MODULUS * (spread / rest - 1.0)
+    alive = (slot_row < count_ref[0]).astype(f32)
     for d in range(3):
         rows = slice(d * cells, (d + 1) * cells)
         x_ref[rows] = -(BENDING_MODULUS * twice[rows] + stretch * relative[rows]) * alive
@@ -492,8 +519,9 @@
         for one in along[c] + on[c]:
             one.wait()
 
-def halo(pos, vel, mpos, mvel, bending, cell, index, partner, vertex):
+def halo(pos, vel, mpos, mvel, bending, index, partner, vertex, rest, count):
     size = 6 * BOXES
+    arrays = pos, vel, mpos, mvel, bending, index, partner, vertex
     nx, ny = lax.axis_size("gx"), lax.axis_size("gy")
     vmem, anywhere = pl.BlockSpec(memory_space=pltpu.VMEM), pl.BlockSpec(memory_space=pl.ANY)
     return pl.pallas_call(
@@ -504,20 +532,19 @@
             jax.ShapeDtypeStruct(mpos.shape, f32),
             jax.ShapeDtypeStruct((16, TILE), jnp.int32),
         ),
-        in_specs=[vmem] * 9,
+        in_specs=[pl.BlockSpec(memory_space=pltpu.HBM)] * 8 + [pl.BlockSpec(memory_space=pltpu.SMEM)] * 2,
         out_specs=(anywhere, vmem, vmem, vmem),
-        scratch_shapes=[pltpu.VMEM((size, TILE), f32), pltpu.VMEM((3 * cell.shape[0], V), f32),
-                        pltpu.SemaphoreType.DMA((9, CHUNKS)), pltpu.SemaphoreType.DMA((9, CHUNKS)), pltpu.SemaphoreType.DMA],
-        compiler_params=pltpu.CompilerParams(collective_id=0, has_side_effects=True, vmem_limit_bytes=30 * 2**20),
+        scratch_shapes=[pltpu.VMEM((size, TILE), f32), pltpu.VMEM((3 * rest.shape[0], V), f32),
+                        pltpu.SemaphoreType.DMA((9, CHUNKS)), pltpu.SemaphoreType.DMA((9, CHUNKS)), pltpu.SemaphoreType.DMA,
+                        pltpu.SemaphoreType.DMA((8,))] + [pltpu.VMEM(x.shape, x.dtype) for x in arrays],
+        compiler_params=pltpu.CompilerParams(collective_id=0, has_side_effects=True, vmem_limit_bytes=56 * 2**20),
         name="halo",
-    )(pos, vel, mpos, mvel, bending, cell, index, partner, vertex)
+    )(*arrays, rest, count)
 
 def on_device(solvent_pos, solvent_vel, pair_index, random_pairs, membrane_pos, membrane_vel, mem_vertex, mem_partner,
               bending, rest_size, cell_count):
-    cells = rest_size.shape[0]
-    alive = (jnp.arange(cells, dtype=jnp.int32) < cell_count[0]).astype(f32)
-    tab, mem, internal, ranges = halo(solvent_pos, solvent_vel, membrane_pos, membrane_vel, bending,
-                                      jnp.stack([rest_size, alive], axis=1), pair_index, mem_partner, mem_vertex)
+    tab, mem, internal, ranges = halo(solvent_pos, solvent_vel, membrane_pos, membrane_vel, bending, pair_index, mem_partner,
+                                      mem_vertex, rest_size, cell_count)
     rea, held, membrane_velocity = contact(ranges, tab, mem, internal, membrane_vel, mem_vertex, mem_partner, pair_index, cell_count)
     solvent_velocity = pairs(held, random_pairs, tab, rea).reshape(3, BOXES * TILE)
     return solvent_velocity, membrane_velocity

time: 78.8 us -> 73.2 us (0.929)
  local copies, waits for them, and re-layouts: 8.53 us -> 1.66 us
  Pallas kernels: 67.8 us -> 70 us
    unnamed x22 -> x0, local copies, waits for them, and re-layouts: 7.69 us -> none
    pallas_call x1, Pallas kernels: 20.6 us -> 23.4 us  [halo(): pl.pallas_call(functools.partial(halo_kernel, nx, ny), out_shape=(jax.Sha...]
    pallas_call x1, Pallas kernels: 27.3 us -> 25 us  [pairs(): pl.pallas_call(functools.partial(pair_kernel, nx, ny), out_shape=jax.Shap...]
    pallas_call x1, Pallas kernels: 19.9 us -> 21.6 us  [contact(): pl.pallas_call(contact_kernel, out_shape=(jax.ShapeDtypeStruct((9 * 3 * B...]
    reshape x1, local copies, waits for them, and re-layouts: 0.75 us -> 1.66 us  [on_device(): pairs(held, random_pairs, tab, rea).reshape(3, BOXES * TILE)]
where the time goes in v5:
time: 73.2 us; the launch traced here: 73 us
  Pallas kernels  70 us (96%)
  local copies, waits for them, and re-layouts  1.66 us (2%)
  between operations  1.3 us (2%)
    pallas_call x1, Pallas kernels, pairs(): pl.pallas_call(functools.partial(pair_kernel, nx, ny), out_shape=jax.Shap...  25 us
    pallas_call x1, Pallas kernels, halo(): pl.pallas_call(functools.partial(halo_kernel, nx, ny), out_shape=(jax.Sha...  23.4 us
    pallas_call x1, Pallas kernels, contact(): pl.pallas_call(contact_kernel, out_shape=(jax.ShapeDtypeStruct((9 * 3 * B...  21.6 us
    reshape x1, local copies, waits for them, and re-layouts, on_device(): pairs(held, random_pairs, tab, rea).reshape(3, BOXES * TILE)  1.66 us

profile of v5, /device:TPU:1, one launch (start us, length us, event | category | flops | bytes accessed | tf_op | source)
XLA Modules:
  0.0 73.0 jit_solution(6241086031892568145)
XLA Ops:
  1.3 23.4 %halo.1 = (f32[5184,128]{1,0:T(8,128)}, f32[576,128]{1,0:T(8,128)}, f32[3,10272]{1,0:T(4,128)}, s32[16,128]{1,0:T(8,128)}) custom-call(f32[3,12288]{1,0:T(4,128)} %refs_0_.1, f32[3,12288]{1,0:T(4,128)} %refs_1_.1, f32[3,10272]{1,0:T(4,128)} %refs_2_.2, f32[3,10272]{1,0:T(4,128)} %refs_7_.3, f32[642,642]{1,0:T(8,128)} %refs_4_.2, s32[384,128]{1,0:T(8,128)} %refs_4_.3, ...), custom_call_target="tpu_custom_call" | custom-call | tf_op jit(solution)/shard_map/halo/pallas_call | solution.py:527
  24.7 21.6 %contact.1 = (f32[2592,128]{1,0:T(8,128)}, f32[384,8,128]{2,1,0:T(8,128)}, f32[3,10272]{1,0:T(4,128)}) custom-call(s32[1]{0:T(128)S(6)} %copy.13.refs_9_.count, s32[16,128]{1,0:T(8,128)} %get-tuple-element.9.refs_0_, f32[576,128]{1,0:T(8,128)} %get-tuple-element.10.refs_1_, s32[64,128]{1,0:T(8,128)} %refs_2_.3, s32[64,128]{1,0:T(8,128)} %refs_3_.3, ...), custom_call_target="tpu_custom_call" | custom-call | tf_op jit(solution)/shard_map/contact/pallas_call | solution.py:399
  46.3 25.0 %pairs.1 = f32[288,128]{1,0:T(8,128)} custom-call(f32[384,8,128]{2,1,0:T(8,128)} %get-tuple-element.13.held_ref, bf16[384,128,128]{2,1,0:T(8,128)(2,1)} %theta_ref.1, f32[5184,128]{1,0:T(8,128)} %get-tuple-element.11.refs_5_.own_ref, f32[2592,128]{1,0:T(8,128)} %get-tuple-element.14.rea_ref), custom_call_target="tpu_custom_call" | custom-call | tf_op jit(solution)/shard_map/pairs/pallas_call | solution.py:146
  71.3 1.7 %reshape.7 = f32[3,12288]{1,0:T(4,128)} reshape(f32[288,128]{1,0:T(8,128)} %pairs.1) | data formatting | bytes 294912 | tf_op jit(solution)/shard_map/reshape | solution.py:549

commit v6 on v5

--- a/solution.py
+++ b/solution.py
@@ -166,7 +166,7 @@
 MB = 96
 WIN = 8
 SPAN = 16
-UNG, UNC, UNS = 16, 8, 16
+UNG, UNC, UNS = 32, 16, 32
 P_LOW, P_HIGH, V_LOW, V_HIGH = 6, 7, 8, 9
 
 def gather_window(tab_ref, base, low, high, held):
@@ -469,34 +469,8 @@
             on[c][2 * k].start()
             on[c][2 * k + 1].start()
 
-    for load in loads[2:]:
-        load.wait()
-    cells = x_ref.shape[0] // 3
-    for d in range(3):
-        for j in range(cells):
-            x_ref[d * cells + j:d * cells + j + 1, :] = mpos_ref[d:d + 1, j * V:(j + 1) * V]
-    x = x_ref[...]
-    relative = x - jnp.sum(x, axis=1, keepdims=True) * (1.0 / V)
-    once = lax.dot_general(relative, bend_ref[...], NT, precision=lax.Precision.HIGHEST, preferred_element_type=f32)
-    forward(0)
-    twice = lax.dot_general(once, bend_ref[...], NT, precision=lax.Precision.HIGHEST, preferred_element_type=f32)
-    forward(1)
-    square = jnp.sum(relative * relative, axis=1, keepdims=True)
-    spread = (square[:cells] + square[cells:2 * cells] + square[2 * cells:]) * (1.0 / V)
-    slot_row = lax.broadcasted_iota(jnp.int32, (cells, 1), 0)
-    rest = jnp.ones((cells, 1), f32)
-    for j in range(cells):
-        rest = jnp.where(slot_row == j, rest_ref[j], rest)
-    stretch = AREA_MODULUS * (spread / rest - 1.0)
-    alive = (slot_row < count_ref[0]).astype(f32)
-    for d in range(3):
-        rows = slice(d * cells, (d + 1) * cells)
-        x_ref[rows] = -(BENDING_MODULUS * twice[rows] + stretch * relative[rows]) * alive
-    forward(2)
-    for d in range(3):
-        for j in range(cells):
-            internal_ref[d:d + 1, j * V:(j + 1) * V] = x_ref[d * cells + j:d * cells + j + 1, :]
-
+    for k in (2, 3, 5, 6, 7):
+        loads[k].wait()
     width = mpos_ref.shape[1]
     rows = mem_ref.shape[0] // 6
     mem_ref[...] = jnp.zeros_like(mem_ref)
@@ -512,6 +486,33 @@
         low, high = block_range(ref[...], 9 * BOXES * TILE)
         range_ref[k:k + 1, :low.shape[1]] = low
         range_ref[k + 1:k + 2, :low.shape[1]] = high
+    forward(0)
+    cells = x_ref.shape[0] // 3
+    for d in range(3):
+        for j in range(cells):
+            x_ref[d * cells + j:d * cells + j + 1, :] = mpos_ref[d:d + 1, j * V:(j + 1) * V]
+    x = x_ref[...]
+    relative = x - jnp.sum(x, axis=1, keepdims=True) * (1.0 / V)
+    loads[4].wait()
+    once = lax.dot_general(relative, bend_ref[...], NT, precision=lax.Precision.HIGHEST, preferred_element_type=f32)
+    forward(1)
+    twice = lax.dot_general(once, bend_ref[...], NT, precision=lax.Precision.HIGHEST, preferred_element_type=f32)
+    forward(2)
+    square = jnp.sum(relative * relative, axis=1, keepdims=True)
+    spread = (square[:cells] + square[cells:2 * cells] + square[2 * cells:]) * (1.0 / V)
+    slot_row = lax.broadcasted_iota(jnp.int32, (cells, 1), 0)
+    rest = jnp.ones((cells, 1), f32)
+    for j in range(cells):
+        rest = jnp.where(slot_row == j, rest_ref[j], rest)
+    stretch = AREA_MODULUS * (spread / rest - 1.0)
+    alive = (slot_row < count_ref[0]).astype(f32)
+    for d in range(3):
+        rows = slice(d * cells, (d + 1) * cells)
+        x_ref[rows] = -(BENDING_MODULUS * twice[rows] + stretch * relative[rows]) * alive
+    for d in range(3):
+        for j in range(cells):
+            internal_ref[d:d + 1, j * V:(j + 1) * V] = x_ref[d * cells + j:d * cells + j + 1, :]
+
     keep.wait()
     for c in range(CHUNKS):
         for one in first[c]:

time: 73.2 us -> 71.8 us (0.981)
  Pallas kernels: 70 us -> 68.6 us
    pallas_call x1, Pallas kernels: 21.6 us -> 19.9 us  [contact(): pl.pallas_call(contact_kernel, out_shape=(jax.ShapeDtypeStruct((9 * 3 * B...]
where the time goes in v6:
time: 71.8 us; the launch traced here: 71.6 us
  Pallas kernels  68.6 us (96%)
  local copies, waits for them, and re-layouts  1.66 us (2%)
  between operations  1.3 us (2%)
    pallas_call x1, Pallas kernels, pairs(): pl.pallas_call(functools.partial(pair_kernel, nx, ny), out_shape=jax.Shap...  25 us
    pallas_call x1, Pallas kernels, halo(): pl.pallas_call(functools.partial(halo_kernel, nx, ny), out_shape=(jax.Sha...  23.7 us
    pallas_call x1, Pallas kernels, contact(): pl.pallas_call(contact_kernel, out_shape=(jax.ShapeDtypeStruct((9 * 3 * B...  19.9 us
    reshape x1, local copies, waits for them, and re-layouts, on_device(): pairs(held, random_pairs, tab, rea).reshape(3, BOXES * TILE)  1.66 us

profile of v6, /device:TPU:1, one launch (start us, length us, event | category | flops | bytes accessed | tf_op | source)
XLA Modules:
  0.0 71.6 jit_solution(15922054637478620817)
XLA Ops:
  1.3 23.7 %halo.1 = (f32[5184,128]{1,0:T(8,128)}, f32[576,128]{1,0:T(8,128)}, f32[3,10272]{1,0:T(4,128)}, s32[16,128]{1,0:T(8,128)}) custom-call(f32[3,12288]{1,0:T(4,128)} %refs_0_.1, f32[3,12288]{1,0:T(4,128)} %refs_1_.1, f32[3,10272]{1,0:T(4,128)} %refs_2_.2, f32[3,10272]{1,0:T(4,128)} %refs_7_.3, f32[642,642]{1,0:T(8,128)} %refs_4_.2, s32[384,128]{1,0:T(8,128)} %refs_4_.3, ...), custom_call_target="tpu_custom_call" | custom-call | tf_op jit(solution)/shard_map/halo/pallas_call | solution.py:528
  25.0 19.9 %contact.1 = (f32[2592,128]{1,0:T(8,128)}, f32[384,8,128]{2,1,0:T(8,128)}, f32[3,10272]{1,0:T(4,128)}) custom-call(s32[1]{0:T(128)S(6)} %copy.13.refs_9_.count, s32[16,128]{1,0:T(8,128)} %get-tuple-element.9.refs_0_, f32[576,128]{1,0:T(8,128)} %get-tuple-element.10.refs_1_, s32[64,128]{1,0:T(8,128)} %refs_2_.3, s32[64,128]{1,0:T(8,128)} %refs_3_.3, ...), custom_call_target="tpu_custom_call" | custom-call | tf_op jit(solution)/shard_map/contact/pallas_call | solution.py:399
  45.0 25.0 %pairs.1 = f32[288,128]{1,0:T(8,128)} custom-call(f32[384,8,128]{2,1,0:T(8,128)} %get-tuple-element.13.held_ref, bf16[384,128,128]{2,1,0:T(8,128)(2,1)} %theta_ref.1, f32[5184,128]{1,0:T(8,128)} %get-tuple-element.11.refs_5_.own_ref, f32[2592,128]{1,0:T(8,128)} %get-tuple-element.14.rea_ref), custom_call_target="tpu_custom_call" | custom-call | tf_op jit(solution)/shard_map/pairs/pallas_call | solution.py:146
  69.9 1.7 %reshape.7 = f32[3,12288]{1,0:T(4,128)} reshape(f32[288,128]{1,0:T(8,128)} %pairs.1) | data formatting | bytes 294912 | tf_op jit(solution)/shard_map/reshape | solution.py:550
